TPU v7x, 512 devices: a whole 4x8x8 slice. The times are simulated.
512 devices in a mesh: ia: 32 (over x_lo, y, core), ja: 16 (over x_hi, z).
Axes of the slice: x: 4 (x_hi: 2, x_lo: 2; x = x_hi * 2 + x_lo), y: 8, z: 8, core: 2. Of those that a mesh axis runs over, the one named last changes fastest.
Arguments:
- pair: bfloat16 [384, 384, 128], P('ia', 'ja'), may hold values from -6 to 6
- token_mask: int32 [384], replicated, may hold values 0 or 1
- norm_in_gain: float32 [128], replicated, may hold values from 0.1 to 1.9
- norm_in_bias: float32 [128], replicated, may hold values from -3 to 3
- left_gate: bfloat16 [128, 128], replicated, may hold values from -0.5 to 0.5
- left_value: bfloat16 [128, 128], replicated, may hold values from -0.5 to 0.5
- right_gate: bfloat16 [128, 128], replicated, may hold values from -0.5 to 0.5
- right_value: bfloat16 [128, 128], replicated, may hold values from -0.5 to 0.5
- output_gate: bfloat16 [128, 128], replicated, may hold values from -0.5 to 0.5
- norm_out_gain: float32 [128], replicated, may hold values from 0.1 to 1.9
- norm_out_bias: float32 [128], replicated, may hold values from -3 to 3
- output_weight: bfloat16 [128, 128], replicated, may hold values from -0.5 to 0.5
Outputs:
- update: bfloat16 [384, 384, 128], P('ia', 'ja')
All inputs are finite; a program needn't handle non-finite values.
Results may differ from a plain program's by a relative error of at most 0.0054.
Values may be sent and summed in bfloat16 or wider, within the bound.
No kernel may reach another device: no remote copies, remote signals or barrier semaphores. Data moves between devices by JAX's collectives and lax.ppermute only.
A program may use at most 64 MiB of HBM per device.

v0:
```python
import jax
import jax.numpy as jnp
from jax import lax
from jax.sharding import PartitionSpec as P


def from_root(shard, axis, root):
    mine = lax.axis_index(axis) == root
    return lax.psum(jnp.where(mine, shard, jnp.zeros_like(shard)), axis)


def layer_norm(values, gain, bias):
    mean = jnp.mean(values, axis=-1, keepdims=True)
    centered = values - mean
    variance = jnp.mean(centered * centered, axis=-1, keepdims=True)
    return centered * lax.rsqrt(variance + 1e-05) * gain + bias


def shards(
    pair,
    token_mask,
    norm_in_gain,
    norm_in_bias,
    left_gate,
    left_value,
    right_gate,
    right_value,
    output_gate,
    norm_out_gain,
    norm_out_bias,
    output_weight,
):
    rows, cols, width = pair.shape
    hidden = left_gate.shape[1]
    row_index = lax.axis_index("ia")
    col_index = lax.axis_index("ja")
    normed = layer_norm(pair.astype(jnp.float32), norm_in_gain, norm_in_bias).astype(jnp.bfloat16)
    flat = normed.reshape(rows * cols, width)
    weights = jnp.concatenate([left_gate, left_value, right_gate, right_value, output_gate], axis=1)
    projected = jnp.dot(flat, weights, preferred_element_type=jnp.float32).reshape(
        rows, cols, 4 * hidden + width
    )
    row_valid = lax.dynamic_slice_in_dim(token_mask, row_index * rows, rows).astype(jnp.float32)
    col_valid = lax.dynamic_slice_in_dim(token_mask, col_index * cols, cols).astype(jnp.float32)
    pair_mask = (row_valid[:, None] * col_valid[None, :])[:, :, None]
    left = (
        pair_mask * jax.nn.sigmoid(projected[:, :, :hidden]) * projected[:, :, hidden : 2 * hidden]
    ).astype(jnp.bfloat16)
    right = (
        pair_mask
        * jax.nn.sigmoid(projected[:, :, 2 * hidden : 3 * hidden])
        * projected[:, :, 3 * hidden : 4 * hidden]
    ).astype(jnp.bfloat16)
    gated = jax.nn.sigmoid(projected[:, :, 4 * hidden :])
    ratio = cols // rows
    right_whole = lax.all_gather(right, "ja", axis=1, tiled=True)
    blocks = []
    for offset in range(ratio):
        blocks.append(from_root(right_whole, "ia", col_index * ratio + offset))
    right_block = jnp.concatenate(blocks, axis=0)
    left_whole = lax.all_gather(left, "ja", axis=1, tiled=True)
    mixed = jnp.einsum("ikc,jkc->ijc", left_whole, right_block, preferred_element_type=jnp.float32)
    mixed_normed = layer_norm(mixed, norm_out_gain, norm_out_bias).astype(jnp.bfloat16)
    output = jnp.dot(
        mixed_normed.reshape(rows * cols, hidden), output_weight, preferred_element_type=jnp.float32
    )
    return (gated * output.reshape(rows, cols, width)).astype(jnp.bfloat16)


def solution(mesh):
    placed = (P("ia", "ja", None), P(), P(), P(), P(), P(), P(), P(), P(), P(), P(), P())
    return jax.shard_map(
        shards, mesh=mesh, in_specs=placed, out_specs=P("ia", "ja", None), check_vma=False
    )
```

profile of v0, /device:TPU:1, one launch (start us, length us, event | category | flops | bytes accessed | tf_op | source)
XLA Modules:
  0.0 437.0 jit_solution(11378134321547657740)
XLA Ops:
  6.5 0.0 copy-start
  6.5 0.0 all-gather.3.cloned.1.call-start
  6.5 0.8 dynamic-slice_convert_fusion.1
  7.3 0.8 dynamic-slice_convert_fusion
  8.1 1.0 convert_reduce_fusion
  9.1 1.1 fusion.5
  10.2 0.8 constant_dynamic-update-slice_fusion.4
  10.9 0.1 broadcast_multiply_fusion
  11.0 0.8 constant_dynamic-update-slice_fusion.3
  11.8 0.8 constant_dynamic-update-slice_fusion.2
  12.5 0.8 constant_dynamic-update-slice_fusion.1
  13.3 0.8 constant_dynamic-update-slice_fusion
  14.1 1.3 fusion.3
  15.3 0.8 fusion.9
  16.1 0.0 all-gather.3.cloned.1.call-update
  16.1 0.0 all-gather.5.cloned.1.call-start
  16.2 0.7 all-gather.5.cloned.1.call-update
  16.9 0.0 all-reduce.3.cloned.1.call-start
  16.9 84.4 %all-gather.3.cloned.1.call-done = bf16[12,384,128]{2,1,0:T(8,128)(2,1)} async-done(((bf16[12,24,128]{2,1,0:T(8,128)(2,1)}), bf16[12,384,128]{2,1,0:T(8,128)(2,1)}) %all-gather.3.cloned.1.call-update) | async-done | bytes 1179664 | tf_op jit(solution)/shard_map/all_gather | solution.py:56
  101.3 2.9 broadcast_select_fusion.1
  104.2 0.0 all-reduce.3.cloned.1.call-update
  104.3 79.3 %all-gather.5.cloned.1.call-done = bf16[12,384,128]{2,1,0:T(8,128)(2,1)} async-done(((bf16[12,24,128]{2,1,0:T(8,128)(2,1)}), bf16[12,384,128]{2,1,0:T(8,128)(2,1)}) %all-gather.5.cloned.1.call-update) | async-done | bytes 1179664 | tf_op jit(solution)/shard_map/all_gather | solution.py:61
  183.6 3.0 copy.17
  186.6 234.5 %all-reduce.3.cloned.1.call-done = (bf16[12,384,128]{2,1,0:T(8,128)(2,1)}, bf16[12,384,128]{2,1,0:T(8,128)(2,1)}) async-done(((bf16[12,384,128]{2,1,0:T(8,128)(2,1)}, bf16[12,384,128]{2,1,0:T(8,128)(2,1)}), (bf16[12,384,128]{2,1,0:T(8,128)(2,1)}, bf16[12,384,128]{2,1,0:T(8,128)(2,1)})) %all-reduce.3.cloned.1.call-update) | async-done | bytes 2359312 | tf_op jit(solution)/shard_map/psum | solution.py:9
  421.1 1.8 pad_maximum_fusion
  422.9 2.8 copy.16
  425.7 3.2 fusion.32
  428.9 0.3 copy.18
  429.2 0.1 bitcast_reduce_fusion
  429.3 0.2 multiply_reduce_fusion
  429.6 0.0 copy-done
  429.6 0.9 fusion
  (8 shorter events, 0.0 us)
Async XLA Ops:
  6.5 423.0 %copy-start = (bf16[128,128]{1,0:T(8,128)(2,1)S(1)}, bf16[128,128]{1,0:T(8,128)(2,1)}, u32[]{:S(2)}) copy-start(bf16[128,128]{1,0:T(8,128)(2,1)} %param.23) | copy-start | bytes 98308
  6.5 94.8 %all-gather.3.cloned.1.call-start = ((), (), s32[]{:S(2)}) async-start(), calls=%async_computation | async-start | bytes 1253376 | tf_op jit(solution)/shard_map/all_gather | solution.py:56
  16.1 167.5 %all-gather.5.cloned.1.call-start = ((), (), s32[]{:S(2)}) async-start(), calls=%async_computation.1 | async-start | bytes 1253376 | tf_op jit(solution)/shard_map/all_gather | solution.py:61
  16.9 404.2 %all-reduce.3.cloned.1.call-start = ((), (), s32[]{:S(2)}) async-start(), calls=%async_computation.2 | async-start | bytes 4718592 | tf_op jit(solution)/shard_map/psum | solution.py:9
  425.7 3.9 copy-start.1
  425.7 3.9 copy-start.2
Sparse Core Ops, SparseCore 0:
  16.3 85.0 all-gather.2
  104.4 79.1 all-gather.4
  186.6 234.4 all-reduce.2
where the time goes:
time: 438 us; the launch traced here: 437 us
  waiting for transfers between devices  399 us (91%)
  between operations  13.2 us (3%)
  local copies, waits for them, and re-layouts  9.98 us (2%)
  other arithmetic  9.5 us (2%)
  matrix products  5.32 us (1%)
    psum x1, waiting for transfers between devices, from_root(): return lax.psum(jnp.where(mine, shard, jnp.zeros_like(shard)), axis)  234 us
    all_gather x1, waiting for transfers between devices, shards(): right_whole = lax.all_gather(right, 'ja', axis=1, tiled=True)  84.4 us
    all_gather x1, waiting for transfers between devices, shards(): left_whole = lax.all_gather(left, 'ja', axis=1, tiled=True)  79.3 us
  transfers between devices with their start and end apart: 3, of which 3 were waited for; matrix products, arithmetic and copies ran while one was open for 1% of the time, Pallas kernels for 0%

commit v1 on v0

v1 whole, which is shorter than its diff:
```python
import jax
import jax.numpy as jnp
import numpy as np
from jax import lax
from jax.experimental import pallas as pl
from jax.experimental.pallas import tpu as pltpu
from jax.sharding import Mesh
from jax.sharding import PartitionSpec as P

AXES = ("xl", "y2", "y1", "y0", "c", "xh", "z2", "z1", "z0")
ROWS = ("xl", "y2", "y1", "y0", "c")
COLS = ("xh", "z2", "z1", "z0")
NEAR = ("xl", "y0", "c", "xh", "z0")
EPS = 1e-5
WIDE = 32
F32 = jnp.float32
BF16 = jnp.bfloat16
VMEM = pl.BlockSpec(memory_space=pltpu.VMEM)
SMEM = pl.BlockSpec(memory_space=pltpu.SMEM)


def sigmoid(x):
    return 1.0 / (1.0 + jnp.exp(-x))


def iota(shape, axis):
    return lax.broadcasted_iota(jnp.int32, shape, axis)


def contract(a, b, da, db):
    return lax.dot_general(a, b, (((da,), (db,)), ((), ())), preferred_element_type=F32)


def edges_kernel(place_ref, mask_ref, pair_ref, gain_ref, bias_ref, lg_ref, lv_ref, rg_ref, rv_ref, og_ref, sent_ref, gate_ref):
    rows, cols, width = pair_ref.shape
    x = pair_ref[...].astype(F32).reshape(rows * cols, width)
    mean = jnp.mean(x, axis=-1, keepdims=True)
    centered = x - mean
    variance = jnp.mean(centered * centered, axis=-1, keepdims=True)
    normed = centered * lax.rsqrt(variance + EPS) * gain_ref[...] + bias_ref[...]
    rounded = normed.astype(BF16)
    gate_ref[...] = sigmoid(contract(rounded, og_ref[...], 1, 0))
    place = iota((cols, width), 0)
    col_valid = jnp.zeros((cols, width), F32)
    for k in range(cols):
        col_valid = jnp.where(place == k, mask_ref[place_ref[1] + k].astype(F32), col_valid)
    parts = []
    for i in range(rows):
        row_valid = mask_ref[place_ref[0] + i].astype(F32)
        parts.append(normed[i * cols : (i + 1) * cols] * (col_valid * row_valid))
        parts.append(jnp.zeros((WIDE - cols, width), F32))
    masked = jnp.concatenate(parts, axis=0).astype(BF16)
    left = sigmoid(contract(lg_ref[...], masked, 0, 1)) * contract(lv_ref[...], masked, 0, 1)
    right = sigmoid(contract(rg_ref[...], masked, 0, 1)) * contract(rv_ref[...], masked, 0, 1)
    lanes = rows * WIDE
    left = left.reshape(width // 8, 8, lanes)
    right = right.reshape(width // 8, 8, lanes)
    low = iota((1, 8, lanes), 1) < 4
    even = jnp.where(low, left, pltpu.roll(right, 4, 1))
    odd = jnp.where(low, pltpu.roll(left, 4, 1), right)
    for t in range(width // 8):
        sent_ref[2 * t] = even[t].astype(BF16)
        sent_ref[2 * t + 1] = odd[t].astype(BF16)


def swap_blocks(blocks, lane):
    out = []
    for b in range(4):
        total = None
        for a in range(4):
            moved = blocks[a] if a == b else pltpu.roll(blocks[a], (WIDE * (a - b)) % 128, blocks[a].ndim - 1)
            total = moved if total is None else jnp.where(lane // WIDE == a, moved, total)
        out.append(total)
    return out


def arrange_kernel(got_ref, left_ref, right_ref, rows_ref):
    lane = iota((8, 128), 1)
    for g in range(8):
        for q in range(3):
            blocks = [got_ref[g * 4 + kg, :, q * 128 : (q + 1) * 128].astype(F32) for kg in range(4)]
            for ii, block in enumerate(swap_blocks(blocks, lane)):
                rows_ref[pl.ds((g * 12 + q * 4 + ii) * 8, 8), :] = block
    for c in range(4):
        left = rows_ref[pl.ds(c, 96, stride=8), :].astype(BF16)
        for copy in range(4):
            left_ref[copy, c] = left
        right_ref[c] = rows_ref[pl.ds(4 + c, 96, stride=8), :].astype(BF16)


def mix_kernel(place_ref, left_ref, r0_ref, r1_ref, r2_ref, r3_ref, sent_ref, wide_ref, rows_ref):
    lane = iota((96, 128), 1)
    wide_ref[...] = jnp.zeros((96, 128), F32)
    for c in range(4):
        mixed = None
        for s, r_ref in enumerate((r0_ref, r1_ref, r2_ref, r3_ref)):
            part = contract(left_ref[lax.rem(place_ref[2] + 4 - s, 4), c], r_ref[c], 1, 1)
            mixed = part if mixed is None else mixed + part
        wide_ref[:, 0:96] = mixed
        flat = wide_ref[...]
        spread = flat
        for jg in range(1, 4):
            spread = jnp.where(lane // WIDE == jg, pltpu.roll(flat, 8 * jg, 1), spread)
        spread = jnp.where(lane % WIDE < 24, spread, 0.0)
        high = spread.astype(BF16).astype(F32)
        rows_ref[pl.ds(c, 96, stride=8), :] = high
        rows_ref[pl.ds(4 + c, 96, stride=8), :] = spread - high
    lane = iota((8, 128), 1)
    for g in range(8):
        for q in range(3):
            blocks = [rows_ref[pl.ds((g * 12 + q * 4 + ii) * 8, 8), :] for ii in range(4)]
            for jg, block in enumerate(swap_blocks(blocks, lane)):
                sent_ref[g * 4 + jg, :, q * 128 : (q + 1) * 128] = block.astype(BF16)


def update_kernel(got_ref, gate_ref, gain_ref, bias_ref, weight_ref, out_ref):
    rows, cols, width = out_ref.shape
    lanes = rows * WIDE
    low = iota((8, lanes), 0) < 4
    tiles = []
    for t in range(width // 8):
        pair = []
        for p in (2 * t, 2 * t + 1):
            both = got_ref[p].astype(F32)
            pair.append(both + pltpu.roll(both, 4, 0))
        tiles.append(jnp.where(low, pair[0], pair[1]))
    mixed = jnp.concatenate(tiles, axis=0)
    mean = jnp.mean(mixed, axis=0, keepdims=True)
    centered = mixed - mean
    variance = jnp.mean(centered * centered, axis=0, keepdims=True)
    gain = jnp.transpose(jnp.broadcast_to(gain_ref[...], (width, width)))[:, 0:1]
    bias = jnp.transpose(jnp.broadcast_to(bias_ref[...], (width, width)))[:, 0:1]
    normed = (centered * lax.rsqrt(variance + EPS) * gain + bias).astype(BF16)
    output = contract(normed, weight_ref[...], 0, 0)
    for i in range(rows):
        gated = gate_ref[i * cols : (i + 1) * cols] * output[i * WIDE : i * WIDE + cols]
        out_ref[i] = gated.astype(BF16)


def shards(
    pair,
    token_mask,
    norm_in_gain,
    norm_in_bias,
    left_gate,
    left_value,
    right_gate,
    right_value,
    output_gate,
    norm_out_gain,
    norm_out_bias,
    output_weight,
):
    rows, cols, width = pair.shape
    params = pltpu.CompilerParams(vmem_limit_bytes=32 * 1024 * 1024)
    row_block = lax.axis_index(("y2", "y1"))
    place = jnp.stack([lax.axis_index(ROWS) * rows, lax.axis_index(COLS) * cols, row_block, row_block]).astype(jnp.int32)
    struct = jax.ShapeDtypeStruct
    sent, gate = pl.pallas_call(
        edges_kernel,
        name="edges",
        out_shape=(struct((32, 8, rows * WIDE), BF16), struct((rows * cols, width), F32)),
        in_specs=[SMEM, SMEM] + [VMEM] * 8,
        out_specs=(VMEM, VMEM),
        compiler_params=params,
    )(place, token_mask, pair, norm_in_gain.reshape(1, -1), norm_in_bias.reshape(1, -1), left_gate, left_value, right_gate, right_value, output_gate)
    got = lax.all_to_all(sent, NEAR, 0, 0)
    left, right = pl.pallas_call(
        arrange_kernel,
        name="arrange",
        out_shape=(struct((4, 4, 96, 128), BF16), struct((4, 96, 128), BF16)),
        in_specs=[VMEM],
        out_specs=(VMEM, VMEM),
        scratch_shapes=[pltpu.VMEM((768, 128), F32)],
        compiler_params=params,
    )(got)
    lefts = lax.all_to_all(left, ("z2", "z1"), 0, 0)
    rights = []
    for shift in range(4):
        moves = [(y * 4 + z, ((z + shift) % 4) * 4 + y) for y in range(4) for z in range(4)]
        rights.append(lax.ppermute(right, ("y2", "y1", "z2", "z1"), moves))
    sent = pl.pallas_call(
        mix_kernel,
        name="mix",
        out_shape=struct((32, 8, rows * WIDE), BF16),
        in_specs=[SMEM] + [VMEM] * 5,
        out_specs=VMEM,
        scratch_shapes=[pltpu.VMEM((96, 128), F32), pltpu.VMEM((768, 128), F32)],
        compiler_params=params,
    )(place, lefts, *rights)
    got = lax.all_to_all(sent, NEAR, 0, 0)
    return pl.pallas_call(
        update_kernel,
        name="update",
        out_shape=struct((rows, cols, width), BF16),
        in_specs=[VMEM] * 5,
        out_specs=VMEM,
        compiler_params=params,
    )(got, gate, norm_out_gain.reshape(1, -1), norm_out_bias.reshape(1, -1), output_weight)


def solution(mesh):
    fine = Mesh(np.asarray(mesh.devices).reshape((2,) * len(AXES)), AXES)
    placed = (P(ROWS, COLS, None),) + (P(),) * 11
    return jax.shard_map(shards, mesh=fine, in_specs=placed, out_specs=P(ROWS, COLS, None), check_vma=False)
```

time: 438 us -> 78.8 us (0.18)
  the two profiles are of different devices: /device:TPU:1 before, /device:TPU:48 now
where the time goes in v1:
time: 78.8 us; the launch traced here: 78.1 us
  starting transfers between devices  32.5 us (41%)
  blocking collectives  26.1 us (33%)
  waiting for transfers between devices  9.8 us (12%)
  local copies, waits for them, and re-layouts  5.27 us (7%)
  Pallas kernels  4.28 us (5%)
    all_to_all x2, blocking collectives, shards(): got = lax.all_to_all(sent, NEAR, 0, 0)  26.1 us
    ppermute x4, starting transfers between devices, shards(): rights.append(lax.ppermute(right, ('y2', 'y1', 'z2', 'z1'), moves))  23.1 us
    ppermute x4, waiting for transfers between devices, shards(): rights.append(lax.ppermute(right, ('y2', 'y1', 'z2', 'z1'), moves))  9.79 us
    all_to_all x1, starting transfers between devices, shards(): lefts = lax.all_to_all(left, ('z2', 'z1'), 0, 0)  9.4 us
    unnamed x24, local copies, waits for them, and re-layouts  5.27 us
  transfers between devices with their start and end apart: 5, of which 2 were waited for; matrix products, arithmetic and copies ran while one was open for 0% of the time, Pallas kernels for 0%

profile of v1, /device:TPU:48, one launch (start us, length us, event | category | flops | bytes accessed | tf_op | source)
XLA Modules:
  0.0 78.1 jit_solution(8722073133011189657)
XLA Ops:
  0.0 0.0 copy-start
  0.0 0.1 pad_add_fusion.place_ref
  0.1 0.0 copy-start.7
  0.1 0.8 %copy-done = bf16[12,24,128]{2,1,0:T(8,128)(2,1)S(1)} copy-done((bf16[12,24,128]{2,1,0:T(8,128)(2,1)S(1)}, bf16[12,24,128]{2,1,0:T(8,128)(2,1)}, u32[]{:S(2)}) %copy-start) | copy-done | bytes 73752
  0.9 0.0 copy-done.7
  0.9 0.0 copy-done.8
  0.9 0.0 copy-done.9
  0.9 0.8 copy-done.2
  1.7 0.8 copy-done.3
  2.4 0.8 copy-done.4
  3.2 0.8 copy-done.5
  3.9 0.8 copy-done.6
  4.7 1.0 %edges.1 = (bf16[32,8,384]{2,1,0:T(8,128)(2,1)S(1)}, f32[288,128]{1,0:T(8,128)S(1)}) custom-call(s32[4]{0:T(128)S(1)} %pad_add_fusion.place_ref, s32[384]{0:T(512)S(1)} %copy-done.7, bf16[12,24,128]{2,1,0:T(8,128)(2,1)S(1)} %copy-done, f32[1,128]{1,0:T(1,128)S(1)} %bitcast.7, f32[1,128]{1,0:T(1,128)S(1)} %bitcast.8, bf16[128,128]{1,0:T(8,128)(2,1)S(1)} %copy-done.2, ...), custom_call_target="tpu_custom_call" | custom-call | tf_op jit(solution)/shard_map/edges/pallas_call | solution.py:159
  5.7 14.7 %all_to_all.15.got_ref = bf16[32,8,384]{2,1,0:T(8,128)(2,1)S(1)} all-to-all(bf16[32,8,384]{2,1,0:T(8,128)(2,1)S(1)} %get-tuple-element.9), channel_id=1, replica_groups=mesh['xl'=2,'y2'=2,'y1'=2,'y0'=2,'c'=2,'xh'=2,'z2'=2,'z1'=2,'z0'=2] {'xl..., dimensions={0} | all-to-all | bytes 393216 | tf_op jit(solution)/shard_map/all_to_all | solution.py:167
  20.4 1.0 %arrange.1 = (bf16[4,4,96,128]{3,2,1,0:T(8,128)(2,1)}, bf16[4,96,128]{2,1,0:T(8,128)(2,1)S(1)}) custom-call(bf16[32,8,384]{2,1,0:T(8,128)(2,1)S(1)} %all_to_all.15.got_ref), custom_call_target="tpu_custom_call" | custom-call | tf_op jit(solution)/shard_map/arrange/pallas_call | solution.py:168
  21.4 9.4 %all-to-all-start.1 = ((bf16[4,4,96,128]{3,2,1,0:T(8,128)(2,1)}), bf16[4,4,96,128]{3,2,1,0:T(8,128)(2,1)S(1)}, u32[]{:S(2)}, u32[]{:S(2)}) async-start(bf16[4,4,96,128]{3,2,1,0:T(8,128)(2,1)} %get-tuple-element.10), calls=%async_computation.1 | async-start | bytes 786432 | tf_op jit(solution)/shard_map/all_to_all | solution.py:177
  30.9 6.0 %collective-permute-start.3 = (bf16[4,96,128]{2,1,0:T(8,128)(2,1)S(1)}, bf16[4,96,128]{2,1,0:T(8,128)(2,1)S(1)}, u32[]{:S(2)}, u32[]{:S(2)}) collective-permute-start(bf16[4,96,128]{2,1,0:T(8,128)(2,1)S(1)} %get-tuple-element.11), channel_id=1, source_target_pairs={{0,192},{2,0},{4,64},{6,128},{64,194},{66,2},{68,66},{70,130},{128... | collective-permute-start | bytes 294920 | tf_op jit(solution)/shard_map/ppermute | solution.py:181
  36.9 5.8 %collective-permute-start.2 = (bf16[4,96,128]{2,1,0:T(8,128)(2,1)S(1)}, bf16[4,96,128]{2,1,0:T(8,128)(2,1)S(1)}, u32[]{:S(2)}, u32[]{:S(2)}) collective-permute-start(bf16[4,96,128]{2,1,0:T(8,128)(2,1)S(1)} %get-tuple-element.11), channel_id=1, source_target_pairs={{0,128},{2,192},{4,0},{6,64},{64,130},{66,194},{68,2},{70,66},{128... | collective-permute-start | bytes 294920 | tf_op jit(solution)/shard_map/ppermute | solution.py:181
  42.7 4.9 %collective-permute-start.1 = (bf16[4,96,128]{2,1,0:T(8,128)(2,1)S(1)}, bf16[4,96,128]{2,1,0:T(8,128)(2,1)S(1)}, u32[]{:S(2)}, u32[]{:S(2)}) collective-permute-start(bf16[4,96,128]{2,1,0:T(8,128)(2,1)S(1)} %get-tuple-element.11), channel_id=1, source_target_pairs={{0,64},{2,128},{4,192},{6,0},{64,66},{66,130},{68,194},{70,2},{128... | collective-permute-start | bytes 294920 | tf_op jit(solution)/shard_map/ppermute | solution.py:181
  47.7 6.3 %collective-permute-start = (bf16[4,96,128]{2,1,0:T(8,128)(2,1)S(1)}, bf16[4,96,128]{2,1,0:T(8,128)(2,1)S(1)}, u32[]{:S(2)}, u32[]{:S(2)}) collective-permute-start(bf16[4,96,128]{2,1,0:T(8,128)(2,1)S(1)} %get-tuple-element.11), channel_id=1, source_target_pairs={{0,0},{2,64},{4,128},{6,192},{64,2},{66,66},{68,130},{70,194},{128... | collective-permute-start | bytes 294920 | tf_op jit(solution)/shard_map/ppermute | solution.py:181
  53.9 0.0 collective-permute-done.3.r3_ref
  54.0 0.0 collective-permute-done.2.r2_ref
  54.0 8.0 %collective-permute-done.1.r1_ref = bf16[4,96,128]{2,1,0:T(8,128)(2,1)S(1)} collective-permute-done((bf16[4,96,128]{2,1,0:T(8,128)(2,1)S(1)}, bf16[4,96,128]{2,1,0:T(8,128)(2,1)S(1)}, u32[]{:S(2)}, u32[]{:S(2)}) %collective-permute-start.1) | collective-permute-done | bytes 98336 | tf_op jit(solution)/shard_map/ppermute | solution.py:181
  62.0 1.8 %collective-permute-done.r0_ref = bf16[4,96,128]{2,1,0:T(8,128)(2,1)S(1)} collective-permute-done((bf16[4,96,128]{2,1,0:T(8,128)(2,1)S(1)}, bf16[4,96,128]{2,1,0:T(8,128)(2,1)S(1)}, u32[]{:S(2)}, u32[]{:S(2)}) %collective-permute-start) | collective-permute-done | bytes 98336 | tf_op jit(solution)/shard_map/ppermute | solution.py:181
  63.7 0.0 all-to-all-done.1.left_ref
  63.8 1.2 %mix.1 = bf16[32,8,384]{2,1,0:T(8,128)(2,1)S(1)} custom-call(s32[4]{0:T(128)S(1)} %pad_add_fusion.place_ref, bf16[4,4,96,128]{3,2,1,0:T(8,128)(2,1)S(1)} %all-to-all-done.1.left_ref, bf16[4,96,128]{2,1,0:T(8,128)(2,1)S(1)} %collective-permute-done.r0_ref, bf16[4,96,128]{2,1,0:T(8,128)(2,1)S(1)} %collective-permute-done.1.r1_ref, ...), custom_call_target="tpu_custom_call" | custom-call | tf_op jit(solution)/shard_map/mix/pallas_call | solution.py:182
  65.0 0.0 copy-start.1
  65.0 11.4 %all_to_all.16.got_ref = bf16[32,8,384]{2,1,0:T(8,128)(2,1)S(1)} all-to-all(bf16[32,8,384]{2,1,0:T(8,128)(2,1)S(1)} %mix.1), channel_id=1, replica_groups=mesh['xl'=2,'y2'=2,'y1'=2,'y0'=2,'c'=2,'xh'=2,'z2'=2,'z1'=2,'z0'=2] {'xl..., dimensions={0} | all-to-all | bytes 393216 | tf_op jit(solution)/shard_map/all_to_all | solution.py:191
  76.4 0.0 copy-done.1
  76.4 0.6 copy-done.10
  77.0 0.0 copy-done.11
  77.1 1.0 %update.1 = bf16[12,24,128]{2,1,0:T(8,128)(2,1)} custom-call(bf16[32,8,384]{2,1,0:T(8,128)(2,1)S(1)} %all_to_all.16.got_ref, f32[288,128]{1,0:T(8,128)S(1)} %get-tuple-element.12.gate_ref, f32[1,128]{1,0:T(1,128)S(1)} %bitcast.9, f32[1,128]{1,0:T(1,128)S(1)} %bitcast.10, bf16[128,128]{1,0:T(8,128)(2,1)S(1)} %copy-done.1), custom_call_target="tpu_custom_call" | custom-call | tf_op jit(solution)/shard_map/update/pallas_call | solution.py:192
  (9 shorter events, 0.0 us)
Async XLA Ops:
  0.0 0.9 %copy-start = (bf16[12,24,128]{2,1,0:T(8,128)(2,1)S(1)}, bf16[12,24,128]{2,1,0:T(8,128)(2,1)}, u32[]{:S(2)}) copy-start(bf16[12,24,128]{2,1,0:T(8,128)(2,1)} %pair_ref.1) | copy-start | bytes 221188
  0.1 0.8 %copy-start.7 = (s32[384]{0:T(512)S(1)}, s32[384]{0:T(512)}, u32[]{:S(2)}) copy-start(s32[384]{0:T(512)} %mask_ref.1) | copy-start | bytes 4612
  0.1 0.8 %copy-start.8 = (f32[128]{0:T(128)S(1)}, f32[128]{0:T(128)}, u32[]{:S(2)}) copy-start(f32[128]{0:T(128)} %param.14) | copy-start | bytes 1540
  0.1 0.8 %copy-start.9 = (f32[128]{0:T(128)S(1)}, f32[128]{0:T(128)}, u32[]{:S(2)}) copy-start(f32[128]{0:T(128)} %param.15) | copy-start | bytes 1540
  0.9 0.8 copy-start.2
  1.7 0.8 copy-start.3
  2.4 0.8 copy-start.4
  3.2 0.8 copy-start.5
  3.9 0.8 copy-start.6
  21.4 42.3 %all-to-all-start.1 = ((bf16[4,4,96,128]{3,2,1,0:T(8,128)(2,1)}), bf16[4,4,96,128]{3,2,1,0:T(8,128)(2,1)S(1)}, u32[]{:S(2)}, u32[]{:S(2)}) async-start(bf16[4,4,96,128]{3,2,1,0:T(8,128)(2,1)} %get-tuple-element.10), calls=%async_computation.1 | async-start | bytes 786432 | tf_op jit(solution)/shard_map/all_to_all | solution.py:177
  30.9 23.1 %collective-permute-start.3 = (bf16[4,96,128]{2,1,0:T(8,128)(2,1)S(1)}, bf16[4,96,128]{2,1,0:T(8,128)(2,1)S(1)}, u32[]{:S(2)}, u32[]{:S(2)}) collective-permute-start(bf16[4,96,128]{2,1,0:T(8,128)(2,1)S(1)} %get-tuple-element.11), channel_id=1, source_target_pairs={{0,192},{2,0},{4,64},{6,128},{64,194},{66,2},{68,66},{70,130},{128... | collective-permute-start | bytes 294920 | tf_op jit(solution)/shard_map/ppermute | solution.py:181
  36.9 17.1 %collective-permute-start.2 = (bf16[4,96,128]{2,1,0:T(8,128)(2,1)S(1)}, bf16[4,96,128]{2,1,0:T(8,128)(2,1)S(1)}, u32[]{:S(2)}, u32[]{:S(2)}) collective-permute-start(bf16[4,96,128]{2,1,0:T(8,128)(2,1)S(1)} %get-tuple-element.11), channel_id=1, source_target_pairs={{0,128},{2,192},{4,0},{6,64},{64,130},{66,194},{68,2},{70,66},{128... | collective-permute-start | bytes 294920 | tf_op jit(solution)/shard_map/ppermute | solution.py:181
  42.7 19.2 %collective-permute-start.1 = (bf16[4,96,128]{2,1,0:T(8,128)(2,1)S(1)}, bf16[4,96,128]{2,1,0:T(8,128)(2,1)S(1)}, u32[]{:S(2)}, u32[]{:S(2)}) collective-permute-start(bf16[4,96,128]{2,1,0:T(8,128)(2,1)S(1)} %get-tuple-element.11), channel_id=1, source_target_pairs={{0,64},{2,128},{4,192},{6,0},{64,66},{66,130},{68,194},{70,2},{128... | collective-permute-start | bytes 294920 | tf_op jit(solution)/shard_map/ppermute | solution.py:181
  47.7 16.1 %collective-permute-start = (bf16[4,96,128]{2,1,0:T(8,128)(2,1)S(1)}, bf16[4,96,128]{2,1,0:T(8,128)(2,1)S(1)}, u32[]{:S(2)}, u32[]{:S(2)}) collective-permute-start(bf16[4,96,128]{2,1,0:T(8,128)(2,1)S(1)} %get-tuple-element.11), channel_id=1, source_target_pairs={{0,0},{2,64},{4,128},{6,192},{64,2},{66,66},{68,130},{70,194},{128... | collective-permute-start | bytes 294920 | tf_op jit(solution)/shard_map/ppermute | solution.py:181
  65.0 11.4 %copy-start.1 = (bf16[128,128]{1,0:T(8,128)(2,1)S(1)}, bf16[128,128]{1,0:T(8,128)(2,1)}, u32[]{:S(2)}) copy-start(bf16[128,128]{1,0:T(8,128)(2,1)} %weight_ref.1) | copy-start | bytes 98308
  76.4 0.7 copy-start.10
  76.4 0.7 copy-start.11

commit v2 on v1

--- a/solution.py
+++ b/solution.py
@@ -17,6 +17,7 @@
 BF16 = jnp.bfloat16
 VMEM = pl.BlockSpec(memory_space=pltpu.VMEM)
 SMEM = pl.BlockSpec(memory_space=pltpu.SMEM)
+HBM = pl.BlockSpec(memory_space=pltpu.HBM)
 
 
 def sigmoid(x):
@@ -31,7 +32,29 @@
     return lax.dot_general(a, b, (((da,), (db,)), ((), ())), preferred_element_type=F32)
 
 
-def edges_kernel(place_ref, mask_ref, pair_ref, gain_ref, bias_ref, lg_ref, lv_ref, rg_ref, rv_ref, og_ref, sent_ref, gate_ref):
+def edges_kernel(
+    place_ref,
+    mask_ref,
+    pair_ref,
+    gain_ref,
+    bias_ref,
+    out_gain_ref,
+    out_bias_ref,
+    lg_hbm,
+    lv_hbm,
+    rg_hbm,
+    rv_hbm,
+    og_hbm,
+    sent_ref,
+    gate_ref,
+    columns_ref,
+    weights_ref,
+    arrived,
+):
+    copies = []
+    for n, source in enumerate((og_hbm, lg_hbm, lv_hbm, rg_hbm, rv_hbm)):
+        copies.append(pltpu.make_async_copy(source, weights_ref.at[n], arrived.at[n]))
+        copies[n].start()
     rows, cols, width = pair_ref.shape
     x = pair_ref[...].astype(F32).reshape(rows * cols, width)
     mean = jnp.mean(x, axis=-1, keepdims=True)
@@ -39,7 +62,8 @@
     variance = jnp.mean(centered * centered, axis=-1, keepdims=True)
     normed = centered * lax.rsqrt(variance + EPS) * gain_ref[...] + bias_ref[...]
     rounded = normed.astype(BF16)
-    gate_ref[...] = sigmoid(contract(rounded, og_ref[...], 1, 0))
+    columns_ref[0] = jnp.transpose(jnp.broadcast_to(out_gain_ref[...], (width, width)))
+    columns_ref[1] = jnp.transpose(jnp.broadcast_to(out_bias_ref[...], (width, width)))
     place = iota((cols, width), 0)
     col_valid = jnp.zeros((cols, width), F32)
     for k in range(cols):
@@ -50,8 +74,11 @@
         parts.append(normed[i * cols : (i + 1) * cols] * (col_valid * row_valid))
         parts.append(jnp.zeros((WIDE - cols, width), F32))
     masked = jnp.concatenate(parts, axis=0).astype(BF16)
-    left = sigmoid(contract(lg_ref[...], masked, 0, 1)) * contract(lv_ref[...], masked, 0, 1)
-    right = sigmoid(contract(rg_ref[...], masked, 0, 1)) * contract(rv_ref[...], masked, 0, 1)
+    for copy in copies:
+        copy.wait()
+    gate_ref[...] = sigmoid(contract(rounded, weights_ref[0], 1, 0))
+    left = sigmoid(contract(weights_ref[1], masked, 0, 1)) * contract(weights_ref[2], masked, 0, 1)
+    right = sigmoid(contract(weights_ref[3], masked, 0, 1)) * contract(weights_ref[4], masked, 0, 1)
     lanes = rows * WIDE
     left = left.reshape(width // 8, 8, lanes)
     right = right.reshape(width // 8, 8, lanes)
@@ -81,21 +108,30 @@
             blocks = [got_ref[g * 4 + kg, :, q * 128 : (q + 1) * 128].astype(F32) for kg in range(4)]
             for ii, block in enumerate(swap_blocks(blocks, lane)):
                 rows_ref[pl.ds((g * 12 + q * 4 + ii) * 8, 8), :] = block
-    for c in range(4):
-        left = rows_ref[pl.ds(c, 96, stride=8), :].astype(BF16)
-        for copy in range(4):
-            left_ref[copy, c] = left
-        right_ref[c] = rows_ref[pl.ds(4 + c, 96, stride=8), :].astype(BF16)
-
-
-def mix_kernel(place_ref, left_ref, r0_ref, r1_ref, r2_ref, r3_ref, sent_ref, wide_ref, rows_ref):
+    wide = iota((96, 128), 1) % WIDE < 24
+    for side in range(2):
+        found = [rows_ref[pl.ds(4 * side + c, 96, stride=8), :] for c in range(4)]
+        for v in range(3):
+            dense = jnp.where(wide, found[v], pltpu.roll(found[3], 24 - 8 * v, 1)).astype(BF16)
+            if side == 0:
+                for copy in range(4):
+                    left_ref[copy, :, v * 128 : (v + 1) * 128] = dense
+            else:
+                right_ref[:, v * 128 : (v + 1) * 128] = dense
+
+
+def mix_kernel(left_ref, right_ref, sent_ref, wide_ref, rows_ref):
     lane = iota((96, 128), 1)
     wide_ref[...] = jnp.zeros((96, 128), F32)
     for c in range(4):
         mixed = None
-        for s, r_ref in enumerate((r0_ref, r1_ref, r2_ref, r3_ref)):
-            part = contract(left_ref[lax.rem(place_ref[2] + 4 - s, 4), c], r_ref[c], 1, 1)
-            mixed = part if mixed is None else mixed + part
+        for s in range(4):
+            for v in (c,) if c < 3 else (0, 1, 2):
+                held = (lane % WIDE < 24) if c < 3 else (lane % WIDE >= 24)
+                left = left_ref[s, :, v * 128 : (v + 1) * 128]
+                left = jnp.where(held, left, jnp.zeros_like(left))
+                part = contract(left, right_ref[s, :, v * 128 : (v + 1) * 128], 1, 1)
+                mixed = part if mixed is None else mixed + part
         wide_ref[:, 0:96] = mixed
         flat = wide_ref[...]
         spread = flat
@@ -113,7 +149,7 @@
                 sent_ref[g * 4 + jg, :, q * 128 : (q + 1) * 128] = block.astype(BF16)
 
 
-def update_kernel(got_ref, gate_ref, gain_ref, bias_ref, weight_ref, out_ref):
+def update_kernel(got_ref, gate_ref, columns_ref, weight_ref, out_ref):
     rows, cols, width = out_ref.shape
     lanes = rows * WIDE
     low = iota((8, lanes), 0) < 4
@@ -128,9 +164,7 @@
     mean = jnp.mean(mixed, axis=0, keepdims=True)
     centered = mixed - mean
     variance = jnp.mean(centered * centered, axis=0, keepdims=True)
-    gain = jnp.transpose(jnp.broadcast_to(gain_ref[...], (width, width)))[:, 0:1]
-    bias = jnp.transpose(jnp.broadcast_to(bias_ref[...], (width, width)))[:, 0:1]
-    normed = (centered * lax.rsqrt(variance + EPS) * gain + bias).astype(BF16)
+    normed = (centered * lax.rsqrt(variance + EPS) * columns_ref[0][:, 0:1] + columns_ref[1][:, 0:1]).astype(BF16)
     output = contract(normed, weight_ref[...], 0, 0)
     for i in range(rows):
         gated = gate_ref[i * cols : (i + 1) * cols] * output[i * WIDE : i * WIDE + cols]
@@ -153,50 +187,65 @@
 ):
     rows, cols, width = pair.shape
     params = pltpu.CompilerParams(vmem_limit_bytes=32 * 1024 * 1024)
-    row_block = lax.axis_index(("y2", "y1"))
-    place = jnp.stack([lax.axis_index(ROWS) * rows, lax.axis_index(COLS) * cols, row_block, row_block]).astype(jnp.int32)
+    place = jnp.stack([lax.axis_index(ROWS) * rows, lax.axis_index(COLS) * cols]).astype(jnp.int32)
     struct = jax.ShapeDtypeStruct
-    sent, gate = pl.pallas_call(
+    sent, gate, columns = pl.pallas_call(
         edges_kernel,
         name="edges",
-        out_shape=(struct((32, 8, rows * WIDE), BF16), struct((rows * cols, width), F32)),
-        in_specs=[SMEM, SMEM] + [VMEM] * 8,
-        out_specs=(VMEM, VMEM),
-        compiler_params=params,
-    )(place, token_mask, pair, norm_in_gain.reshape(1, -1), norm_in_bias.reshape(1, -1), left_gate, left_value, right_gate, right_value, output_gate)
+        out_shape=(
+            struct((32, 8, rows * WIDE), BF16),
+            struct((rows * cols, width), F32),
+            struct((2, width, width), F32),
+        ),
+        in_specs=[SMEM, SMEM] + [VMEM] * 5 + [HBM] * 5,
+        out_specs=(VMEM, VMEM, VMEM),
+        scratch_shapes=[pltpu.VMEM((5, width, width), BF16), pltpu.SemaphoreType.DMA((5,))],
+        compiler_params=params,
+    )(
+        place,
+        token_mask,
+        pair,
+        norm_in_gain.reshape(1, -1),
+        norm_in_bias.reshape(1, -1),
+        norm_out_gain.reshape(1, -1),
+        norm_out_bias.reshape(1, -1),
+        left_gate,
+        left_value,
+        right_gate,
+        right_value,
+        output_gate,
+    )
     got = lax.all_to_all(sent, NEAR, 0, 0)
     left, right = pl.pallas_call(
         arrange_kernel,
         name="arrange",
-        out_shape=(struct((4, 4, 96, 128), BF16), struct((4, 96, 128), BF16)),
+        out_shape=(struct((4, 96, 384), BF16), struct((96, 384), BF16)),
         in_specs=[VMEM],
         out_specs=(VMEM, VMEM),
         scratch_shapes=[pltpu.VMEM((768, 128), F32)],
         compiler_params=params,
     )(got)
     lefts = lax.all_to_all(left, ("z2", "z1"), 0, 0)
-    rights = []
-    for shift in range(4):
-        moves = [(y * 4 + z, ((z + shift) % 4) * 4 + y) for y in range(4) for z in range(4)]
-        rights.append(lax.ppermute(right, ("y2", "y1", "z2", "z1"), moves))
+    right = lax.ppermute(right, ("y2", "y1", "z2", "z1"), [(y * 4 + z, z * 4 + y) for y in range(4) for z in range(4)])
+    rights = lax.all_to_all(jnp.broadcast_to(right, (4, 96, 384)), ("y2", "y1"), 0, 0)
     sent = pl.pallas_call(
         mix_kernel,
         name="mix",
         out_shape=struct((32, 8, rows * WIDE), BF16),
-        in_specs=[SMEM] + [VMEM] * 5,
+        in_specs=[VMEM] * 2,
         out_specs=VMEM,
         scratch_shapes=[pltpu.VMEM((96, 128), F32), pltpu.VMEM((768, 128), F32)],
         compiler_params=params,
-    )(place, lefts, *rights)
+    )(lefts, rights)
     got = lax.all_to_all(sent, NEAR, 0, 0)
     return pl.pallas_call(
         update_kernel,
         name="update",
         out_shape=struct((rows, cols, width), BF16),
-        in_specs=[VMEM] * 5,
+        in_specs=[VMEM] * 4,
         out_specs=VMEM,
         compiler_params=params,
-    )(got, gate, norm_out_gain.reshape(1, -1), norm_out_bias.reshape(1, -1), output_weight)
+    )(got, gate, columns, output_weight)
 
 
 def solution(mesh):

time: 78.8 us -> 79.2 us (level)
  the two profiles are of different devices: /device:TPU:48 before, /device:TPU:1 now
where the time goes in v2:
time: 79.2 us; the launch traced here: 78.5 us
  blocking collectives  53 us (67%)
  starting transfers between devices  8.78 us (11%)
  waiting for transfers between devices  7.64 us (10%)
  local copies, waits for them, and re-layouts  4.62 us (6%)
  Pallas kernels  4.26 us (5%)
    all_to_all x2, blocking collectives, shards(): got = lax.all_to_all(sent, NEAR, 0, 0)  32 us
    all_to_all x1, blocking collectives, shards(): lax.all_to_all(jnp.broadcast_to(right, (4, 96, 384)), ('y2', 'y1'), 0, 0)  21 us
    all_to_all x1, starting transfers between devices, shards(): lefts = lax.all_to_all(left, ('z2', 'z1'), 0, 0)  8.12 us
    all_to_all x1, waiting for transfers between devices, shards(): lefts = lax.all_to_all(left, ('z2', 'z1'), 0, 0)  7.64 us
    unnamed x24, local copies, waits for them, and re-layouts  4.6 us
  transfers between devices with their start and end apart: 2, of which 1 were waited for; matrix products, arithmetic and copies ran while one was open for 0% of the time, Pallas kernels for 0%

profile of v2, /device:TPU:1, one launch (start us, length us, event | category | flops | bytes accessed | tf_op | source)
XLA Modules:
  0.0 78.5 jit_solution(1079726157253517768)
XLA Ops:
  0.0 0.0 copy-start
  0.0 0.1 pad_add_fusion.place_ref
  0.1 0.0 copy-start.11
  0.1 0.0 copy-start.7
  0.1 0.0 copy-start.8
  0.1 0.0 copy-start.9
  0.1 0.0 copy-start.10
  0.1 0.8 copy-done
  0.9 0.0 copy-done.11
  0.9 0.0 copy-done.7
  0.9 0.0 copy-done.8
  0.9 0.0 copy-done.9
  0.9 0.0 copy-done.10
  0.9 0.0 copy-start.2
  0.9 0.7 copy-done.2
  1.7 0.8 copy-done.3
  2.4 0.8 copy-done.4
  3.2 0.8 copy-done.5
  3.9 0.8 copy-done.6
  4.7 1.4 %edges.1 = (bf16[32,8,384]{2,1,0:T(8,128)(2,1)S(1)}, f32[288,128]{1,0:T(8,128)S(1)}, f32[2,128,128]{2,1,0:T(8,128)S(1)}) custom-call(s32[2]{0:T(128)S(1)} %pad_add_fusion.place_ref, s32[384]{0:T(512)S(1)} %copy-done.7, bf16[12,24,128]{2,1,0:T(8,128)(2,1)S(1)} %copy-done, f32[1,128]{1,0:T(1,128)S(1)} %bitcast.6, f32[1,128]{1,0:T(1,128)S(1)} %bitcast.7, ...), custom_call_target="tpu_custom_call" | custom-call | tf_op jit(solution)/shard_map/edges/pallas_call | solution.py:192
  6.1 16.8 %all_to_all.20.got_ref = bf16[32,8,384]{2,1,0:T(8,128)(2,1)S(1)} all-to-all(bf16[32,8,384]{2,1,0:T(8,128)(2,1)S(1)} %get-tuple-element.10), channel_id=1, replica_groups=mesh['xl'=2,'y2'=2,'y1'=2,'y0'=2,'c'=2,'xh'=2,'z2'=2,'z1'=2,'z0'=2] {'xl..., dimensions={0} | all-to-all | bytes 393216 | tf_op jit(solution)/shard_map/all_to_all | solution.py:218
  23.0 1.0 %arrange.1 = (bf16[4,96,384]{2,1,0:T(8,128)(2,1)}, bf16[96,384]{1,0:T(8,128)(2,1)S(1)}) custom-call(bf16[32,8,384]{2,1,0:T(8,128)(2,1)S(1)} %all_to_all.20.got_ref), custom_call_target="tpu_custom_call" | custom-call | tf_op jit(solution)/shard_map/arrange/pallas_call | solution.py:219
  24.0 8.1 %all-to-all-start.1 = ((bf16[4,96,384]{2,1,0:T(8,128)(2,1)}), bf16[4,96,384]{2,1,0:T(8,128)(2,1)S(1)}, u32[]{:S(2)}, u32[]{:S(2)}) async-start(bf16[4,96,384]{2,1,0:T(8,128)(2,1)} %get-tuple-element.11), calls=%async_computation.1 | async-start | bytes 589824 | tf_op jit(solution)/shard_map/all_to_all | solution.py:228
  32.1 0.7 collective-permute-start
  32.8 0.0 collective-permute-done
  32.8 7.6 %all-to-all-done.1.left_ref = bf16[4,96,384]{2,1,0:T(8,128)(2,1)S(1)} async-done(((bf16[4,96,384]{2,1,0:T(8,128)(2,1)}), bf16[4,96,384]{2,1,0:T(8,128)(2,1)S(1)}, u32[]{:S(2)}, u32[]{:S(2)}) %all-to-all-start.1) | async-done | bytes 294944 | tf_op jit(solution)/shard_map/all_to_all | solution.py:228
  40.5 21.0 %all_to_all.21.right_ref = bf16[4,96,384]{2,1,0:T(8,128)(2,1)S(1)} all-to-all(bf16[4,96,384]{2,1,0:T(8,128)(2,1)S(1)} %broadcast_in_dim.3), channel_id=1, replica_groups=mesh['xl'=2,'y2'=2,'y1'=2,'y0'=2,'c'=2,'xh'=2,'z2'=2,'z1'=2,'z0'=2] {'y2..., dimensions={0} | all-to-all | bytes 589824 | tf_op jit(solution)/shard_map/all_to_all | solution.py:230
  61.5 0.8 %mix.1 = bf16[32,8,384]{2,1,0:T(8,128)(2,1)S(1)} custom-call(bf16[4,96,384]{2,1,0:T(8,128)(2,1)S(1)} %all-to-all-done.1.left_ref, bf16[4,96,384]{2,1,0:T(8,128)(2,1)S(1)} %all_to_all.21.right_ref), custom_call_target="tpu_custom_call" | custom-call | tf_op jit(solution)/shard_map/mix/pallas_call | solution.py:231
  62.4 0.0 copy-start.1
  62.4 15.2 %all_to_all.22.got_ref = bf16[32,8,384]{2,1,0:T(8,128)(2,1)S(1)} all-to-all(bf16[32,8,384]{2,1,0:T(8,128)(2,1)S(1)} %mix.1), channel_id=1, replica_groups=mesh['xl'=2,'y2'=2,'y1'=2,'y0'=2,'c'=2,'xh'=2,'z2'=2,'z1'=2,'z0'=2] {'xl..., dimensions={0} | all-to-all | bytes 393216 | tf_op jit(solution)/shard_map/all_to_all | solution.py:240
  77.5 0.0 copy-done.1
  77.5 1.0 %update.1 = bf16[12,24,128]{2,1,0:T(8,128)(2,1)} custom-call(bf16[32,8,384]{2,1,0:T(8,128)(2,1)S(1)} %all_to_all.22.got_ref, f32[288,128]{1,0:T(8,128)S(1)} %get-tuple-element.13.gate_ref, f32[2,128,128]{2,1,0:T(8,128)S(1)} %get-tuple-element.14.columns_ref, bf16[128,128]{1,0:T(8,128)(2,1)S(1)} %copy-done.1), custom_call_target="tpu_custom_call" | custom-call | tf_op jit(solution)/shard_map/update/pallas_call | solution.py:241
  (5 shorter events, 0.0 us)
Async XLA Ops:
  0.0 0.9 %copy-start = (bf16[12,24,128]{2,1,0:T(8,128)(2,1)S(1)}, bf16[12,24,128]{2,1,0:T(8,128)(2,1)}, u32[]{:S(2)}) copy-start(bf16[12,24,128]{2,1,0:T(8,128)(2,1)} %pair_ref.1) | copy-start | bytes 221188
  0.1 0.8 %copy-start.11 = (f32[128]{0:T(128)S(1)}, f32[128]{0:T(128)}, u32[]{:S(2)}) copy-start(f32[128]{0:T(128)} %param.22) | copy-start | bytes 1540
  0.1 0.8 %copy-start.7 = (s32[384]{0:T(512)S(1)}, s32[384]{0:T(512)}, u32[]{:S(2)}) copy-start(s32[384]{0:T(512)} %mask_ref.1) | copy-start | bytes 4612
  0.1 0.8 %copy-start.8 = (f32[128]{0:T(128)S(1)}, f32[128]{0:T(128)}, u32[]{:S(2)}) copy-start(f32[128]{0:T(128)} %param.14) | copy-start | bytes 1540
  0.1 0.8 %copy-start.9 = (f32[128]{0:T(128)S(1)}, f32[128]{0:T(128)}, u32[]{:S(2)}) copy-start(f32[128]{0:T(128)} %param.15) | copy-start | bytes 1540
  0.1 0.8 %copy-start.10 = (f32[128]{0:T(128)S(1)}, f32[128]{0:T(128)}, u32[]{:S(2)}) copy-start(f32[128]{0:T(128)} %param.21) | copy-start | bytes 1540
  0.9 0.8 copy-start.2
  1.7 0.8 copy-start.3
  2.4 0.8 copy-start.4
  3.2 0.8 copy-start.5
  3.9 0.8 copy-start.6
  24.0 16.4 %all-to-all-start.1 = ((bf16[4,96,384]{2,1,0:T(8,128)(2,1)}), bf16[4,96,384]{2,1,0:T(8,128)(2,1)S(1)}, u32[]{:S(2)}, u32[]{:S(2)}) async-start(bf16[4,96,384]{2,1,0:T(8,128)(2,1)} %get-tuple-element.11), calls=%async_computation.1 | async-start | bytes 589824 | tf_op jit(solution)/shard_map/all_to_all | solution.py:228
  32.1 0.7 collective-permute-start
  62.4 15.2 %copy-start.1 = (bf16[128,128]{1,0:T(8,128)(2,1)S(1)}, bf16[128,128]{1,0:T(8,128)(2,1)}, u32[]{:S(2)}) copy-start(bf16[128,128]{1,0:T(8,128)(2,1)} %weight_ref.1) | copy-start | bytes 98308

commit v3 on v1

v3 whole, which is shorter than its diff:
```python
import jax
import jax.numpy as jnp
from jax import lax
from jax.experimental import pallas as pl
from jax.experimental.pallas import tpu as pltpu
from jax.sharding import PartitionSpec as P

BOTH = ("ia", "ja")
EPS = 1e-5
WIDE = 32
F32 = jnp.float32
BF16 = jnp.bfloat16
VMEM = pl.BlockSpec(memory_space=pltpu.VMEM)
SMEM = pl.BlockSpec(memory_space=pltpu.SMEM)


def device(xl, y, core, xh, z):
    return (((xl * 8 + y) * 2 + core) * 2 + xh) * 8 + z


def fold(half, m):
    return m if half == 0 else 7 - m


SHARING = [
    [device(xl, fold(half, m), core, xh, z) for xl in range(2) for m in range(4) for xh in range(2) for z in range(8)]
    for half in range(2)
    for core in range(2)
]
SAME = [[group[n] for group in SHARING] for n in range(128)]


def sigmoid(x):
    return 1.0 / (1.0 + jnp.exp(-x))


def iota(shape, axis):
    return lax.broadcasted_iota(jnp.int32, shape, axis)


def contract(a, b, da, db):
    return lax.dot_general(a, b, (((da,), (db,)), ((), ())), preferred_element_type=F32)


def norm_kernel(place_ref, mask_ref, pair_ref, gain_ref, bias_ref, out_gain_ref, out_bias_ref, normed_ref, masked_ref, columns_ref):
    rows, cols, width = pair_ref.shape
    x = pair_ref[...].astype(F32).reshape(rows * cols, width)
    mean = jnp.mean(x, axis=-1, keepdims=True)
    centered = x - mean
    variance = jnp.mean(centered * centered, axis=-1, keepdims=True)
    normed = centered * lax.rsqrt(variance + EPS) * gain_ref[...] + bias_ref[...]
    normed_ref[...] = normed.astype(BF16)
    columns_ref[0] = jnp.transpose(jnp.broadcast_to(out_gain_ref[...], (width, width)))
    columns_ref[1] = jnp.transpose(jnp.broadcast_to(out_bias_ref[...], (width, width)))
    place = iota((cols, width), 0)
    col_valid = jnp.zeros((cols, width), F32)
    for k in range(cols):
        col_valid = jnp.where(place == k, mask_ref[place_ref[1] + k].astype(F32), col_valid)
    parts = []
    for i in [3 * ii + iq for iq in range(3) for ii in range(4)]:
        row_valid = mask_ref[place_ref[0] + i].astype(F32)
        parts.append(normed[i * cols : (i + 1) * cols] * (col_valid * row_valid))
        parts.append(jnp.zeros((WIDE - cols, width), F32))
    masked_ref[...] = jnp.concatenate(parts, axis=0).astype(BF16)


def edges_kernel(normed_ref, masked_ref, lg_ref, lv_ref, rg_ref, rv_ref, og_ref, sent_ref, gate_ref, rows_ref):
    width = lg_ref.shape[0]
    masked = masked_ref[...]
    left = sigmoid(contract(lg_ref[...], masked, 0, 1)) * contract(lv_ref[...], masked, 0, 1)
    right = sigmoid(contract(rg_ref[...], masked, 0, 1)) * contract(rv_ref[...], masked, 0, 1)
    for iq in range(3):
        rows_ref[pl.ds(iq, width, stride=8), :] = right[:, iq * 128 : (iq + 1) * 128]
        rows_ref[pl.ds(3 + iq, width, stride=8), :] = left[:, iq * 128 : (iq + 1) * 128]
    for iq in range(6, 8):
        rows_ref[pl.ds(iq, width, stride=8), :] = jnp.zeros((width, 128), F32)
    sent_ref[...] = rows_ref[...].reshape(width, 8, 128).astype(BF16)
    gate_ref[...] = sigmoid(contract(normed_ref[...], og_ref[...], 1, 0))


def swap_blocks(blocks, lane):
    out = []
    for b in range(4):
        total = None
        for a in range(4):
            moved = blocks[a] if a == b else pltpu.roll(blocks[a], (WIDE * (a - b)) % 128, blocks[a].ndim - 1)
            total = moved if total is None else jnp.where(lane // WIDE == a, moved, total)
        out.append(total)
    return out


def arrange_kernel(got_ref, left_ref, right_ref, rows_ref, padded_ref):
    lane = iota((8, 128), 1)
    padded_ref[...] = jnp.zeros_like(padded_ref)
    for g in range(8):
        for quad in range(4):
            blocks = [got_ref[g * 16 + quad * 4 + k].astype(F32) for k in range(4)]
            for ii, block in enumerate(swap_blocks(blocks, lane)):
                rows_ref[quad, pl.ds((g * 4 + ii) * 8, 8), :] = block
                padded_ref[quad, pl.ds(g * 16 + ii * 3, 3), :] = block[0:3]
    wide = iota((32, 128), 1) % WIDE < 24
    for iq in range(3):
        found = [rows_ref[quad, pl.ds(3 + iq, 32, stride=8), :] for quad in range(4)]
        for v in range(3):
            dense = jnp.where(wide, found[v], pltpu.roll(found[3], 24 - 8 * v, 1))
            left_ref[iq * 32 : (iq + 1) * 32, v * 128 : (v + 1) * 128] = dense.astype(BF16)
    wide = iota((128, 128), 1) % WIDE < 24
    for v in range(3):
        dense = jnp.where(wide, padded_ref[v], pltpu.roll(padded_ref[3], 24 - 8 * v, 1)).astype(BF16)
        for copy in range(4):
            right_ref[copy, :, v * 128 : (v + 1) * 128] = dense


def mix_kernel(left_ref, right_ref, sent_ref, rows_ref):
    lane = iota((8, 128), 1)
    left = left_ref[...]
    for quad in range(4):
        pieces = []
        for k in range(quad * 4, quad * 4 + 4):
            xl, y = k // 8, k % 8
            half, m = (0, y) if y < 4 else (1, 7 - y)
            at = (xl * 4 + m) * 16
            for core in range(2):
                pieces.append(right_ref[half * 2 + core, at : at + 16, :])
        mixed = contract(left, jnp.concatenate(pieces, axis=0), 1, 1)
        high = mixed.astype(BF16).astype(F32)
        low = mixed - high
        for iq in range(3):
            rows_ref[pl.ds(iq, 32, stride=8), :] = high[iq * 32 : (iq + 1) * 32]
            rows_ref[pl.ds(3 + iq, 32, stride=8), :] = low[iq * 32 : (iq + 1) * 32]
        for iq in range(6, 8):
            rows_ref[pl.ds(iq, 32, stride=8), :] = jnp.zeros((32, 128), F32)
        for g in range(8):
            blocks = [rows_ref[pl.ds((g * 4 + ii) * 8, 8), :] for ii in range(4)]
            for k, block in enumerate(swap_blocks(blocks, lane)):
                sent_ref[g * 16 + quad * 4 + k] = block.astype(BF16)


def update_kernel(got_ref, gate_ref, columns_ref, weight_ref, out_ref, rows_ref, flat_ref):
    rows, cols, width = out_ref.shape
    rows_ref[...] = got_ref[...].astype(F32).reshape(width * 8, 128)
    gain = columns_ref[0][:, 0:1]
    bias = columns_ref[1][:, 0:1]
    for iq in range(3):
        mixed = rows_ref[pl.ds(iq, width, stride=8), :] + rows_ref[pl.ds(3 + iq, width, stride=8), :]
        mean = jnp.mean(mixed, axis=0, keepdims=True)
        centered = mixed - mean
        variance = jnp.mean(centered * centered, axis=0, keepdims=True)
        normed = (centered * lax.rsqrt(variance + EPS) * gain + bias).astype(BF16)
        output = contract(normed, weight_ref[...], 0, 0)
        for ii in range(4):
            at = (3 * ii + iq) * cols
            flat_ref[at : at + 12, :] = output[ii * WIDE : ii * WIDE + 12]
            flat_ref[at + 12 : at + 24, :] = output[ii * WIDE + 16 : ii * WIDE + 28]
    out_ref[...] = (gate_ref[...] * flat_ref[...]).astype(BF16).reshape(rows, cols, width)


def shards(
    pair,
    token_mask,
    norm_in_gain,
    norm_in_bias,
    left_gate,
    left_value,
    right_gate,
    right_value,
    output_gate,
    norm_out_gain,
    norm_out_bias,
    output_weight,
):
    rows, cols, width = pair.shape
    params = pltpu.CompilerParams(vmem_limit_bytes=32 * 1024 * 1024)
    place = jnp.stack([lax.axis_index("ia") * rows, lax.axis_index("ja") * cols]).astype(jnp.int32)
    struct = jax.ShapeDtypeStruct
    normed, masked, columns = pl.pallas_call(
        norm_kernel,
        name="norm",
        out_shape=(
            struct((rows * cols, width), BF16),
            struct((rows * WIDE, width), BF16),
            struct((2, width, width), F32),
        ),
        in_specs=[SMEM, SMEM] + [VMEM] * 5,
        out_specs=(VMEM, VMEM, VMEM),
        compiler_params=params,
    )(
        place,
        token_mask,
        pair,
        norm_in_gain.reshape(1, -1),
        norm_in_bias.reshape(1, -1),
        norm_out_gain.reshape(1, -1),
        norm_out_bias.reshape(1, -1),
    )
    sent, gate = pl.pallas_call(
        edges_kernel,
        name="edges",
        out_shape=(struct((128, 8, 128), BF16), struct((rows * cols, width), F32)),
        in_specs=[VMEM] * 7,
        out_specs=(VMEM, VMEM),
        scratch_shapes=[pltpu.VMEM((1024, 128), F32)],
        compiler_params=params,
    )(normed, masked, left_gate, left_value, right_gate, right_value, output_gate)
    got = lax.all_to_all(sent, BOTH, 0, 0, axis_index_groups=SHARING)
    left, right = pl.pallas_call(
        arrange_kernel,
        name="arrange",
        out_shape=(struct((96, 384), BF16), struct((4, 128, 384), BF16)),
        in_specs=[VMEM],
        out_specs=(VMEM, VMEM),
        scratch_shapes=[pltpu.VMEM((4, 256, 128), F32), pltpu.VMEM((4, 128, 128), F32)],
        compiler_params=params,
    )(got)
    rights = lax.all_to_all(right, BOTH, 0, 0, axis_index_groups=SAME)
    sent = pl.pallas_call(
        mix_kernel,
        name="mix",
        out_shape=struct((128, 8, 128), BF16),
        in_specs=[VMEM] * 2,
        out_specs=VMEM,
        scratch_shapes=[pltpu.VMEM((256, 128), F32)],
        compiler_params=params,
    )(left, rights)
    got = lax.all_to_all(sent, BOTH, 0, 0, axis_index_groups=SHARING)
    return pl.pallas_call(
        update_kernel,
        name="update",
        out_shape=struct((rows, cols, width), BF16),
        in_specs=[VMEM] * 4,
        out_specs=VMEM,
        scratch_shapes=[pltpu.VMEM((1024, 128), F32), pltpu.VMEM((rows * cols, 128), F32)],
        compiler_params=params,
    )(got, gate, columns, output_weight)


def solution(mesh):
    placed = (P("ia", "ja", None),) + (P(),) * 11
    return jax.shard_map(shards, mesh=mesh, in_specs=placed, out_specs=P("ia", "ja", None), check_vma=False)
```

time: 78.8 us -> 75.4 us (0.957)
  the two profiles are of different devices: /device:TPU:48 before, /device:TPU:1 now
where the time goes in v3:
time: 75.4 us; the launch traced here: 74.9 us
  blocking collectives  67.8 us (90%)
  local copies, waits for them, and re-layouts  3.87 us (5%)
  Pallas kernels  3.07 us (4%)
    all_to_all x2, blocking collectives, shards(): got = lax.all_to_all(sent, BOTH, 0, 0, axis_index_groups=SHARING)  50 us
    all_to_all x1, blocking collectives, shards(): rights = lax.all_to_all(right, BOTH, 0, 0, axis_index_groups=SAME)  17.9 us
    unnamed x24, local copies, waits for them, and re-layouts  3.87 us

profile of v3, /device:TPU:1, one launch (start us, length us, event | category | flops | bytes accessed | tf_op | source)
XLA Modules:
  0.0 74.9 jit_solution(16896058166415002153)
XLA Ops:
  0.0 0.1 pad_add_fusion.place_ref
  0.1 0.0 copy-start.11
  0.1 0.0 copy-start.7
  0.1 0.0 copy-start.8
  0.1 0.0 copy-start.9
  0.1 0.0 copy-start.10
  0.1 0.6 copy-done.11
  0.7 0.0 copy-done.7
  0.8 0.0 copy-done.8
  0.8 0.0 copy-done.9
  0.8 0.0 copy-done.10
  0.8 0.0 copy-start
  0.8 0.9 %copy-done = bf16[12,24,128]{2,1,0:T(8,128)(2,1)S(1)} copy-done((bf16[12,24,128]{2,1,0:T(8,128)(2,1)S(1)}, bf16[12,24,128]{2,1,0:T(8,128)(2,1)}, u32[]{:S(2)}) %copy-start) | copy-done | bytes 73752
  1.7 0.0 copy-start.2
  1.7 0.0 copy-start.3
  1.7 0.8 %norm.1 = (bf16[288,128]{1,0:T(8,128)(2,1)S(1)}, bf16[384,128]{1,0:T(8,128)(2,1)S(1)}, f32[2,128,128]{2,1,0:T(8,128)S(1)}) custom-call(s32[2]{0:T(128)S(1)} %pad_add_fusion.place_ref, s32[384]{0:T(512)S(1)} %copy-done.7, bf16[12,24,128]{2,1,0:T(8,128)(2,1)S(1)} %copy-done, f32[1,128]{1,0:T(1,128)S(1)} %bitcast.6, f32[1,128]{1,0:T(1,128)S(1)} %bitcast.7, ...), custom_call_target="tpu_custom_call" | custom-call | tf_op jit(solution)/shard_map/norm/pallas_call | solution.py:176
  2.5 0.0 copy-done.2
  2.5 0.0 copy-done.3
  2.5 0.0 copy-start.4
  2.5 0.7 copy-done.4
  3.3 0.0 copy-start.5
  3.3 0.8 %copy-done.5 = bf16[128,128]{1,0:T(8,128)(2,1)S(1)} copy-done((bf16[128,128]{1,0:T(8,128)(2,1)S(1)}, bf16[128,128]{1,0:T(8,128)(2,1)}, u32[]{:S(2)}) %copy-start.5) | copy-done | bytes 32792
  4.0 0.8 %copy-done.6 = bf16[128,128]{1,0:T(8,128)(2,1)S(1)} copy-done((bf16[128,128]{1,0:T(8,128)(2,1)S(1)}, bf16[128,128]{1,0:T(8,128)(2,1)}, u32[]{:S(2)}) %copy-start.6) | copy-done | bytes 32792
  4.8 0.4 edges.1
  5.2 31.4 %all_to_all.15.got_ref = bf16[128,8,128]{2,1,0:T(8,128)(2,1)S(1)} all-to-all(bf16[128,8,128]{2,1,0:T(8,128)(2,1)S(1)} %get-tuple-element.14), channel_id=1, replica_groups={{0,1,2,3,4,5,6,7,8,9,10,11,12,13,14,15,32,33,34,35,36,37,38,39,40,41,42..., dimensions={0} | all-to-all | bytes 524288 | tf_op jit(solution)/shard_map/all_to_all | solution.py:205
  36.6 0.4 arrange.1
  37.0 17.9 %all_to_all.16.right_ref = bf16[4,128,384]{2,1,0:T(8,128)(2,1)S(1)} all-to-all(bf16[4,128,384]{2,1,0:T(8,128)(2,1)S(1)} %get-tuple-element.16), channel_id=1, replica_groups={{0,16,224,240},{1,17,225,241},{2,18,226,242},{3,19,227,243},{4,20,228,2..., dimensions={0} | all-to-all | bytes 786432 | tf_op jit(solution)/shard_map/all_to_all | solution.py:215
  54.9 0.5 mix.1
  55.4 0.0 copy-start.1
  55.4 18.5 %all_to_all.17.got_ref = bf16[128,8,128]{2,1,0:T(8,128)(2,1)S(1)} all-to-all(bf16[128,8,128]{2,1,0:T(8,128)(2,1)S(1)} %mix.1), channel_id=1, replica_groups={{0,1,2,3,4,5,6,7,8,9,10,11,12,13,14,15,32,33,34,35,36,37,38,39,40,41,42..., dimensions={0} | all-to-all | bytes 524288 | tf_op jit(solution)/shard_map/all_to_all | solution.py:225
  73.9 0.0 copy-done.1
  73.9 1.0 %update.1 = bf16[12,24,128]{2,1,0:T(8,128)(2,1)} custom-call(bf16[128,8,128]{2,1,0:T(8,128)(2,1)S(1)} %all_to_all.17.got_ref, f32[288,128]{1,0:T(8,128)S(1)} %get-tuple-element.17.gate_ref, f32[2,128,128]{2,1,0:T(8,128)S(1)} %get-tuple-element.18.columns_ref, bf16[128,128]{1,0:T(8,128)(2,1)S(1)} %copy-done.1), custom_call_target="tpu_custom_call" | custom-call | tf_op jit(solution)/shard_map/update/pallas_call | solution.py:226
  (1 shorter events, 0.0 us)
Async XLA Ops:
  0.1 0.7 copy-start.11
  0.1 0.7 copy-start.7
  0.1 0.7 copy-start.8
  0.1 0.7 copy-start.9
  0.1 0.7 copy-start.10
  0.8 0.9 %copy-start = (bf16[12,24,128]{2,1,0:T(8,128)(2,1)S(1)}, bf16[12,24,128]{2,1,0:T(8,128)(2,1)}, u32[]{:S(2)}) copy-start(bf16[12,24,128]{2,1,0:T(8,128)(2,1)} %pair_ref.1) | copy-start | bytes 221188
  1.7 0.8 %copy-start.2 = (bf16[128,128]{1,0:T(8,128)(2,1)S(1)}, bf16[128,128]{1,0:T(8,128)(2,1)}, u32[]{:S(2)}) copy-start(bf16[128,128]{1,0:T(8,128)(2,1)} %lg_ref.1) | copy-start | bytes 98308
  1.7 0.8 %copy-start.3 = (bf16[128,128]{1,0:T(8,128)(2,1)S(1)}, bf16[128,128]{1,0:T(8,128)(2,1)}, u32[]{:S(2)}) copy-start(bf16[128,128]{1,0:T(8,128)(2,1)} %lv_ref.1) | copy-start | bytes 98308
  2.5 0.8 %copy-start.4 = (bf16[128,128]{1,0:T(8,128)(2,1)S(1)}, bf16[128,128]{1,0:T(8,128)(2,1)}, u32[]{:S(2)}) copy-start(bf16[128,128]{1,0:T(8,128)(2,1)} %rg_ref.1) | copy-start | bytes 98308
  3.3 0.8 %copy-start.5 = (bf16[128,128]{1,0:T(8,128)(2,1)S(1)}, bf16[128,128]{1,0:T(8,128)(2,1)}, u32[]{:S(2)}) copy-start(bf16[128,128]{1,0:T(8,128)(2,1)} %rv_ref.1) | copy-start | bytes 98308
  4.0 0.8 %copy-start.6 = (bf16[128,128]{1,0:T(8,128)(2,1)S(1)}, bf16[128,128]{1,0:T(8,128)(2,1)}, u32[]{:S(2)}) copy-start(bf16[128,128]{1,0:T(8,128)(2,1)} %og_ref.1) | copy-start | bytes 98308
  55.4 18.5 %copy-start.1 = (bf16[128,128]{1,0:T(8,128)(2,1)S(1)}, bf16[128,128]{1,0:T(8,128)(2,1)}, u32[]{:S(2)}) copy-start(bf16[128,128]{1,0:T(8,128)(2,1)} %weight_ref.1) | copy-start | bytes 98308

commit v4 on v3

v4 whole, which is shorter than its diff:
```python
import jax
import jax.numpy as jnp
from jax import lax
from jax.experimental import pallas as pl
from jax.experimental.pallas import tpu as pltpu
from jax.sharding import PartitionSpec as P

BOTH = ("ia", "ja")
EPS = 1e-5
WIDE = 32
NORM_BYTES = 32 * 1024 * 1024
F32 = jnp.float32
BF16 = jnp.bfloat16
VMEM = pl.BlockSpec(memory_space=pltpu.VMEM)
SMEM = pl.BlockSpec(memory_space=pltpu.SMEM)


def device(xl, y, core, xh, z):
    return (((xl * 8 + y) * 2 + core) * 2 + xh) * 8 + z


def fold(half, m):
    return m if half == 0 else 7 - m


SHARING = [
    [device(xl, fold(half, m), core, xh, z) for xl in range(2) for m in range(4) for xh in range(2) for z in range(8)]
    for half in range(2)
    for core in range(2)
]
PLACES = [(xl, y, core, xh, z) for xl in range(2) for y in range(8) for core in range(2) for xh in range(2) for z in range(8)]
CORE_FLIP = [(device(xl, y, core, xh, z), device(xl, y, 1 - core, xh, z)) for xl, y, core, xh, z in PLACES]
HALF_FLIP = [(device(xl, y, core, xh, z), device(xl, 7 - y, core, xh, z)) for xl, y, core, xh, z in PLACES]


def sigmoid(x):
    return 1.0 / (1.0 + jnp.exp(-x))


def iota(shape, axis):
    return lax.broadcasted_iota(jnp.int32, shape, axis)


def contract(a, b, da, db):
    return lax.dot_general(a, b, (((da,), (db,)), ((), ())), preferred_element_type=F32)


def norm_kernel(place_ref, mask_ref, pair_ref, gain_ref, bias_ref, normed_ref, masked_ref):
    rows, cols, width = pair_ref.shape
    x = pair_ref[...].astype(F32).reshape(rows * cols, width)
    mean = jnp.mean(x, axis=-1, keepdims=True)
    centered = x - mean
    variance = jnp.mean(centered * centered, axis=-1, keepdims=True)
    normed = centered * lax.rsqrt(variance + EPS) * gain_ref[...] + bias_ref[...]
    normed_ref[...] = normed.astype(BF16)
    place = iota((cols, width), 0)
    col_valid = jnp.zeros((cols, width), F32)
    for k in range(cols):
        col_valid = jnp.where(place == k, mask_ref[place_ref[1] + k].astype(F32), col_valid)
    parts = []
    for i in [3 * ii + iq for iq in range(3) for ii in range(4)]:
        row_valid = mask_ref[place_ref[0] + i].astype(F32)
        parts.append(normed[i * cols : (i + 1) * cols] * (col_valid * row_valid))
        parts.append(jnp.zeros((WIDE - cols, width), F32))
    masked_ref[...] = jnp.concatenate(parts, axis=0).astype(BF16)


def edges_kernel(
    masked_ref,
    lg_ref,
    lv_ref,
    rg_ref,
    rv_ref,
    out_gain_ref,
    out_bias_ref,
    sent_ref,
    columns_ref,
    rows_ref,
):
    width = lg_ref.shape[0]
    columns_ref[0] = jnp.transpose(jnp.broadcast_to(out_gain_ref[...], (width, width)))
    columns_ref[1] = jnp.transpose(jnp.broadcast_to(out_bias_ref[...], (width, width)))
    masked = masked_ref[...]
    left = sigmoid(contract(lg_ref[...], masked, 0, 1)) * contract(lv_ref[...], masked, 0, 1)
    right = sigmoid(contract(rg_ref[...], masked, 0, 1)) * contract(rv_ref[...], masked, 0, 1)
    for iq in range(3):
        rows_ref[pl.ds(iq, width, stride=8), :] = right[:, iq * 128 : (iq + 1) * 128]
        rows_ref[pl.ds(3 + iq, width, stride=8), :] = left[:, iq * 128 : (iq + 1) * 128]
    for iq in range(6, 8):
        rows_ref[pl.ds(iq, width, stride=8), :] = jnp.zeros((width, 128), F32)
    sent_ref[...] = rows_ref[...].reshape(width, 8, 128).astype(BF16)


def swap_blocks(blocks, lane):
    out = []
    for b in range(4):
        total = None
        for a in range(4):
            moved = blocks[a] if a == b else pltpu.roll(blocks[a], (WIDE * (a - b)) % 128, blocks[a].ndim - 1)
            total = moved if total is None else jnp.where(lane // WIDE == a, moved, total)
        out.append(total)
    return out


def arrange_kernel(got_ref, left_ref, right_ref, rows_ref, padded_ref):
    lane = iota((8, 128), 1)
    padded_ref[...] = jnp.zeros_like(padded_ref)
    for g in range(8):
        for quad in range(4):
            blocks = [got_ref[g * 16 + quad * 4 + k].astype(F32) for k in range(4)]
            for ii, block in enumerate(swap_blocks(blocks, lane)):
                rows_ref[quad, pl.ds((g * 4 + ii) * 8, 8), :] = block
                padded_ref[quad, pl.ds(g * 16 + ii * 3, 3), :] = block[0:3]
    wide = iota((32, 128), 1) % WIDE < 24
    for iq in range(3):
        found = [rows_ref[quad, pl.ds(3 + iq, 32, stride=8), :] for quad in range(4)]
        for v in range(3):
            dense = jnp.where(wide, found[v], pltpu.roll(found[3], 24 - 8 * v, 1))
            left_ref[iq * 32 : (iq + 1) * 32, v * 128 : (v + 1) * 128] = dense.astype(BF16)
    wide = iota((128, 128), 1) % WIDE < 24
    for v in range(3):
        dense = jnp.where(wide, padded_ref[v], pltpu.roll(padded_ref[3], 24 - 8 * v, 1))
        right_ref[:, v * 128 : (v + 1) * 128] = dense.astype(BF16)


def mix_kernel(place_ref, left_ref, own_ref, near_ref, far_ref, both_ref, sent_ref, rows_ref):
    lane = iota((8, 128), 1)
    left = left_ref[...]
    core = place_ref[2]
    for other in range(2):
        mine, theirs = ((own_ref, near_ref), (far_ref, both_ref))[other]
        mine, theirs = mine[...], theirs[...]
        first = jnp.where(core == 0, mine, theirs)
        second = jnp.where(core == 0, theirs, mine)
        half = place_ref[3 + other]
        for xl in range(2):
            pieces = []
            for m in range(4):
                at = (xl * 4 + m) * 16
                pieces += [first[at : at + 16], second[at : at + 16]]
            mixed = contract(left, jnp.concatenate(pieces, axis=0), 1, 1)
            high = mixed.astype(BF16).astype(F32)
            low = mixed - high
            for iq in range(3):
                rows_ref[pl.ds(iq, 32, stride=8), :] = high[iq * 32 : (iq + 1) * 32]
                rows_ref[pl.ds(3 + iq, 32, stride=8), :] = low[iq * 32 : (iq + 1) * 32]
            for iq in range(6, 8):
                rows_ref[pl.ds(iq, 32, stride=8), :] = jnp.zeros((32, 128), F32)
            for g in range(8):
                blocks = [rows_ref[pl.ds((g * 4 + ii) * 8, 8), :] for ii in range(4)]
                for m, block in enumerate(swap_blocks(blocks, lane)):
                    sent_ref[g * 16 + xl * 8 + m + half * (7 - 2 * m)] = block.astype(BF16)


def update_kernel(got_ref, normed_ref, gate_ref, columns_ref, weight_ref, out_ref, rows_ref, flat_ref):
    rows, cols, width = out_ref.shape
    rows_ref[...] = got_ref[...].astype(F32).reshape(width * 8, 128)
    gain = columns_ref[0][:, 0:1]
    bias = columns_ref[1][:, 0:1]
    for iq in range(3):
        mixed = rows_ref[pl.ds(iq, width, stride=8), :] + rows_ref[pl.ds(3 + iq, width, stride=8), :]
        mean = jnp.mean(mixed, axis=0, keepdims=True)
        centered = mixed - mean
        variance = jnp.mean(centered * centered, axis=0, keepdims=True)
        normed = (centered * lax.rsqrt(variance + EPS) * gain + bias).astype(BF16)
        output = contract(normed, weight_ref[...], 0, 0)
        for ii in range(4):
            at = (3 * ii + iq) * cols
            flat_ref[at : at + 12, :] = output[ii * WIDE : ii * WIDE + 12]
            flat_ref[at + 12 : at + 24, :] = output[ii * WIDE + 16 : ii * WIDE + 28]
    gated = sigmoid(contract(normed_ref[...], gate_ref[...], 1, 0))
    out_ref[...] = (gated * flat_ref[...]).astype(BF16).reshape(rows, cols, width)


def shards(
    pair,
    token_mask,
    norm_in_gain,
    norm_in_bias,
    left_gate,
    left_value,
    right_gate,
    right_value,
    output_gate,
    norm_out_gain,
    norm_out_bias,
    output_weight,
):
    rows, cols, width = pair.shape
    params = pltpu.CompilerParams(vmem_limit_bytes=32 * 1024 * 1024)
    row_block = lax.axis_index("ia")
    half = row_block // 8 % 2
    place = jnp.stack([row_block * rows, lax.axis_index("ja") * cols, row_block % 2, half, 1 - half]).astype(jnp.int32)
    struct = jax.ShapeDtypeStruct
    normed, masked = pl.pallas_call(
        norm_kernel,
        name="norm",
        out_shape=(struct((rows * cols, width), BF16), struct((rows * WIDE, width), BF16)),
        in_specs=[SMEM, SMEM] + [VMEM] * 3,
        out_specs=(VMEM, VMEM),
        compiler_params=params,
        cost_estimate=pl.CostEstimate(flops=0, bytes_accessed=NORM_BYTES, transcendentals=0),
    )(place, token_mask, pair, norm_in_gain.reshape(1, -1), norm_in_bias.reshape(1, -1))
    sent, columns = pl.pallas_call(
        edges_kernel,
        name="edges",
        out_shape=(
            struct((128, 8, 128), BF16),
            struct((2, width, width), F32),
        ),
        in_specs=[VMEM] * 7,
        out_specs=(VMEM, VMEM),
        scratch_shapes=[pltpu.VMEM((1024, 128), F32)],
        compiler_params=params,
    )(
        masked,
        left_gate,
        left_value,
        right_gate,
        right_value,
        norm_out_gain.reshape(1, -1),
        norm_out_bias.reshape(1, -1),
    )
    got = lax.all_to_all(sent, BOTH, 0, 0, axis_index_groups=SHARING)
    left, right = pl.pallas_call(
        arrange_kernel,
        name="arrange",
        out_shape=(struct((96, 384), BF16), struct((128, 384), BF16)),
        in_specs=[VMEM],
        out_specs=(VMEM, VMEM),
        scratch_shapes=[pltpu.VMEM((4, 256, 128), F32), pltpu.VMEM((4, 128, 128), F32)],
        compiler_params=params,
    )(got)
    near = lax.ppermute(right, BOTH, CORE_FLIP)
    far = lax.ppermute(right, BOTH, HALF_FLIP)
    both = lax.ppermute(far, BOTH, CORE_FLIP)
    sent = pl.pallas_call(
        mix_kernel,
        name="mix",
        out_shape=struct((128, 8, 128), BF16),
        in_specs=[SMEM] + [VMEM] * 5,
        out_specs=VMEM,
        scratch_shapes=[pltpu.VMEM((256, 128), F32)],
        compiler_params=params,
    )(place, left, right, near, far, both)
    got = lax.all_to_all(sent, BOTH, 0, 0, axis_index_groups=SHARING)
    return pl.pallas_call(
        update_kernel,
        name="update",
        out_shape=struct((rows, cols, width), BF16),
        in_specs=[VMEM] * 5,
        out_specs=VMEM,
        scratch_shapes=[pltpu.VMEM((1024, 128), F32), pltpu.VMEM((rows * cols, 128), F32)],
        compiler_params=params,
    )(got, normed, output_gate, columns, output_weight)


def solution(mesh):
    placed = (P("ia", "ja", None),) + (P(),) * 11
    return jax.shard_map(shards, mesh=mesh, in_specs=placed, out_specs=P("ia", "ja", None), check_vma=False)
```

time: 75.4 us -> 71.1 us (0.943)
  blocking collectives: 67.8 us -> 51.5 us
  starting transfers between devices: 0 us -> 12.8 us
  local copies, waits for them, and re-layouts: 3.87 us -> 1.63 us
  waiting for transfers between devices: 0 us -> 0.92 us
    all_to_all x1 -> x0, blocking collectives: 17.9 us -> none  [shards(): rights = lax.all_to_all(right, BOTH, 0, 0, axis_index_groups=SAME)]
    ppermute x0 -> x3, starting transfers between devices: none -> 12.8 us  [the longest x1 4.43 us: shards(): far = lax.ppermute(right, BOTH, HALF_FLIP)]
    unnamed x24, local copies, waits for them, and re-layouts: 3.87 us -> 1.55 us
    all_to_all x2, blocking collectives: 50 us -> 51.5 us  [shards(): got = lax.all_to_all(sent, BOTH, 0, 0, axis_index_groups=SHARING)]
    ppermute x0 -> x3, waiting for transfers between devices: none -> 0.92 us  [the longest x1 0.91 us: shards(): both = lax.ppermute(far, BOTH, CORE_FLIP)]
  transfers between devices with their start and end apart: 0 -> 3, of which waited for: 0 -> 1; matrix products, arithmetic and copies ran while one was open for 0% -> 0% of each run, Pallas kernels for 0% -> 0%
where the time goes in v4:
time: 71.1 us; the launch traced here: 70.7 us
  blocking collectives  51.5 us (72%)
  starting transfers between devices  12.8 us (18%)
  Pallas kernels  3.59 us (5%)
  local copies, waits for them, and re-layouts  1.63 us (2%)
  waiting for transfers between devices  0.92 us (1%)
    all_to_all x2, blocking collectives, shards(): got = lax.all_to_all(sent, BOTH, 0, 0, axis_index_groups=SHARING)  51.5 us
    ppermute x1, starting transfers between devices, shards(): far = lax.ppermute(right, BOTH, HALF_FLIP)  4.43 us
    ppermute x1, starting transfers between devices, shards(): near = lax.ppermute(right, BOTH, CORE_FLIP)  4.34 us
    ppermute x1, starting transfers between devices, shards(): both = lax.ppermute(far, BOTH, CORE_FLIP)  4.04 us
    unnamed x24, local copies, waits for them, and re-layouts  1.55 us
  transfers between devices with their start and end apart: 3, of which 1 were waited for; matrix products, arithmetic and copies ran while one was open for 0% of the time, Pallas kernels for 0%

profile of v4, /device:TPU:1, one launch (start us, length us, event | category | flops | bytes accessed | tf_op | source)
XLA Modules:
  0.0 70.7 jit_solution(6091610186942918103)
XLA Ops:
  0.0 0.0 copy-start.7
  0.0 0.0 copy-start.8
  0.0 0.0 copy-start.9
  0.0 0.0 copy-start.3
  0.1 0.1 stack.23.place_ref
  0.1 0.7 %copy-done = bf16[12,24,128]{2,1,0:T(8,128)(2,1)S(1)} copy-done((bf16[12,24,128]{2,1,0:T(8,128)(2,1)S(1)}, bf16[12,24,128]{2,1,0:T(8,128)(2,1)}, u32[]{:S(2)}) %copy-start) | copy-done | bytes 73752
  0.9 0.0 copy-done.7
  0.9 0.0 copy-done.8
  0.9 0.0 copy-done.9
  0.9 0.0 copy-start.2
  0.9 0.8 %norm.1 = (bf16[288,128]{1,0:T(8,128)(2,1)S(1)}, bf16[384,128]{1,0:T(8,128)(2,1)S(1)}) custom-call(s32[5]{0:T(128)S(1)} %stack.23.place_ref, s32[384]{0:T(512)S(1)} %copy-done.7, bf16[12,24,128]{2,1,0:T(8,128)(2,1)S(1)} %copy-done, f32[1,128]{1,0:T(1,128)S(1)} %bitcast.9, f32[1,128]{1,0:T(1,128)S(1)} %bitcast.10), custom_call_target="tpu_custom_call" | custom-call | bytes 33554432 | tf_op jit(solution)/shard_map/norm/pallas_call | solution.py:195
  1.7 0.0 copy-done.10
  1.7 0.0 copy-done.11
  1.7 0.0 copy-done.3
  1.7 0.0 copy-done.1
  1.7 0.0 copy-start.4
  1.7 0.7 %copy-done.4 = bf16[128,128]{1,0:T(8,128)(2,1)S(1)} copy-done((bf16[128,128]{1,0:T(8,128)(2,1)S(1)}, bf16[128,128]{1,0:T(8,128)(2,1)}, u32[]{:S(2)}) %copy-start.4) | copy-done | bytes 32792
  2.5 0.4 edges.1
  2.9 31.4 %all_to_all.10.got_ref = bf16[128,8,128]{2,1,0:T(8,128)(2,1)S(1)} all-to-all(bf16[128,8,128]{2,1,0:T(8,128)(2,1)S(1)} %get-tuple-element.12), channel_id=1, replica_groups={{0,1,2,3,4,5,6,7,8,9,10,11,12,13,14,15,32,33,34,35,36,37,38,39,40,41,42..., dimensions={0} | all-to-all | bytes 524288 | tf_op jit(solution)/shard_map/all_to_all | solution.py:224
  34.3 0.4 arrange.1
  34.7 4.4 %collective-permute-start.1 = (bf16[128,384]{1,0:T(8,128)(2,1)S(1)}, bf16[128,384]{1,0:T(8,128)(2,1)S(1)}, u32[]{:S(2)}, u32[]{:S(2)}) collective-permute-start(bf16[128,384]{1,0:T(8,128)(2,1)S(1)} %get-tuple-element.14.own_ref), channel_id=1, source_target_pairs={{0,224},{1,225},{2,226},{3,227},{4,228},{5,229},{6,230},{7,231},{8... | collective-permute-start | bytes 294920 | tf_op jit(solution)/shard_map/ppermute | solution.py:235
  39.2 4.3 %collective-permute-start = (bf16[128,384]{1,0:T(8,128)(2,1)S(1)}, bf16[128,384]{1,0:T(8,128)(2,1)S(1)}, u32[]{:S(2)}, u32[]{:S(2)}) collective-permute-start(bf16[128,384]{1,0:T(8,128)(2,1)S(1)} %get-tuple-element.14.own_ref), channel_id=1, source_target_pairs={{0,16},{1,17},{2,18},{3,19},{4,20},{5,21},{6,22},{7,23},{8,24},{9,... | collective-permute-start | bytes 294920 | tf_op jit(solution)/shard_map/ppermute | solution.py:234
  43.5 0.0 collective-permute-done.1.far_ref
  43.5 4.0 %collective-permute-start.2 = (bf16[128,384]{1,0:T(8,128)(2,1)S(1)}, bf16[128,384]{1,0:T(8,128)(2,1)S(1)}, u32[]{:S(2)}, u32[]{:S(2)}) collective-permute-start(bf16[128,384]{1,0:T(8,128)(2,1)S(1)} %collective-permute-done.1.far_ref), channel_id=1, source_target_pairs={{0,16},{1,17},{2,18},{3,19},{4,20},{5,21},{6,22},{7,23},{8,24},{9,... | collective-permute-start | bytes 294920 | tf_op jit(solution)/shard_map/ppermute | solution.py:236
  47.6 0.0 collective-permute-done.near_ref
  47.6 0.9 %collective-permute-done.2.both_ref = bf16[128,384]{1,0:T(8,128)(2,1)S(1)} collective-permute-done((bf16[128,384]{1,0:T(8,128)(2,1)S(1)}, bf16[128,384]{1,0:T(8,128)(2,1)S(1)}, u32[]{:S(2)}, u32[]{:S(2)}) %collective-permute-start.2) | collective-permute-done | bytes 98336 | tf_op jit(solution)/shard_map/ppermute | solution.py:236
  48.5 1.0 %mix.1 = bf16[128,8,128]{2,1,0:T(8,128)(2,1)S(1)} custom-call(s32[5]{0:T(128)S(1)} %stack.23.place_ref, bf16[96,384]{1,0:T(8,128)(2,1)S(1)} %get-tuple-element.13.left_ref, bf16[128,384]{1,0:T(8,128)(2,1)S(1)} %get-tuple-element.14.own_ref, bf16[128,384]{1,0:T(8,128)(2,1)S(1)} %collective-permute-done.near_ref, ...), custom_call_target="tpu_custom_call" | custom-call | tf_op jit(solution)/shard_map/mix/pallas_call | solution.py:237
  49.5 0.0 copy-start.5
  49.5 0.0 copy-start.6
  49.6 20.1 %all_to_all.11.got_ref = bf16[128,8,128]{2,1,0:T(8,128)(2,1)S(1)} all-to-all(bf16[128,8,128]{2,1,0:T(8,128)(2,1)S(1)} %mix.1), channel_id=1, replica_groups={{0,1,2,3,4,5,6,7,8,9,10,11,12,13,14,15,32,33,34,35,36,37,38,39,40,41,42..., dimensions={0} | all-to-all | bytes 524288 | tf_op jit(solution)/shard_map/all_to_all | solution.py:246
  69.6 0.0 copy-done.5
  69.6 1.0 %update.1 = bf16[12,24,128]{2,1,0:T(8,128)(2,1)} custom-call(bf16[128,8,128]{2,1,0:T(8,128)(2,1)S(1)} %all_to_all.11.got_ref, bf16[288,128]{1,0:T(8,128)(2,1)S(1)} %get-tuple-element.15.normed_ref, bf16[128,128]{1,0:T(8,128)(2,1)S(1)} %copy-done.5, f32[2,128,128]{2,1,0:T(8,128)S(1)} %get-tuple-element.16.columns_ref, bf16[128,128]{1,0:T(8,128)(2,1)S(1)} %copy-done.6), custom_call_target="tpu_custom_call" | custom-call | tf_op jit(solution)/shard_map/update/pallas_call | solution.py:247
  (6 shorter events, 0.0 us)
Async XLA Ops:
  0.0 0.9 %copy-start = (bf16[12,24,128]{2,1,0:T(8,128)(2,1)S(1)}, bf16[12,24,128]{2,1,0:T(8,128)(2,1)}, u32[]{:S(2)}) copy-start(bf16[12,24,128]{2,1,0:T(8,128)(2,1)} %pair_ref.1) | copy-start | bytes 221188
  0.0 1.7 %copy-start.10 = (f32[128]{0:T(128)S(1)}, f32[128]{0:T(128)}, u32[]{:S(2)}) copy-start(f32[128]{0:T(128)} %param.21) | copy-start | bytes 1540
  0.0 1.7 %copy-start.11 = (f32[128]{0:T(128)S(1)}, f32[128]{0:T(128)}, u32[]{:S(2)}) copy-start(f32[128]{0:T(128)} %param.22) | copy-start | bytes 1540
  0.0 0.9 %copy-start.7 = (s32[384]{0:T(512)S(1)}, s32[384]{0:T(512)}, u32[]{:S(2)}) copy-start(s32[384]{0:T(512)} %mask_ref.1) | copy-start | bytes 4612
  0.0 0.9 %copy-start.8 = (f32[128]{0:T(128)S(1)}, f32[128]{0:T(128)}, u32[]{:S(2)}) copy-start(f32[128]{0:T(128)} %param.14) | copy-start | bytes 1540
  0.0 0.9 %copy-start.9 = (f32[128]{0:T(128)S(1)}, f32[128]{0:T(128)}, u32[]{:S(2)}) copy-start(f32[128]{0:T(128)} %param.15) | copy-start | bytes 1540
  0.0 1.7 %copy-start.3 = (bf16[128,128]{1,0:T(8,128)(2,1)S(1)}, bf16[128,128]{1,0:T(8,128)(2,1)}, u32[]{:S(2)}) copy-start(bf16[128,128]{1,0:T(8,128)(2,1)} %rg_ref.1) | copy-start | bytes 98308
  0.9 0.8 %copy-start.1 = (bf16[128,128]{1,0:T(8,128)(2,1)S(1)}, bf16[128,128]{1,0:T(8,128)(2,1)}, u32[]{:S(2)}) copy-start(bf16[128,128]{1,0:T(8,128)(2,1)} %lg_ref.1) | copy-start | bytes 98308
  0.9 0.8 %copy-start.2 = (bf16[128,128]{1,0:T(8,128)(2,1)S(1)}, bf16[128,128]{1,0:T(8,128)(2,1)}, u32[]{:S(2)}) copy-start(bf16[128,128]{1,0:T(8,128)(2,1)} %lv_ref.1) | copy-start | bytes 98308
  1.7 0.8 %copy-start.4 = (bf16[128,128]{1,0:T(8,128)(2,1)S(1)}, bf16[128,128]{1,0:T(8,128)(2,1)}, u32[]{:S(2)}) copy-start(bf16[128,128]{1,0:T(8,128)(2,1)} %rv_ref.1) | copy-start | bytes 98308
  34.7 8.8 %collective-permute-start.1 = (bf16[128,384]{1,0:T(8,128)(2,1)S(1)}, bf16[128,384]{1,0:T(8,128)(2,1)S(1)}, u32[]{:S(2)}, u32[]{:S(2)}) collective-permute-start(bf16[128,384]{1,0:T(8,128)(2,1)S(1)} %get-tuple-element.14.own_ref), channel_id=1, source_target_pairs={{0,224},{1,225},{2,226},{3,227},{4,228},{5,229},{6,230},{7,231},{8... | collective-permute-start | bytes 294920 | tf_op jit(solution)/shard_map/ppermute | solution.py:235
  39.2 8.4 %collective-permute-start = (bf16[128,384]{1,0:T(8,128)(2,1)S(1)}, bf16[128,384]{1,0:T(8,128)(2,1)S(1)}, u32[]{:S(2)}, u32[]{:S(2)}) collective-permute-start(bf16[128,384]{1,0:T(8,128)(2,1)S(1)} %get-tuple-element.14.own_ref), channel_id=1, source_target_pairs={{0,16},{1,17},{2,18},{3,19},{4,20},{5,21},{6,22},{7,23},{8,24},{9,... | collective-permute-start | bytes 294920 | tf_op jit(solution)/shard_map/ppermute | solution.py:234
  43.5 5.0 %collective-permute-start.2 = (bf16[128,384]{1,0:T(8,128)(2,1)S(1)}, bf16[128,384]{1,0:T(8,128)(2,1)S(1)}, u32[]{:S(2)}, u32[]{:S(2)}) collective-permute-start(bf16[128,384]{1,0:T(8,128)(2,1)S(1)} %collective-permute-done.1.far_ref), channel_id=1, source_target_pairs={{0,16},{1,17},{2,18},{3,19},{4,20},{5,21},{6,22},{7,23},{8,24},{9,... | collective-permute-start | bytes 294920 | tf_op jit(solution)/shard_map/ppermute | solution.py:236
  49.5 20.1 %copy-start.5 = (bf16[128,128]{1,0:T(8,128)(2,1)S(1)}, bf16[128,128]{1,0:T(8,128)(2,1)}, u32[]{:S(2)}) copy-start(bf16[128,128]{1,0:T(8,128)(2,1)} %gate_ref.1) | copy-start | bytes 98308
  49.5 20.1 %copy-start.6 = (bf16[128,128]{1,0:T(8,128)(2,1)S(1)}, bf16[128,128]{1,0:T(8,128)(2,1)}, u32[]{:S(2)}) copy-start(bf16[128,128]{1,0:T(8,128)(2,1)} %weight_ref.1) | copy-start | bytes 98308

commit v5 on v4

--- a/solution.py
+++ b/solution.py
@@ -83,12 +83,11 @@
     masked = masked_ref[...]
     left = sigmoid(contract(lg_ref[...], masked, 0, 1)) * contract(lv_ref[...], masked, 0, 1)
     right = sigmoid(contract(rg_ref[...], masked, 0, 1)) * contract(rv_ref[...], masked, 0, 1)
-    for iq in range(3):
-        rows_ref[pl.ds(iq, width, stride=8), :] = right[:, iq * 128 : (iq + 1) * 128]
-        rows_ref[pl.ds(3 + iq, width, stride=8), :] = left[:, iq * 128 : (iq + 1) * 128]
-    for iq in range(6, 8):
-        rows_ref[pl.ds(iq, width, stride=8), :] = jnp.zeros((width, 128), F32)
-    sent_ref[...] = rows_ref[...].reshape(width, 8, 128).astype(BF16)
+    for t in range(3):
+        lanes = slice(t * 128, (t + 1) * 128)
+        rows_ref[t, pl.ds(0, width, stride=2), :] = right[:, lanes]
+        rows_ref[t, pl.ds(1, width, stride=2), :] = left[:, lanes]
+        sent_ref[:, :, lanes] = rows_ref[t].astype(BF16).reshape(width, 2, 128)
 
 
 def swap_blocks(blocks, lane):
@@ -102,25 +101,31 @@
     return out
 
 
-def arrange_kernel(got_ref, left_ref, right_ref, rows_ref, padded_ref):
-    lane = iota((8, 128), 1)
+def arrange_kernel(got_ref, left_ref, right_ref, rows_ref, quads_ref, padded_ref):
+    for t in range(3):
+        rows_ref[t] = got_ref[:, :, t * 128 : (t + 1) * 128].astype(F32).reshape(256, 128)
+    lane = iota((32, 128), 1)
     padded_ref[...] = jnp.zeros_like(padded_ref)
-    for g in range(8):
-        for quad in range(4):
-            blocks = [got_ref[g * 16 + quad * 4 + k].astype(F32) for k in range(4)]
+    wide = iota((8, 128), 1) % WIDE < 24
+    for side in range(2):
+        for iq in range(3):
+            blocks = [rows_ref[iq, pl.ds(2 * k + side, 32, stride=8), :] for k in range(4)]
+            done = []
             for ii, block in enumerate(swap_blocks(blocks, lane)):
-                rows_ref[quad, pl.ds((g * 4 + ii) * 8, 8), :] = block
-                padded_ref[quad, pl.ds(g * 16 + ii * 3, 3), :] = block[0:3]
-    wide = iota((32, 128), 1) % WIDE < 24
-    for iq in range(3):
-        found = [rows_ref[quad, pl.ds(3 + iq, 32, stride=8), :] for quad in range(4)]
-        for v in range(3):
-            dense = jnp.where(wide, found[v], pltpu.roll(found[3], 24 - 8 * v, 1))
-            left_ref[iq * 32 : (iq + 1) * 32, v * 128 : (v + 1) * 128] = dense.astype(BF16)
-    wide = iota((128, 128), 1) % WIDE < 24
+                at = (side * 12 + iq * 4 + ii) * 32
+                quads_ref[pl.ds(at, 32), :] = block
+                found = [quads_ref[pl.ds(at + quad, 8, stride=4), :] for quad in range(4)]
+                dense = [jnp.where(wide, found[v], pltpu.roll(found[3], 24 - 8 * v, 1)) for v in range(3)]
+                done.append(dense)
+                if side == 0:
+                    for v in range(3):
+                        padded_ref[v, pl.ds(ii * 3 + iq, 8, stride=16), :] = dense[v]
+            if side == 1:
+                for v in range(3):
+                    block = jnp.concatenate([dense[v] for dense in done], axis=0)
+                    left_ref[iq * 32 : (iq + 1) * 32, v * 128 : (v + 1) * 128] = block.astype(BF16)
     for v in range(3):
-        dense = jnp.where(wide, padded_ref[v], pltpu.roll(padded_ref[3], 24 - 8 * v, 1))
-        right_ref[:, v * 128 : (v + 1) * 128] = dense.astype(BF16)
+        right_ref[:, v * 128 : (v + 1) * 128] = padded_ref[v].astype(BF16)
 
 
 def mix_kernel(place_ref, left_ref, own_ref, near_ref, far_ref, both_ref, sent_ref, rows_ref):
@@ -140,25 +145,23 @@
                 pieces += [first[at : at + 16], second[at : at + 16]]
             mixed = contract(left, jnp.concatenate(pieces, axis=0), 1, 1)
             high = mixed.astype(BF16).astype(F32)
-            low = mixed - high
-            for iq in range(3):
-                rows_ref[pl.ds(iq, 32, stride=8), :] = high[iq * 32 : (iq + 1) * 32]
-                rows_ref[pl.ds(3 + iq, 32, stride=8), :] = low[iq * 32 : (iq + 1) * 32]
-            for iq in range(6, 8):
-                rows_ref[pl.ds(iq, 32, stride=8), :] = jnp.zeros((32, 128), F32)
-            for g in range(8):
-                blocks = [rows_ref[pl.ds((g * 4 + ii) * 8, 8), :] for ii in range(4)]
-                for m, block in enumerate(swap_blocks(blocks, lane)):
-                    sent_ref[g * 16 + xl * 8 + m + half * (7 - 2 * m)] = block.astype(BF16)
+            for part, values in enumerate((high, mixed - high)):
+                for iq in range(3):
+                    blocks = [values[(iq * 4 + ii) * 8 : (iq * 4 + ii + 1) * 8] for ii in range(4)]
+                    for m, block in enumerate(swap_blocks(blocks, lane)):
+                        to = (xl * 8 + m + half * (7 - 2 * m)) * 2 + part
+                        rows_ref[iq, pl.ds(to, 8, stride=32), :] = block
+    for t in range(3):
+        sent_ref[:, :, t * 128 : (t + 1) * 128] = rows_ref[t].astype(BF16).reshape(128, 2, 128)
 
 
 def update_kernel(got_ref, normed_ref, gate_ref, columns_ref, weight_ref, out_ref, rows_ref, flat_ref):
     rows, cols, width = out_ref.shape
-    rows_ref[...] = got_ref[...].astype(F32).reshape(width * 8, 128)
     gain = columns_ref[0][:, 0:1]
     bias = columns_ref[1][:, 0:1]
     for iq in range(3):
-        mixed = rows_ref[pl.ds(iq, width, stride=8), :] + rows_ref[pl.ds(3 + iq, width, stride=8), :]
+        rows_ref[iq] = got_ref[:, :, iq * 128 : (iq + 1) * 128].astype(F32).reshape(2 * width, 128)
+        mixed = rows_ref[iq, pl.ds(0, width, stride=2), :] + rows_ref[iq, pl.ds(1, width, stride=2), :]
         mean = jnp.mean(mixed, axis=0, keepdims=True)
         centered = mixed - mean
         variance = jnp.mean(centered * centered, axis=0, keepdims=True)
@@ -205,12 +208,12 @@
         edges_kernel,
         name="edges",
         out_shape=(
-            struct((128, 8, 128), BF16),
+            struct((128, 2, rows * WIDE), BF16),
             struct((2, width, width), F32),
         ),
         in_specs=[VMEM] * 7,
         out_specs=(VMEM, VMEM),
-        scratch_shapes=[pltpu.VMEM((1024, 128), F32)],
+        scratch_shapes=[pltpu.VMEM((3, 256, 128), F32)],
         compiler_params=params,
     )(
         masked,
@@ -228,7 +231,7 @@
         out_shape=(struct((96, 384), BF16), struct((128, 384), BF16)),
         in_specs=[VMEM],
         out_specs=(VMEM, VMEM),
-        scratch_shapes=[pltpu.VMEM((4, 256, 128), F32), pltpu.VMEM((4, 128, 128), F32)],
+        scratch_shapes=[pltpu.VMEM((3, 256, 128), F32), pltpu.VMEM((768, 128), F32), pltpu.VMEM((3, 128, 128), F32)],
         compiler_params=params,
     )(got)
     near = lax.ppermute(right, BOTH, CORE_FLIP)
@@ -237,10 +240,10 @@
     sent = pl.pallas_call(
         mix_kernel,
         name="mix",
-        out_shape=struct((128, 8, 128), BF16),
+        out_shape=struct((128, 2, rows * WIDE), BF16),
         in_specs=[SMEM] + [VMEM] * 5,
         out_specs=VMEM,
-        scratch_shapes=[pltpu.VMEM((256, 128), F32)],
+        scratch_shapes=[pltpu.VMEM((3, 256, 128), F32)],
         compiler_params=params,
     )(place, left, right, near, far, both)
     got = lax.all_to_all(sent, BOTH, 0, 0, axis_index_groups=SHARING)
@@ -250,7 +253,7 @@
         out_shape=struct((rows, cols, width), BF16),
         in_specs=[VMEM] * 5,
         out_specs=VMEM,
-        scratch_shapes=[pltpu.VMEM((1024, 128), F32), pltpu.VMEM((rows * cols, 128), F32)],
+        scratch_shapes=[pltpu.VMEM((3, 256, 128), F32), pltpu.VMEM((rows * cols, 128), F32)],
         compiler_params=params,
     )(got, normed, output_gate, columns, output_weight)
 

time: 71.1 us -> 69.4 us (0.976)
  blocking collectives: 51.5 us -> 49.2 us
  Pallas kernels: 3.59 us -> 4.36 us
    all_to_all x2, blocking collectives: 51.5 us -> 49.2 us  [shards(): got = lax.all_to_all(sent, BOTH, 0, 0, axis_index_groups=SHARING)]
where the time goes in v5:
time: 69.4 us; the launch traced here: 69 us
  blocking collectives  49.2 us (71%)
  starting transfers between devices  12.8 us (18%)
  Pallas kernels  4.36 us (6%)
  local copies, waits for them, and re-layouts  1.63 us (2%)
  waiting for transfers between devices  0.92 us (1%)
    all_to_all x2, blocking collectives, shards(): got = lax.all_to_all(sent, BOTH, 0, 0, axis_index_groups=SHARING)  49.2 us
    ppermute x1, starting transfers between devices, shards(): far = lax.ppermute(right, BOTH, HALF_FLIP)  4.41 us
    ppermute x1, starting transfers between devices, shards(): near = lax.ppermute(right, BOTH, CORE_FLIP)  4.32 us
    ppermute x1, starting transfers between devices, shards(): both = lax.ppermute(far, BOTH, CORE_FLIP)  4.04 us
    unnamed x24, local copies, waits for them, and re-layouts  1.55 us
  transfers between devices with their start and end apart: 3, of which 1 were waited for; matrix products, arithmetic and copies ran while one was open for 0% of the time, Pallas kernels for 0%

profile of v5, /device:TPU:1, one launch (start us, length us, event | category | flops | bytes accessed | tf_op | source)
XLA Modules:
  0.0 69.0 jit_solution(2583422413396190156)
XLA Ops:
  0.0 0.0 copy-start.7
  0.0 0.0 copy-start.8
  0.0 0.0 copy-start.9
  0.0 0.0 copy-start.3
  0.1 0.1 stack.23.place_ref
  0.1 0.7 %copy-done = bf16[12,24,128]{2,1,0:T(8,128)(2,1)S(1)} copy-done((bf16[12,24,128]{2,1,0:T(8,128)(2,1)S(1)}, bf16[12,24,128]{2,1,0:T(8,128)(2,1)}, u32[]{:S(2)}) %copy-start) | copy-done | bytes 73752
  0.9 0.0 copy-done.7
  0.9 0.0 copy-done.8
  0.9 0.0 copy-done.9
  0.9 0.0 copy-start.2
  0.9 0.8 %norm.1 = (bf16[288,128]{1,0:T(8,128)(2,1)S(1)}, bf16[384,128]{1,0:T(8,128)(2,1)S(1)}) custom-call(s32[5]{0:T(128)S(1)} %stack.23.place_ref, s32[384]{0:T(512)S(1)} %copy-done.7, bf16[12,24,128]{2,1,0:T(8,128)(2,1)S(1)} %copy-done, f32[1,128]{1,0:T(1,128)S(1)} %bitcast.9, f32[1,128]{1,0:T(1,128)S(1)} %bitcast.10), custom_call_target="tpu_custom_call" | custom-call | bytes 33554432 | tf_op jit(solution)/shard_map/norm/pallas_call | solution.py:198
  1.7 0.0 copy-done.10
  1.7 0.0 copy-done.11
  1.7 0.0 copy-done.3
  1.7 0.0 copy-done.1
  1.7 0.0 copy-start.4
  1.7 0.7 %copy-done.4 = bf16[128,128]{1,0:T(8,128)(2,1)S(1)} copy-done((bf16[128,128]{1,0:T(8,128)(2,1)S(1)}, bf16[128,128]{1,0:T(8,128)(2,1)}, u32[]{:S(2)}) %copy-start.4) | copy-done | bytes 32792
  2.5 0.4 edges.1
  2.9 30.4 %all_to_all.10.got_ref = bf16[128,2,384]{2,1,0:T(2,128)(2,1)S(1)} all-to-all(bf16[128,2,384]{2,1,0:T(2,128)(2,1)S(1)} %get-tuple-element.12), channel_id=1, replica_groups={{0,1,2,3,4,5,6,7,8,9,10,11,12,13,14,15,32,33,34,35,36,37,38,39,40,41,42..., dimensions={0} | all-to-all | bytes 393216 | tf_op jit(solution)/shard_map/all_to_all | solution.py:227
  33.4 0.8 %arrange.1 = (bf16[96,384]{1,0:T(8,128)(2,1)S(1)}, bf16[128,384]{1,0:T(8,128)(2,1)S(1)}) custom-call(bf16[128,2,384]{2,1,0:T(2,128)(2,1)S(1)} %all_to_all.10.got_ref), custom_call_target="tpu_custom_call" | custom-call | tf_op jit(solution)/shard_map/arrange/pallas_call | solution.py:228
  34.2 4.4 %collective-permute-start.1 = (bf16[128,384]{1,0:T(8,128)(2,1)S(1)}, bf16[128,384]{1,0:T(8,128)(2,1)S(1)}, u32[]{:S(2)}, u32[]{:S(2)}) collective-permute-start(bf16[128,384]{1,0:T(8,128)(2,1)S(1)} %get-tuple-element.14.own_ref), channel_id=1, source_target_pairs={{0,224},{1,225},{2,226},{3,227},{4,228},{5,229},{6,230},{7,231},{8... | collective-permute-start | bytes 294920 | tf_op jit(solution)/shard_map/ppermute | solution.py:238
  38.6 4.3 %collective-permute-start = (bf16[128,384]{1,0:T(8,128)(2,1)S(1)}, bf16[128,384]{1,0:T(8,128)(2,1)S(1)}, u32[]{:S(2)}, u32[]{:S(2)}) collective-permute-start(bf16[128,384]{1,0:T(8,128)(2,1)S(1)} %get-tuple-element.14.own_ref), channel_id=1, source_target_pairs={{0,16},{1,17},{2,18},{3,19},{4,20},{5,21},{6,22},{7,23},{8,24},{9,... | collective-permute-start | bytes 294920 | tf_op jit(solution)/shard_map/ppermute | solution.py:237
  42.9 0.0 collective-permute-done.1.far_ref
  43.0 4.0 %collective-permute-start.2 = (bf16[128,384]{1,0:T(8,128)(2,1)S(1)}, bf16[128,384]{1,0:T(8,128)(2,1)S(1)}, u32[]{:S(2)}, u32[]{:S(2)}) collective-permute-start(bf16[128,384]{1,0:T(8,128)(2,1)S(1)} %collective-permute-done.1.far_ref), channel_id=1, source_target_pairs={{0,16},{1,17},{2,18},{3,19},{4,20},{5,21},{6,22},{7,23},{8,24},{9,... | collective-permute-start | bytes 294920 | tf_op jit(solution)/shard_map/ppermute | solution.py:239
  47.0 0.0 collective-permute-done.near_ref
  47.0 0.9 %collective-permute-done.2.both_ref = bf16[128,384]{1,0:T(8,128)(2,1)S(1)} collective-permute-done((bf16[128,384]{1,0:T(8,128)(2,1)S(1)}, bf16[128,384]{1,0:T(8,128)(2,1)S(1)}, u32[]{:S(2)}, u32[]{:S(2)}) %collective-permute-start.2) | collective-permute-done | bytes 98336 | tf_op jit(solution)/shard_map/ppermute | solution.py:239
  47.9 1.2 %mix.1 = bf16[128,2,384]{2,1,0:T(2,128)(2,1)S(1)} custom-call(s32[5]{0:T(128)S(1)} %stack.23.place_ref, bf16[96,384]{1,0:T(8,128)(2,1)S(1)} %get-tuple-element.13.left_ref, bf16[128,384]{1,0:T(8,128)(2,1)S(1)} %get-tuple-element.14.own_ref, bf16[128,384]{1,0:T(8,128)(2,1)S(1)} %collective-permute-done.near_ref, ...), custom_call_target="tpu_custom_call" | custom-call | tf_op jit(solution)/shard_map/mix/pallas_call | solution.py:240
  49.1 0.0 copy-start.5
  49.2 0.0 copy-start.6
  49.2 18.7 %all_to_all.11.got_ref = bf16[128,2,384]{2,1,0:T(2,128)(2,1)S(1)} all-to-all(bf16[128,2,384]{2,1,0:T(2,128)(2,1)S(1)} %mix.1), channel_id=1, replica_groups={{0,1,2,3,4,5,6,7,8,9,10,11,12,13,14,15,32,33,34,35,36,37,38,39,40,41,42..., dimensions={0} | all-to-all | bytes 393216 | tf_op jit(solution)/shard_map/all_to_all | solution.py:249
  67.9 0.0 copy-done.5
  67.9 1.1 %update.1 = bf16[12,24,128]{2,1,0:T(8,128)(2,1)} custom-call(bf16[128,2,384]{2,1,0:T(2,128)(2,1)S(1)} %all_to_all.11.got_ref, bf16[288,128]{1,0:T(8,128)(2,1)S(1)} %get-tuple-element.15.normed_ref, bf16[128,128]{1,0:T(8,128)(2,1)S(1)} %copy-done.5, f32[2,128,128]{2,1,0:T(8,128)S(1)} %get-tuple-element.16.columns_ref, bf16[128,128]{1,0:T(8,128)(2,1)S(1)} %copy-done.6), custom_call_target="tpu_custom_call" | custom-call | tf_op jit(solution)/shard_map/update/pallas_call | solution.py:250
  (6 shorter events, 0.0 us)
Async XLA Ops:
  0.0 0.9 %copy-start = (bf16[12,24,128]{2,1,0:T(8,128)(2,1)S(1)}, bf16[12,24,128]{2,1,0:T(8,128)(2,1)}, u32[]{:S(2)}) copy-start(bf16[12,24,128]{2,1,0:T(8,128)(2,1)} %pair_ref.1) | copy-start | bytes 221188
  0.0 1.7 %copy-start.10 = (f32[128]{0:T(128)S(1)}, f32[128]{0:T(128)}, u32[]{:S(2)}) copy-start(f32[128]{0:T(128)} %param.21) | copy-start | bytes 1540
  0.0 1.7 %copy-start.11 = (f32[128]{0:T(128)S(1)}, f32[128]{0:T(128)}, u32[]{:S(2)}) copy-start(f32[128]{0:T(128)} %param.22) | copy-start | bytes 1540
  0.0 0.9 %copy-start.7 = (s32[384]{0:T(512)S(1)}, s32[384]{0:T(512)}, u32[]{:S(2)}) copy-start(s32[384]{0:T(512)} %mask_ref.1) | copy-start | bytes 4612
  0.0 0.9 %copy-start.8 = (f32[128]{0:T(128)S(1)}, f32[128]{0:T(128)}, u32[]{:S(2)}) copy-start(f32[128]{0:T(128)} %param.14) | copy-start | bytes 1540
  0.0 0.9 %copy-start.9 = (f32[128]{0:T(128)S(1)}, f32[128]{0:T(128)}, u32[]{:S(2)}) copy-start(f32[128]{0:T(128)} %param.15) | copy-start | bytes 1540
  0.0 1.7 %copy-start.3 = (bf16[128,128]{1,0:T(8,128)(2,1)S(1)}, bf16[128,128]{1,0:T(8,128)(2,1)}, u32[]{:S(2)}) copy-start(bf16[128,128]{1,0:T(8,128)(2,1)} %rg_ref.1) | copy-start | bytes 98308
  0.9 0.8 %copy-start.1 = (bf16[128,128]{1,0:T(8,128)(2,1)S(1)}, bf16[128,128]{1,0:T(8,128)(2,1)}, u32[]{:S(2)}) copy-start(bf16[128,128]{1,0:T(8,128)(2,1)} %lg_ref.1) | copy-start | bytes 98308
  0.9 0.8 %copy-start.2 = (bf16[128,128]{1,0:T(8,128)(2,1)S(1)}, bf16[128,128]{1,0:T(8,128)(2,1)}, u32[]{:S(2)}) copy-start(bf16[128,128]{1,0:T(8,128)(2,1)} %lv_ref.1) | copy-start | bytes 98308
  1.7 0.8 %copy-start.4 = (bf16[128,128]{1,0:T(8,128)(2,1)S(1)}, bf16[128,128]{1,0:T(8,128)(2,1)}, u32[]{:S(2)}) copy-start(bf16[128,128]{1,0:T(8,128)(2,1)} %rv_ref.1) | copy-start | bytes 98308
  34.2 8.7 %collective-permute-start.1 = (bf16[128,384]{1,0:T(8,128)(2,1)S(1)}, bf16[128,384]{1,0:T(8,128)(2,1)S(1)}, u32[]{:S(2)}, u32[]{:S(2)}) collective-permute-start(bf16[128,384]{1,0:T(8,128)(2,1)S(1)} %get-tuple-element.14.own_ref), channel_id=1, source_target_pairs={{0,224},{1,225},{2,226},{3,227},{4,228},{5,229},{6,230},{7,231},{8... | collective-permute-start | bytes 294920 | tf_op jit(solution)/shard_map/ppermute | solution.py:238
  38.6 8.4 %collective-permute-start = (bf16[128,384]{1,0:T(8,128)(2,1)S(1)}, bf16[128,384]{1,0:T(8,128)(2,1)S(1)}, u32[]{:S(2)}, u32[]{:S(2)}) collective-permute-start(bf16[128,384]{1,0:T(8,128)(2,1)S(1)} %get-tuple-element.14.own_ref), channel_id=1, source_target_pairs={{0,16},{1,17},{2,18},{3,19},{4,20},{5,21},{6,22},{7,23},{8,24},{9,... | collective-permute-start | bytes 294920 | tf_op jit(solution)/shard_map/ppermute | solution.py:237
  43.0 5.0 %collective-permute-start.2 = (bf16[128,384]{1,0:T(8,128)(2,1)S(1)}, bf16[128,384]{1,0:T(8,128)(2,1)S(1)}, u32[]{:S(2)}, u32[]{:S(2)}) collective-permute-start(bf16[128,384]{1,0:T(8,128)(2,1)S(1)} %collective-permute-done.1.far_ref), channel_id=1, source_target_pairs={{0,16},{1,17},{2,18},{3,19},{4,20},{5,21},{6,22},{7,23},{8,24},{9,... | collective-permute-start | bytes 294920 | tf_op jit(solution)/shard_map/ppermute | solution.py:239
  49.1 18.7 %copy-start.5 = (bf16[128,128]{1,0:T(8,128)(2,1)S(1)}, bf16[128,128]{1,0:T(8,128)(2,1)}, u32[]{:S(2)}) copy-start(bf16[128,128]{1,0:T(8,128)(2,1)} %gate_ref.1) | copy-start | bytes 98308
  49.2 18.7 %copy-start.6 = (bf16[128,128]{1,0:T(8,128)(2,1)S(1)}, bf16[128,128]{1,0:T(8,128)(2,1)}, u32[]{:S(2)}) copy-start(bf16[128,128]{1,0:T(8,128)(2,1)} %weight_ref.1) | copy-start | bytes 98308

commit v6 on v5

--- a/solution.py
+++ b/solution.py
@@ -8,7 +8,6 @@
 BOTH = ("ia", "ja")
 EPS = 1e-5
 WIDE = 32
-NORM_BYTES = 32 * 1024 * 1024
 F32 = jnp.float32
 BF16 = jnp.bfloat16
 VMEM = pl.BlockSpec(memory_space=pltpu.VMEM)
@@ -65,18 +64,7 @@
     masked_ref[...] = jnp.concatenate(parts, axis=0).astype(BF16)
 
 
-def edges_kernel(
-    masked_ref,
-    lg_ref,
-    lv_ref,
-    rg_ref,
-    rv_ref,
-    out_gain_ref,
-    out_bias_ref,
-    sent_ref,
-    columns_ref,
-    rows_ref,
-):
+def edges_kernel(masked_ref, lg_ref, lv_ref, rg_ref, rv_ref, out_gain_ref, out_bias_ref, sent_ref, columns_ref, rows_ref):
     width = lg_ref.shape[0]
     columns_ref[0] = jnp.transpose(jnp.broadcast_to(out_gain_ref[...], (width, width)))
     columns_ref[1] = jnp.transpose(jnp.broadcast_to(out_bias_ref[...], (width, width)))
@@ -101,61 +89,86 @@
     return out
 
 
-def arrange_kernel(got_ref, left_ref, right_ref, rows_ref, quads_ref, padded_ref):
-    for t in range(3):
-        rows_ref[t] = got_ref[:, :, t * 128 : (t + 1) * 128].astype(F32).reshape(256, 128)
+def spread_side(side, got_ref, rows_ref, quads_ref):
     lane = iota((32, 128), 1)
+    wide = iota((8, 128), 1) % WIDE < 24
+    spread = {}
+    for iq in range(3):
+        rows_ref[iq] = got_ref[:, :, iq * 128 : (iq + 1) * 128].astype(F32).reshape(256, 128)
+        blocks = [rows_ref[iq, pl.ds(2 * k + side, 32, stride=8), :] for k in range(4)]
+        for ii, block in enumerate(swap_blocks(blocks, lane)):
+            at = (iq * 4 + ii) * 32
+            quads_ref[pl.ds(at, 32), :] = block
+            found = [quads_ref[pl.ds(at + quad, 8, stride=4), :] for quad in range(4)]
+            spread[iq, ii] = [jnp.where(wide, found[v], pltpu.roll(found[3], 24 - 8 * v, 1)) for v in range(3)]
+    return spread
+
+
+def right_kernel(got_ref, right_ref, rows_ref, quads_ref, padded_ref):
     padded_ref[...] = jnp.zeros_like(padded_ref)
-    wide = iota((8, 128), 1) % WIDE < 24
-    for side in range(2):
-        for iq in range(3):
-            blocks = [rows_ref[iq, pl.ds(2 * k + side, 32, stride=8), :] for k in range(4)]
-            done = []
-            for ii, block in enumerate(swap_blocks(blocks, lane)):
-                at = (side * 12 + iq * 4 + ii) * 32
-                quads_ref[pl.ds(at, 32), :] = block
-                found = [quads_ref[pl.ds(at + quad, 8, stride=4), :] for quad in range(4)]
-                dense = [jnp.where(wide, found[v], pltpu.roll(found[3], 24 - 8 * v, 1)) for v in range(3)]
-                done.append(dense)
-                if side == 0:
-                    for v in range(3):
-                        padded_ref[v, pl.ds(ii * 3 + iq, 8, stride=16), :] = dense[v]
-            if side == 1:
-                for v in range(3):
-                    block = jnp.concatenate([dense[v] for dense in done], axis=0)
-                    left_ref[iq * 32 : (iq + 1) * 32, v * 128 : (v + 1) * 128] = block.astype(BF16)
+    for (iq, ii), dense in spread_side(0, got_ref, rows_ref, quads_ref).items():
+        for v in range(3):
+            padded_ref[v, pl.ds(ii * 3 + iq, 8, stride=16), :] = dense[v]
     for v in range(3):
         right_ref[:, v * 128 : (v + 1) * 128] = padded_ref[v].astype(BF16)
 
 
-def mix_kernel(place_ref, left_ref, own_ref, near_ref, far_ref, both_ref, sent_ref, rows_ref):
+def left_kernel(got_ref, left_ref, rows_ref, quads_ref):
+    spread = spread_side(1, got_ref, rows_ref, quads_ref)
+    for iq in range(3):
+        for v in range(3):
+            block = jnp.concatenate([spread[iq, ii][v] for ii in range(4)], axis=0)
+            left_ref[iq * 32 : (iq + 1) * 32, v * 128 : (v + 1) * 128] = block.astype(BF16)
+
+
+def mix_half(place_ref, other, left_ref, mine_ref, theirs_ref, sent_ref, slots_ref):
     lane = iota((8, 128), 1)
     left = left_ref[...]
+    mine, theirs = mine_ref[...], theirs_ref[...]
     core = place_ref[2]
-    for other in range(2):
-        mine, theirs = ((own_ref, near_ref), (far_ref, both_ref))[other]
-        mine, theirs = mine[...], theirs[...]
-        first = jnp.where(core == 0, mine, theirs)
-        second = jnp.where(core == 0, theirs, mine)
-        half = place_ref[3 + other]
-        for xl in range(2):
-            pieces = []
-            for m in range(4):
-                at = (xl * 4 + m) * 16
-                pieces += [first[at : at + 16], second[at : at + 16]]
-            mixed = contract(left, jnp.concatenate(pieces, axis=0), 1, 1)
-            high = mixed.astype(BF16).astype(F32)
+    half = place_ref[3 + other]
+    first = jnp.where(core == 0, mine, theirs)
+    second = jnp.where(core == 0, theirs, mine)
+    for xl in range(2):
+        pieces = []
+        for m in range(4):
+            at = (xl * 4 + m) * 16
+            pieces += [first[at : at + 16], second[at : at + 16]]
+        mixed = contract(left, jnp.concatenate(pieces, axis=0), 1, 1)
+        high = mixed.astype(BF16).astype(F32)
+        for iq in range(3):
             for part, values in enumerate((high, mixed - high)):
-                for iq in range(3):
-                    blocks = [values[(iq * 4 + ii) * 8 : (iq * 4 + ii + 1) * 8] for ii in range(4)]
-                    for m, block in enumerate(swap_blocks(blocks, lane)):
-                        to = (xl * 8 + m + half * (7 - 2 * m)) * 2 + part
-                        rows_ref[iq, pl.ds(to, 8, stride=32), :] = block
-    for t in range(3):
-        sent_ref[:, :, t * 128 : (t + 1) * 128] = rows_ref[t].astype(BF16).reshape(128, 2, 128)
-
-
-def update_kernel(got_ref, normed_ref, gate_ref, columns_ref, weight_ref, out_ref, rows_ref, flat_ref):
+                blocks = [values[(iq * 4 + ii) * 8 : (iq * 4 + ii + 1) * 8] for ii in range(4)]
+                for m, block in enumerate(swap_blocks(blocks, lane)):
+                    slot = (m + half * (3 - 2 * m)) * 2 + part
+                    slots_ref[xl * 3 + iq, pl.ds(pl.multiple_of(slot * 8, 8), 8), :] = block
+            for g in range(8):
+                rows = slots_ref[xl * 3 + iq, pl.ds(g, 8, stride=8), :]
+                to = g * 16 + xl * 8 + half * 4
+                sent_ref[pl.ds(to, 4), :, iq * 128 : (iq + 1) * 128] = rows.astype(BF16).reshape(4, 2, 128)
+
+
+def near_kernel(
+    place_ref,
+    left_ref,
+    mine_ref,
+    theirs_ref,
+    normed_ref,
+    og_ref,
+    sent_ref,
+    gate_ref,
+    slots_ref,
+):
+    mix_half(place_ref, 0, left_ref, mine_ref, theirs_ref, sent_ref, slots_ref)
+    gate_ref[...] = sigmoid(contract(normed_ref[...], og_ref[...], 1, 0))
+
+
+def far_kernel(place_ref, left_ref, mine_ref, theirs_ref, half_ref, sent_ref, slots_ref):
+    del half_ref
+    mix_half(place_ref, 1, left_ref, mine_ref, theirs_ref, sent_ref, slots_ref)
+
+
+def update_kernel(got_ref, gate_ref, columns_ref, weight_ref, out_ref, rows_ref, flat_ref):
     rows, cols, width = out_ref.shape
     gain = columns_ref[0][:, 0:1]
     bias = columns_ref[1][:, 0:1]
@@ -171,8 +184,7 @@
             at = (3 * ii + iq) * cols
             flat_ref[at : at + 12, :] = output[ii * WIDE : ii * WIDE + 12]
             flat_ref[at + 12 : at + 24, :] = output[ii * WIDE + 16 : ii * WIDE + 28]
-    gated = sigmoid(contract(normed_ref[...], gate_ref[...], 1, 0))
-    out_ref[...] = (gated * flat_ref[...]).astype(BF16).reshape(rows, cols, width)
+    out_ref[...] = (gate_ref[...] * flat_ref[...]).astype(BF16).reshape(rows, cols, width)
 
 
 def shards(
@@ -202,60 +214,69 @@
         in_specs=[SMEM, SMEM] + [VMEM] * 3,
         out_specs=(VMEM, VMEM),
         compiler_params=params,
-        cost_estimate=pl.CostEstimate(flops=0, bytes_accessed=NORM_BYTES, transcendentals=0),
     )(place, token_mask, pair, norm_in_gain.reshape(1, -1), norm_in_bias.reshape(1, -1))
+    message = struct((128, 2, rows * WIDE), BF16)
     sent, columns = pl.pallas_call(
         edges_kernel,
         name="edges",
-        out_shape=(
-            struct((128, 2, rows * WIDE), BF16),
-            struct((2, width, width), F32),
-        ),
+        out_shape=(message, struct((2, width, width), F32)),
         in_specs=[VMEM] * 7,
         out_specs=(VMEM, VMEM),
         scratch_shapes=[pltpu.VMEM((3, 256, 128), F32)],
         compiler_params=params,
-    )(
-        masked,
-        left_gate,
-        left_value,
-        right_gate,
-        right_value,
-        norm_out_gain.reshape(1, -1),
-        norm_out_bias.reshape(1, -1),
-    )
+    )(masked, left_gate, left_value, right_gate, right_value, norm_out_gain.reshape(1, -1), norm_out_bias.reshape(1, -1))
     got = lax.all_to_all(sent, BOTH, 0, 0, axis_index_groups=SHARING)
-    left, right = pl.pallas_call(
-        arrange_kernel,
-        name="arrange",
-        out_shape=(struct((96, 384), BF16), struct((128, 384), BF16)),
+    scratch = [pltpu.VMEM((3, 256, 128), F32), pltpu.VMEM((384, 128), F32)]
+    right = pl.pallas_call(
+        right_kernel,
+        name="right",
+        out_shape=struct((128, 384), BF16),
         in_specs=[VMEM],
-        out_specs=(VMEM, VMEM),
-        scratch_shapes=[pltpu.VMEM((3, 256, 128), F32), pltpu.VMEM((768, 128), F32), pltpu.VMEM((3, 128, 128), F32)],
+        out_specs=VMEM,
+        scratch_shapes=scratch + [pltpu.VMEM((3, 128, 128), F32)],
+        compiler_params=params,
+    )(got)
+    left = pl.pallas_call(
+        left_kernel,
+        name="left",
+        out_shape=struct((96, 384), BF16),
+        in_specs=[VMEM],
+        out_specs=VMEM,
+        scratch_shapes=scratch,
         compiler_params=params,
     )(got)
     near = lax.ppermute(right, BOTH, CORE_FLIP)
     far = lax.ppermute(right, BOTH, HALF_FLIP)
     both = lax.ppermute(far, BOTH, CORE_FLIP)
+    sent, gate = pl.pallas_call(
+        near_kernel,
+        name="near",
+        out_shape=(message, struct((rows * cols, width), F32)),
+        in_specs=[SMEM] + [VMEM] * 5,
+        out_specs=(VMEM, VMEM),
+        scratch_shapes=[pltpu.VMEM((6, 64, 128), F32)],
+        compiler_params=params,
+    )(place, left, right, near, normed, output_gate)
     sent = pl.pallas_call(
-        mix_kernel,
-        name="mix",
-        out_shape=struct((128, 2, rows * WIDE), BF16),
-        in_specs=[SMEM] + [VMEM] * 5,
-        out_specs=VMEM,
-        scratch_shapes=[pltpu.VMEM((3, 256, 128), F32)],
-        compiler_params=params,
-    )(place, left, right, near, far, both)
+        far_kernel,
+        name="far",
+        out_shape=message,
+        in_specs=[SMEM] + [VMEM] * 4,
+        out_specs=VMEM,
+        scratch_shapes=[pltpu.VMEM((6, 64, 128), F32)],
+        input_output_aliases={4: 0},
+        compiler_params=params,
+    )(place, left, far, both, sent)
     got = lax.all_to_all(sent, BOTH, 0, 0, axis_index_groups=SHARING)
     return pl.pallas_call(
         update_kernel,
         name="update",
         out_shape=struct((rows, cols, width), BF16),
-        in_specs=[VMEM] * 5,
+        in_specs=[VMEM] * 4,
         out_specs=VMEM,
         scratch_shapes=[pltpu.VMEM((3, 256, 128), F32), pltpu.VMEM((rows * cols, 128), F32)],
         compiler_params=params,
-    )(got, normed, output_gate, columns, output_weight)
+    )(got, gate, columns, output_weight)
 
 
 def solution(mesh):

time: 69.4 us -> 69.4 us (level)
  waiting for transfers between devices: 0.92 us -> 0.01 us
    ppermute x1, waiting for transfers between devices: 0.91 us -> 0.01 us  [shards(): both = lax.ppermute(far, BOTH, CORE_FLIP)]
    pallas_call x3 -> x5, Pallas kernels: 2.45 us -> 3.16 us  [the longest x1 0.94 us: shards(): pl.pallas_call(near_kernel, name='near', out_shape=(message, struct((rows...]
  transfers between devices with their start and end apart: 3 -> 3, of which waited for: 1 -> 0; matrix products, arithmetic and copies ran while one was open for 0% -> 0% of each run, Pallas kernels for 0% -> 2%
where the time goes in v6:
time: 69.4 us; the launch traced here: 68.9 us
  blocking collectives  49.3 us (71%)
  starting transfers between devices  12.8 us (18%)
  Pallas kernels  5.03 us (7%)
  local copies, waits for them, and re-layouts  1.63 us (2%)
    all_to_all x2, blocking collectives, shards(): got = lax.all_to_all(sent, BOTH, 0, 0, axis_index_groups=SHARING)  49.3 us
    ppermute x1, starting transfers between devices, shards(): far = lax.ppermute(right, BOTH, HALF_FLIP)  4.41 us
    ppermute x1, starting transfers between devices, shards(): near = lax.ppermute(right, BOTH, CORE_FLIP)  4.32 us
    ppermute x1, starting transfers between devices, shards(): both = lax.ppermute(far, BOTH, CORE_FLIP)  4.04 us
    unnamed x24, local copies, waits for them, and re-layouts  1.55 us
  transfers between devices with their start and end apart: 3, of which 0 were waited for; matrix products, arithmetic and copies ran while one was open for 0% of the time, Pallas kernels for 2%

profile of v6, /device:TPU:1, one launch (start us, length us, event | category | flops | bytes accessed | tf_op | source)
XLA Modules:
  0.0 68.9 jit_solution(8458583258441498601)
XLA Ops:
  0.0 0.0 copy-start.7
  0.0 0.0 copy-start.8
  0.0 0.0 copy-start.9
  0.0 0.0 copy-start.3
  0.1 0.1 stack.23.place_ref
  0.1 0.7 %copy-done = bf16[12,24,128]{2,1,0:T(8,128)(2,1)S(1)} copy-done((bf16[12,24,128]{2,1,0:T(8,128)(2,1)S(1)}, bf16[12,24,128]{2,1,0:T(8,128)(2,1)}, u32[]{:S(2)}) %copy-start) | copy-done | bytes 73752
  0.9 0.0 copy-done.7
  0.9 0.0 copy-done.8
  0.9 0.0 copy-done.9
  0.9 0.0 copy-start.2
  0.9 0.8 %norm.1 = (bf16[288,128]{1,0:T(8,128)(2,1)S(1)}, bf16[384,128]{1,0:T(8,128)(2,1)S(1)}) custom-call(s32[5]{0:T(128)S(1)} %stack.23.place_ref, s32[384]{0:T(512)S(1)} %copy-done.7, bf16[12,24,128]{2,1,0:T(8,128)(2,1)S(1)} %copy-done, f32[1,128]{1,0:T(1,128)S(1)} %bitcast.9, f32[1,128]{1,0:T(1,128)S(1)} %bitcast.10), custom_call_target="tpu_custom_call" | custom-call | tf_op jit(solution)/shard_map/norm/pallas_call | solution.py:210
  1.7 0.0 copy-done.10
  1.7 0.0 copy-done.11
  1.7 0.0 copy-done.3
  1.7 0.0 copy-start.4
  1.7 0.7 %copy-done.4 = bf16[128,128]{1,0:T(8,128)(2,1)S(1)} copy-done((bf16[128,128]{1,0:T(8,128)(2,1)S(1)}, bf16[128,128]{1,0:T(8,128)(2,1)}, u32[]{:S(2)}) %copy-start.4) | copy-done | bytes 32792
  2.5 0.4 edges.1
  2.9 30.4 %all_to_all.10.got_ref = bf16[128,2,384]{2,1,0:T(2,128)(2,1)S(1)} all-to-all(bf16[128,2,384]{2,1,0:T(2,128)(2,1)S(1)} %get-tuple-element.12), channel_id=1, replica_groups={{0,1,2,3,4,5,6,7,8,9,10,11,12,13,14,15,32,33,34,35,36,37,38,39,40,41,42..., dimensions={0} | all-to-all | bytes 393216 | tf_op jit(solution)/shard_map/all_to_all | solution.py:228
  33.4 0.4 right.1.mine_ref
  33.8 0.0 copy-start.5
  33.9 4.4 %collective-permute-start = (bf16[128,384]{1,0:T(8,128)(2,1)S(1)}, bf16[128,384]{1,0:T(8,128)(2,1)S(1)}, u32[]{:S(2)}, u32[]{:S(2)}) collective-permute-start(bf16[128,384]{1,0:T(8,128)(2,1)S(1)} %right.1.mine_ref), channel_id=1, source_target_pairs={{0,224},{1,225},{2,226},{3,227},{4,228},{5,229},{6,230},{7,231},{8... | collective-permute-start | bytes 294920 | tf_op jit(solution)/shard_map/ppermute | solution.py:249
  38.3 4.3 %collective-permute-start.2 = (bf16[128,384]{1,0:T(8,128)(2,1)S(1)}, bf16[128,384]{1,0:T(8,128)(2,1)S(1)}, u32[]{:S(2)}, u32[]{:S(2)}) collective-permute-start(bf16[128,384]{1,0:T(8,128)(2,1)S(1)} %right.1.mine_ref), channel_id=1, source_target_pairs={{0,16},{1,17},{2,18},{3,19},{4,20},{5,21},{6,22},{7,23},{8,24},{9,... | collective-permute-start | bytes 294920 | tf_op jit(solution)/shard_map/ppermute | solution.py:248
  42.6 0.0 collective-permute-done.mine_ref
  42.6 4.0 %collective-permute-start.1 = (bf16[128,384]{1,0:T(8,128)(2,1)S(1)}, bf16[128,384]{1,0:T(8,128)(2,1)S(1)}, u32[]{:S(2)}, u32[]{:S(2)}) collective-permute-start(bf16[128,384]{1,0:T(8,128)(2,1)S(1)} %collective-permute-done.mine_ref), channel_id=1, source_target_pairs={{0,16},{1,17},{2,18},{3,19},{4,20},{5,21},{6,22},{7,23},{8,24},{9,... | collective-permute-start | bytes 294920 | tf_op jit(solution)/shard_map/ppermute | solution.py:250
  46.7 0.4 left.1.left_ref
  47.1 0.0 collective-permute-done.2.theirs_ref
  47.1 0.9 %near.1 = (bf16[128,2,384]{2,1,0:T(2,128)(2,1)S(1)}, f32[288,128]{1,0:T(8,128)S(1)}) custom-call(s32[5]{0:T(128)S(1)} %stack.23.place_ref, bf16[96,384]{1,0:T(8,128)(2,1)S(1)} %left.1.left_ref, bf16[128,384]{1,0:T(8,128)(2,1)S(1)} %right.1.mine_ref, bf16[128,384]{1,0:T(8,128)(2,1)S(1)} %collective-permute-done.2.theirs_ref, ...), custom_call_target="tpu_custom_call" | custom-call | tf_op jit(solution)/shard_map/near/pallas_call | solution.py:251
  48.0 0.0 collective-permute-done.1.theirs_ref
  48.0 0.9 %far.1 = bf16[128,2,384]{2,1,0:T(2,128)(2,1)S(1)} custom-call(s32[5]{0:T(128)S(1)} %stack.23.place_ref, bf16[96,384]{1,0:T(8,128)(2,1)S(1)} %left.1.left_ref, bf16[128,384]{1,0:T(8,128)(2,1)S(1)} %collective-permute-done.mine_ref, bf16[128,384]{1,0:T(8,128)(2,1)S(1)} %collective-permute-done.1.theirs_ref, ...), custom_call_target="tpu_custom_call", output_to_operand_aliasing={{}: (4, {})} | custom-call | tf_op jit(solution)/shard_map/far/pallas_call | solution.py:260
  49.0 0.0 copy-start.6
  49.0 18.8 %all_to_all.11.got_ref = bf16[128,2,384]{2,1,0:T(2,128)(2,1)S(1)} all-to-all(bf16[128,2,384]{2,1,0:T(2,128)(2,1)S(1)} %far.1), channel_id=1, replica_groups={{0,1,2,3,4,5,6,7,8,9,10,11,12,13,14,15,32,33,34,35,36,37,38,39,40,41,42..., dimensions={0} | all-to-all | bytes 393216 | tf_op jit(solution)/shard_map/all_to_all | solution.py:270
  67.8 1.1 %update.1 = bf16[12,24,128]{2,1,0:T(8,128)(2,1)} custom-call(bf16[128,2,384]{2,1,0:T(2,128)(2,1)S(1)} %all_to_all.11.got_ref, f32[288,128]{1,0:T(8,128)S(1)} %get-tuple-element.15.gate_ref, f32[2,128,128]{2,1,0:T(8,128)S(1)} %get-tuple-element.16.columns_ref, bf16[128,128]{1,0:T(8,128)(2,1)S(1)} %copy-done.6), custom_call_target="tpu_custom_call" | custom-call | tf_op jit(solution)/shard_map/update/pallas_call | solution.py:271
  (8 shorter events, 0.0 us)
Async XLA Ops:
  0.0 0.9 %copy-start = (bf16[12,24,128]{2,1,0:T(8,128)(2,1)S(1)}, bf16[12,24,128]{2,1,0:T(8,128)(2,1)}, u32[]{:S(2)}) copy-start(bf16[12,24,128]{2,1,0:T(8,128)(2,1)} %pair_ref.1) | copy-start | bytes 221188
  0.0 1.7 %copy-start.10 = (f32[128]{0:T(128)S(1)}, f32[128]{0:T(128)}, u32[]{:S(2)}) copy-start(f32[128]{0:T(128)} %param.21) | copy-start | bytes 1540
  0.0 1.7 %copy-start.11 = (f32[128]{0:T(128)S(1)}, f32[128]{0:T(128)}, u32[]{:S(2)}) copy-start(f32[128]{0:T(128)} %param.22) | copy-start | bytes 1540
  0.0 0.9 %copy-start.7 = (s32[384]{0:T(512)S(1)}, s32[384]{0:T(512)}, u32[]{:S(2)}) copy-start(s32[384]{0:T(512)} %mask_ref.1) | copy-start | bytes 4612
  0.0 0.9 %copy-start.8 = (f32[128]{0:T(128)S(1)}, f32[128]{0:T(128)}, u32[]{:S(2)}) copy-start(f32[128]{0:T(128)} %param.14) | copy-start | bytes 1540
  0.0 0.9 %copy-start.9 = (f32[128]{0:T(128)S(1)}, f32[128]{0:T(128)}, u32[]{:S(2)}) copy-start(f32[128]{0:T(128)} %param.15) | copy-start | bytes 1540
  0.0 1.7 %copy-start.3 = (bf16[128,128]{1,0:T(8,128)(2,1)S(1)}, bf16[128,128]{1,0:T(8,128)(2,1)}, u32[]{:S(2)}) copy-start(bf16[128,128]{1,0:T(8,128)(2,1)} %rg_ref.1) | copy-start | bytes 98308
  0.9 0.8 %copy-start.1 = (bf16[128,128]{1,0:T(8,128)(2,1)S(1)}, bf16[128,128]{1,0:T(8,128)(2,1)}, u32[]{:S(2)}) copy-start(bf16[128,128]{1,0:T(8,128)(2,1)} %lg_ref.1) | copy-start | bytes 98308
  0.9 0.8 %copy-start.2 = (bf16[128,128]{1,0:T(8,128)(2,1)S(1)}, bf16[128,128]{1,0:T(8,128)(2,1)}, u32[]{:S(2)}) copy-start(bf16[128,128]{1,0:T(8,128)(2,1)} %lv_ref.1) | copy-start | bytes 98308
  1.7 0.8 %copy-start.4 = (bf16[128,128]{1,0:T(8,128)(2,1)S(1)}, bf16[128,128]{1,0:T(8,128)(2,1)}, u32[]{:S(2)}) copy-start(bf16[128,128]{1,0:T(8,128)(2,1)} %rv_ref.1) | copy-start | bytes 98308
  33.8 13.2 %copy-start.5 = (bf16[128,128]{1,0:T(8,128)(2,1)S(1)}, bf16[128,128]{1,0:T(8,128)(2,1)}, u32[]{:S(2)}) copy-start(bf16[128,128]{1,0:T(8,128)(2,1)} %og_ref.1) | copy-start | bytes 98308
  33.9 8.7 %collective-permute-start = (bf16[128,384]{1,0:T(8,128)(2,1)S(1)}, bf16[128,384]{1,0:T(8,128)(2,1)S(1)}, u32[]{:S(2)}, u32[]{:S(2)}) collective-permute-start(bf16[128,384]{1,0:T(8,128)(2,1)S(1)} %right.1.mine_ref), channel_id=1, source_target_pairs={{0,224},{1,225},{2,226},{3,227},{4,228},{5,229},{6,230},{7,231},{8... | collective-permute-start | bytes 294920 | tf_op jit(solution)/shard_map/ppermute | solution.py:249
  38.3 8.8 %collective-permute-start.2 = (bf16[128,384]{1,0:T(8,128)(2,1)S(1)}, bf16[128,384]{1,0:T(8,128)(2,1)S(1)}, u32[]{:S(2)}, u32[]{:S(2)}) collective-permute-start(bf16[128,384]{1,0:T(8,128)(2,1)S(1)} %right.1.mine_ref), channel_id=1, source_target_pairs={{0,16},{1,17},{2,18},{3,19},{4,20},{5,21},{6,22},{7,23},{8,24},{9,... | collective-permute-start | bytes 294920 | tf_op jit(solution)/shard_map/ppermute | solution.py:248
  42.6 5.4 %collective-permute-start.1 = (bf16[128,384]{1,0:T(8,128)(2,1)S(1)}, bf16[128,384]{1,0:T(8,128)(2,1)S(1)}, u32[]{:S(2)}, u32[]{:S(2)}) collective-permute-start(bf16[128,384]{1,0:T(8,128)(2,1)S(1)} %collective-permute-done.mine_ref), channel_id=1, source_target_pairs={{0,16},{1,17},{2,18},{3,19},{4,20},{5,21},{6,22},{7,23},{8,24},{9,... | collective-permute-start | bytes 294920 | tf_op jit(solution)/shard_map/ppermute | solution.py:250
  49.0 18.8 %copy-start.6 = (bf16[128,128]{1,0:T(8,128)(2,1)S(1)}, bf16[128,128]{1,0:T(8,128)(2,1)}, u32[]{:S(2)}) copy-start(bf16[128,128]{1,0:T(8,128)(2,1)} %weight_ref.1) | copy-start | bytes 98308

commit v7 on v6

--- a/solution.py
+++ b/solution.py
@@ -44,7 +44,11 @@
     return lax.dot_general(a, b, (((da,), (db,)), ((), ())), preferred_element_type=F32)
 
 
-def norm_kernel(place_ref, mask_ref, pair_ref, gain_ref, bias_ref, normed_ref, masked_ref):
+def zeros_kernel(zeros_ref):
+    zeros_ref[...] = jnp.zeros_like(zeros_ref)
+
+
+def norm_kernel(place_ref, mask_ref, pair_ref, gain_ref, bias_ref, zeros_ref, normed_ref, masked_ref):
     rows, cols, width = pair_ref.shape
     x = pair_ref[...].astype(F32).reshape(rows * cols, width)
     mean = jnp.mean(x, axis=-1, keepdims=True)
@@ -60,7 +64,7 @@
     for i in [3 * ii + iq for iq in range(3) for ii in range(4)]:
         row_valid = mask_ref[place_ref[0] + i].astype(F32)
         parts.append(normed[i * cols : (i + 1) * cols] * (col_valid * row_valid))
-        parts.append(jnp.zeros((WIDE - cols, width), F32))
+        parts.append(zeros_ref[0 : WIDE - cols])
     masked_ref[...] = jnp.concatenate(parts, axis=0).astype(BF16)
 
 
@@ -104,13 +108,12 @@
     return spread
 
 
-def right_kernel(got_ref, right_ref, rows_ref, quads_ref, padded_ref):
-    padded_ref[...] = jnp.zeros_like(padded_ref)
+def right_kernel(got_ref, right_ref, rows_ref, quads_ref, dense_ref):
     for (iq, ii), dense in spread_side(0, got_ref, rows_ref, quads_ref).items():
         for v in range(3):
-            padded_ref[v, pl.ds(ii * 3 + iq, 8, stride=16), :] = dense[v]
+            dense_ref[v, pl.ds(ii * 3 + iq, 8, stride=12), :] = dense[v]
     for v in range(3):
-        right_ref[:, v * 128 : (v + 1) * 128] = padded_ref[v].astype(BF16)
+        right_ref[:, v * 128 : (v + 1) * 128] = dense_ref[v].astype(BF16)
 
 
 def left_kernel(got_ref, left_ref, rows_ref, quads_ref):
@@ -124,20 +127,22 @@
 def mix_half(place_ref, other, left_ref, mine_ref, theirs_ref, sent_ref, slots_ref):
     lane = iota((8, 128), 1)
     left = left_ref[...]
-    mine, theirs = mine_ref[...], theirs_ref[...]
     core = place_ref[2]
     half = place_ref[3 + other]
-    first = jnp.where(core == 0, mine, theirs)
-    second = jnp.where(core == 0, theirs, mine)
+    column = iota((96, 128), 0)
+    side = jnp.where(column >= 48, 1, 0)
+    m = sum(jnp.where(column - 48 * side >= 12 * n, 1, 0) for n in range(1, 4))
+    to_lane = column - 48 * side + 20 * m + 16 * jnp.where(side == 0, core, 1 - core)
+    spread = jnp.where(iota((96, 128), 1) == to_lane, 1.0, 0.0).astype(BF16)
     for xl in range(2):
-        pieces = []
-        for m in range(4):
-            at = (xl * 4 + m) * 16
-            pieces += [first[at : at + 16], second[at : at + 16]]
-        mixed = contract(left, jnp.concatenate(pieces, axis=0), 1, 1)
-        high = mixed.astype(BF16).astype(F32)
+        rows = slice(xl * 48, (xl + 1) * 48)
+        right = jnp.concatenate([mine_ref[rows, :], theirs_ref[rows, :]], axis=0)
+        mixed = contract(left, right, 1, 1)
+        high = mixed.astype(BF16)
+        low = (mixed - high.astype(F32)).astype(BF16)
+        high, low = contract(high, spread, 1, 0), contract(low, spread, 1, 0)
         for iq in range(3):
-            for part, values in enumerate((high, mixed - high)):
+            for part, values in enumerate((high, low)):
                 blocks = [values[(iq * 4 + ii) * 8 : (iq * 4 + ii + 1) * 8] for ii in range(4)]
                 for m, block in enumerate(swap_blocks(blocks, lane)):
                     slot = (m + half * (3 - 2 * m)) * 2 + part
@@ -207,14 +212,21 @@
     half = row_block // 8 % 2
     place = jnp.stack([row_block * rows, lax.axis_index("ja") * cols, row_block % 2, half, 1 - half]).astype(jnp.int32)
     struct = jax.ShapeDtypeStruct
+    zeros = pl.pallas_call(
+        zeros_kernel,
+        name="zeros",
+        out_shape=struct((width, width), F32),
+        out_specs=VMEM,
+        compiler_params=params,
+    )()
     normed, masked = pl.pallas_call(
         norm_kernel,
         name="norm",
         out_shape=(struct((rows * cols, width), BF16), struct((rows * WIDE, width), BF16)),
-        in_specs=[SMEM, SMEM] + [VMEM] * 3,
+        in_specs=[SMEM, SMEM] + [VMEM] * 4,
         out_specs=(VMEM, VMEM),
         compiler_params=params,
-    )(place, token_mask, pair, norm_in_gain.reshape(1, -1), norm_in_bias.reshape(1, -1))
+    )(place, token_mask, pair, norm_in_gain.reshape(1, -1), norm_in_bias.reshape(1, -1), zeros)
     message = struct((128, 2, rows * WIDE), BF16)
     sent, columns = pl.pallas_call(
         edges_kernel,
@@ -230,10 +242,10 @@
     right = pl.pallas_call(
         right_kernel,
         name="right",
-        out_shape=struct((128, 384), BF16),
+        out_shape=struct((96, 384), BF16),
         in_specs=[VMEM],
         out_specs=VMEM,
-        scratch_shapes=scratch + [pltpu.VMEM((3, 128, 128), F32)],
+        scratch_shapes=scratch + [pltpu.VMEM((3, 96, 128), F32)],
         compiler_params=params,
     )(got)
     left = pl.pallas_call(

time: 69.4 us -> 68.9 us (level)
  no operation moved by 1% of the time
where the time goes in v7:
time: 68.9 us; the launch traced here: 68.4 us
  blocking collectives  49 us (71%)
  starting transfers between devices  12.2 us (18%)
  Pallas kernels  5.42 us (8%)
  local copies, waits for them, and re-layouts  1.51 us (2%)
    all_to_all x2, blocking collectives, shards(): got = lax.all_to_all(sent, BOTH, 0, 0, axis_index_groups=SHARING)  49 us
    ppermute x1, starting transfers between devices, shards(): far = lax.ppermute(right, BOTH, HALF_FLIP)  4.42 us
    ppermute x1, starting transfers between devices, shards(): near = lax.ppermute(right, BOTH, CORE_FLIP)  4.31 us
    ppermute x1, starting transfers between devices, shards(): both = lax.ppermute(far, BOTH, CORE_FLIP)  3.52 us
    unnamed x24, local copies, waits for them, and re-layouts  1.42 us
  transfers between devices with their start and end apart: 3, of which 0 were waited for; matrix products, arithmetic and copies ran while one was open for 0% of the time, Pallas kernels for 2%

profile of v7, /device:TPU:1, one launch (start us, length us, event | category | flops | bytes accessed | tf_op | source)
XLA Modules:
  0.0 68.4 jit_solution(8930815724764633915)
XLA Ops:
  0.0 0.1 stack.23.place_ref
  0.1 0.8 %copy-done = bf16[12,24,128]{2,1,0:T(8,128)(2,1)S(1)} copy-done((bf16[12,24,128]{2,1,0:T(8,128)(2,1)S(1)}, bf16[12,24,128]{2,1,0:T(8,128)(2,1)}, u32[]{:S(2)}) %copy-start) | copy-done | bytes 73752
  0.9 0.0 copy-done.7
  0.9 0.0 copy-done.9
  0.9 0.0 copy-start.2
  0.9 0.0 copy-start.3
  0.9 0.0 copy-start.4
  0.9 0.8 %norm.1 = (bf16[288,128]{1,0:T(8,128)(2,1)S(1)}, bf16[384,128]{1,0:T(8,128)(2,1)S(1)}) custom-call(s32[5]{0:T(128)S(1)} %stack.23.place_ref, s32[384]{0:T(512)S(1)} %copy-done.7, bf16[12,24,128]{2,1,0:T(8,128)(2,1)S(1)} %copy-done, f32[1,128]{1,0:T(1,128)S(1)} %bitcast.9, f32[1,128]{1,0:T(1,128)S(1)} %bitcast.10, f32[128,128]{1,0:T(8,128)S(1)} %zeros.1.zeros_ref), custom_call_target="tpu_custom_call" | custom-call | tf_op jit(solution)/shard_map/norm/pallas_call | solution.py:222
  1.7 0.0 copy-start.10
  1.7 0.0 copy-start.11
  1.7 0.0 copy-done.1
  1.7 0.0 copy-done.2
  1.8 0.0 copy-done.3
  1.8 0.0 copy-done.4
  1.8 0.6 copy-done.10
  2.4 0.0 copy-done.11
  2.4 0.4 edges.1
  2.8 30.4 %all_to_all.10.got_ref = bf16[128,2,384]{2,1,0:T(2,128)(2,1)S(1)} all-to-all(bf16[128,2,384]{2,1,0:T(2,128)(2,1)S(1)} %get-tuple-element.12), channel_id=1, replica_groups={{0,1,2,3,4,5,6,7,8,9,10,11,12,13,14,15,32,33,34,35,36,37,38,39,40,41,42..., dimensions={0} | all-to-all | bytes 393216 | tf_op jit(solution)/shard_map/all_to_all | solution.py:240
  33.3 0.4 right.1.mine_ref
  33.7 0.0 copy-start.5
  33.7 4.4 %collective-permute-start = (bf16[96,384]{1,0:T(8,128)(2,1)S(1)}, bf16[96,384]{1,0:T(8,128)(2,1)S(1)}, u32[]{:S(2)}, u32[]{:S(2)}) collective-permute-start(bf16[96,384]{1,0:T(8,128)(2,1)S(1)} %right.1.mine_ref), channel_id=1, source_target_pairs={{0,224},{1,225},{2,226},{3,227},{4,228},{5,229},{6,230},{7,231},{8... | collective-permute-start | bytes 221192 | tf_op jit(solution)/shard_map/ppermute | solution.py:261
  38.1 4.3 %collective-permute-start.2 = (bf16[96,384]{1,0:T(8,128)(2,1)S(1)}, bf16[96,384]{1,0:T(8,128)(2,1)S(1)}, u32[]{:S(2)}, u32[]{:S(2)}) collective-permute-start(bf16[96,384]{1,0:T(8,128)(2,1)S(1)} %right.1.mine_ref), channel_id=1, source_target_pairs={{0,16},{1,17},{2,18},{3,19},{4,20},{5,21},{6,22},{7,23},{8,24},{9,... | collective-permute-start | bytes 221192 | tf_op jit(solution)/shard_map/ppermute | solution.py:260
  42.5 0.0 collective-permute-done.mine_ref
  42.5 3.5 %collective-permute-start.1 = (bf16[96,384]{1,0:T(8,128)(2,1)S(1)}, bf16[96,384]{1,0:T(8,128)(2,1)S(1)}, u32[]{:S(2)}, u32[]{:S(2)}) collective-permute-start(bf16[96,384]{1,0:T(8,128)(2,1)S(1)} %collective-permute-done.mine_ref), channel_id=1, source_target_pairs={{0,16},{1,17},{2,18},{3,19},{4,20},{5,21},{6,22},{7,23},{8,24},{9,... | collective-permute-start | bytes 221192 | tf_op jit(solution)/shard_map/ppermute | solution.py:262
  46.0 0.4 left.1.left_ref
  46.4 0.0 collective-permute-done.2.theirs_ref
  46.4 1.2 %near.1 = (bf16[128,2,384]{2,1,0:T(2,128)(2,1)S(1)}, f32[288,128]{1,0:T(8,128)S(1)}) custom-call(s32[5]{0:T(128)S(1)} %stack.23.place_ref, bf16[96,384]{1,0:T(8,128)(2,1)S(1)} %left.1.left_ref, bf16[96,384]{1,0:T(8,128)(2,1)S(1)} %right.1.mine_ref, bf16[96,384]{1,0:T(8,128)(2,1)S(1)} %collective-permute-done.2.theirs_ref, ...), custom_call_target="tpu_custom_call" | custom-call | tf_op jit(solution)/shard_map/near/pallas_call | solution.py:263
  47.6 0.0 collective-permute-done.1.theirs_ref
  47.6 1.1 %far.1 = bf16[128,2,384]{2,1,0:T(2,128)(2,1)S(1)} custom-call(s32[5]{0:T(128)S(1)} %stack.23.place_ref, bf16[96,384]{1,0:T(8,128)(2,1)S(1)} %left.1.left_ref, bf16[96,384]{1,0:T(8,128)(2,1)S(1)} %collective-permute-done.mine_ref, bf16[96,384]{1,0:T(8,128)(2,1)S(1)} %collective-permute-done.1.theirs_ref, ...), custom_call_target="tpu_custom_call", output_to_operand_aliasing={{}: (4, {})} | custom-call | tf_op jit(solution)/shard_map/far/pallas_call | solution.py:272
  48.7 0.0 copy-start.6
  48.7 18.6 %all_to_all.11.got_ref = bf16[128,2,384]{2,1,0:T(2,128)(2,1)S(1)} all-to-all(bf16[128,2,384]{2,1,0:T(2,128)(2,1)S(1)} %far.1), channel_id=1, replica_groups={{0,1,2,3,4,5,6,7,8,9,10,11,12,13,14,15,32,33,34,35,36,37,38,39,40,41,42..., dimensions={0} | all-to-all | bytes 393216 | tf_op jit(solution)/shard_map/all_to_all | solution.py:282
  67.3 1.1 %update.1 = bf16[12,24,128]{2,1,0:T(8,128)(2,1)} custom-call(bf16[128,2,384]{2,1,0:T(2,128)(2,1)S(1)} %all_to_all.11.got_ref, f32[288,128]{1,0:T(8,128)S(1)} %get-tuple-element.15.gate_ref, f32[2,128,128]{2,1,0:T(8,128)S(1)} %get-tuple-element.16.columns_ref, bf16[128,128]{1,0:T(8,128)(2,1)S(1)} %copy-done.6), custom_call_target="tpu_custom_call" | custom-call | tf_op jit(solution)/shard_map/update/pallas_call | solution.py:283
  (9 shorter events, 0.0 us)
Async XLA Ops:
  0.0 0.9 %copy-start = (bf16[12,24,128]{2,1,0:T(8,128)(2,1)S(1)}, bf16[12,24,128]{2,1,0:T(8,128)(2,1)}, u32[]{:S(2)}) copy-start(bf16[12,24,128]{2,1,0:T(8,128)(2,1)} %pair_ref.1) | copy-start | bytes 221188
  0.1 0.8 %copy-start.7 = (s32[384]{0:T(512)S(1)}, s32[384]{0:T(512)}, u32[]{:S(2)}) copy-start(s32[384]{0:T(512)} %mask_ref.1) | copy-start | bytes 4612
  0.1 0.8 %copy-start.8 = (f32[128]{0:T(128)S(1)}, f32[128]{0:T(128)}, u32[]{:S(2)}) copy-start(f32[128]{0:T(128)} %param.14) | copy-start | bytes 1540
  0.1 0.8 %copy-start.9 = (f32[128]{0:T(128)S(1)}, f32[128]{0:T(128)}, u32[]{:S(2)}) copy-start(f32[128]{0:T(128)} %param.15) | copy-start | bytes 1540
  0.9 0.8 %copy-start.1 = (bf16[128,128]{1,0:T(8,128)(2,1)S(1)}, bf16[128,128]{1,0:T(8,128)(2,1)}, u32[]{:S(2)}) copy-start(bf16[128,128]{1,0:T(8,128)(2,1)} %lg_ref.1) | copy-start | bytes 98308
  0.9 0.8 %copy-start.2 = (bf16[128,128]{1,0:T(8,128)(2,1)S(1)}, bf16[128,128]{1,0:T(8,128)(2,1)}, u32[]{:S(2)}) copy-start(bf16[128,128]{1,0:T(8,128)(2,1)} %lv_ref.1) | copy-start | bytes 98308
  0.9 0.8 %copy-start.3 = (bf16[128,128]{1,0:T(8,128)(2,1)S(1)}, bf16[128,128]{1,0:T(8,128)(2,1)}, u32[]{:S(2)}) copy-start(bf16[128,128]{1,0:T(8,128)(2,1)} %rg_ref.1) | copy-start | bytes 98308
  0.9 0.8 %copy-start.4 = (bf16[128,128]{1,0:T(8,128)(2,1)S(1)}, bf16[128,128]{1,0:T(8,128)(2,1)}, u32[]{:S(2)}) copy-start(bf16[128,128]{1,0:T(8,128)(2,1)} %rv_ref.1) | copy-start | bytes 98308
  1.7 0.7 copy-start.10
  1.7 0.7 copy-start.11
  33.7 12.7 %copy-start.5 = (bf16[128,128]{1,0:T(8,128)(2,1)S(1)}, bf16[128,128]{1,0:T(8,128)(2,1)}, u32[]{:S(2)}) copy-start(bf16[128,128]{1,0:T(8,128)(2,1)} %og_ref.1) | copy-start | bytes 98308
  33.7 8.8 %collective-permute-start = (bf16[96,384]{1,0:T(8,128)(2,1)S(1)}, bf16[96,384]{1,0:T(8,128)(2,1)S(1)}, u32[]{:S(2)}, u32[]{:S(2)}) collective-permute-start(bf16[96,384]{1,0:T(8,128)(2,1)S(1)} %right.1.mine_ref), channel_id=1, source_target_pairs={{0,224},{1,225},{2,226},{3,227},{4,228},{5,229},{6,230},{7,231},{8... | collective-permute-start | bytes 221192 | tf_op jit(solution)/shard_map/ppermute | solution.py:261
  38.1 8.3 %collective-permute-start.2 = (bf16[96,384]{1,0:T(8,128)(2,1)S(1)}, bf16[96,384]{1,0:T(8,128)(2,1)S(1)}, u32[]{:S(2)}, u32[]{:S(2)}) collective-permute-start(bf16[96,384]{1,0:T(8,128)(2,1)S(1)} %right.1.mine_ref), channel_id=1, source_target_pairs={{0,16},{1,17},{2,18},{3,19},{4,20},{5,21},{6,22},{7,23},{8,24},{9,... | collective-permute-start | bytes 221192 | tf_op jit(solution)/shard_map/ppermute | solution.py:260
  42.5 5.1 %collective-permute-start.1 = (bf16[96,384]{1,0:T(8,128)(2,1)S(1)}, bf16[96,384]{1,0:T(8,128)(2,1)S(1)}, u32[]{:S(2)}, u32[]{:S(2)}) collective-permute-start(bf16[96,384]{1,0:T(8,128)(2,1)S(1)} %collective-permute-done.mine_ref), channel_id=1, source_target_pairs={{0,16},{1,17},{2,18},{3,19},{4,20},{5,21},{6,22},{7,23},{8,24},{9,... | collective-permute-start | bytes 221192 | tf_op jit(solution)/shard_map/ppermute | solution.py:262
  48.7 18.6 %copy-start.6 = (bf16[128,128]{1,0:T(8,128)(2,1)S(1)}, bf16[128,128]{1,0:T(8,128)(2,1)}, u32[]{:S(2)}) copy-start(bf16[128,128]{1,0:T(8,128)(2,1)} %weight_ref.1) | copy-start | bytes 98308

commit v8 on v7

--- a/solution.py
+++ b/solution.py
@@ -44,11 +44,30 @@
     return lax.dot_general(a, b, (((da,), (db,)), ((), ())), preferred_element_type=F32)
 
 
-def zeros_kernel(zeros_ref):
+def first_kernel(place_ref, zeros_ref, spread_ref):
     zeros_ref[...] = jnp.zeros_like(zeros_ref)
-
-
-def norm_kernel(place_ref, mask_ref, pair_ref, gain_ref, bias_ref, zeros_ref, normed_ref, masked_ref):
+    row = iota(spread_ref.shape, 0)
+    side = jnp.where(row >= 96, 1, 0)
+    row = row - 96 * side
+    run = sum(jnp.where(row >= 12 * n, 1, 0) for n in range(1, 8))
+    core = place_ref[2]
+    to_lane = row + 20 * run + 16 * jnp.where(side == 0, core, 1 - core)
+    spread_ref[...] = jnp.where(iota(spread_ref.shape, 1) == to_lane, 1.0, 0.0).astype(BF16)
+
+
+def norm_kernel(
+    place_ref,
+    mask_ref,
+    pair_ref,
+    gain_ref,
+    bias_ref,
+    out_gain_ref,
+    out_bias_ref,
+    zeros_ref,
+    normed_ref,
+    masked_ref,
+    columns_ref,
+):
     rows, cols, width = pair_ref.shape
     x = pair_ref[...].astype(F32).reshape(rows * cols, width)
     mean = jnp.mean(x, axis=-1, keepdims=True)
@@ -56,6 +75,8 @@
     variance = jnp.mean(centered * centered, axis=-1, keepdims=True)
     normed = centered * lax.rsqrt(variance + EPS) * gain_ref[...] + bias_ref[...]
     normed_ref[...] = normed.astype(BF16)
+    columns_ref[0] = jnp.transpose(jnp.broadcast_to(out_gain_ref[...], (width, width)))
+    columns_ref[1] = jnp.transpose(jnp.broadcast_to(out_bias_ref[...], (width, width)))
     place = iota((cols, width), 0)
     col_valid = jnp.zeros((cols, width), F32)
     for k in range(cols):
@@ -68,10 +89,8 @@
     masked_ref[...] = jnp.concatenate(parts, axis=0).astype(BF16)
 
 
-def edges_kernel(masked_ref, lg_ref, lv_ref, rg_ref, rv_ref, out_gain_ref, out_bias_ref, sent_ref, columns_ref, rows_ref):
+def edges_kernel(masked_ref, lg_ref, lv_ref, rg_ref, rv_ref, sent_ref, rows_ref):
     width = lg_ref.shape[0]
-    columns_ref[0] = jnp.transpose(jnp.broadcast_to(out_gain_ref[...], (width, width)))
-    columns_ref[1] = jnp.transpose(jnp.broadcast_to(out_bias_ref[...], (width, width)))
     masked = masked_ref[...]
     left = sigmoid(contract(lg_ref[...], masked, 0, 1)) * contract(lv_ref[...], masked, 0, 1)
     right = sigmoid(contract(rg_ref[...], masked, 0, 1)) * contract(rv_ref[...], masked, 0, 1)
@@ -124,26 +143,18 @@
             left_ref[iq * 32 : (iq + 1) * 32, v * 128 : (v + 1) * 128] = block.astype(BF16)
 
 
-def mix_half(place_ref, other, left_ref, mine_ref, theirs_ref, sent_ref, slots_ref):
+def mix_half(place_ref, other, left_ref, mine_ref, theirs_ref, spread_ref, sent_ref, slots_ref):
     lane = iota((8, 128), 1)
-    left = left_ref[...]
-    core = place_ref[2]
     half = place_ref[3 + other]
-    column = iota((96, 128), 0)
-    side = jnp.where(column >= 48, 1, 0)
-    m = sum(jnp.where(column - 48 * side >= 12 * n, 1, 0) for n in range(1, 4))
-    to_lane = column - 48 * side + 20 * m + 16 * jnp.where(side == 0, core, 1 - core)
-    spread = jnp.where(iota((96, 128), 1) == to_lane, 1.0, 0.0).astype(BF16)
+    mixed = contract(left_ref[...], jnp.concatenate([mine_ref[...], theirs_ref[...]], axis=0), 1, 1)
+    high = mixed.astype(BF16)
+    low = (mixed - high.astype(F32)).astype(BF16)
+    parts = contract(jnp.concatenate([high, low], axis=0), spread_ref[...], 1, 0)
     for xl in range(2):
-        rows = slice(xl * 48, (xl + 1) * 48)
-        right = jnp.concatenate([mine_ref[rows, :], theirs_ref[rows, :]], axis=0)
-        mixed = contract(left, right, 1, 1)
-        high = mixed.astype(BF16)
-        low = (mixed - high.astype(F32)).astype(BF16)
-        high, low = contract(high, spread, 1, 0), contract(low, spread, 1, 0)
         for iq in range(3):
-            for part, values in enumerate((high, low)):
-                blocks = [values[(iq * 4 + ii) * 8 : (iq * 4 + ii + 1) * 8] for ii in range(4)]
+            for part in range(2):
+                at = part * 96 + iq * 32
+                blocks = [parts[at + ii * 8 : at + (ii + 1) * 8, xl * 128 : (xl + 1) * 128] for ii in range(4)]
                 for m, block in enumerate(swap_blocks(blocks, lane)):
                     slot = (m + half * (3 - 2 * m)) * 2 + part
                     slots_ref[xl * 3 + iq, pl.ds(pl.multiple_of(slot * 8, 8), 8), :] = block
@@ -158,19 +169,20 @@
     left_ref,
     mine_ref,
     theirs_ref,
+    spread_ref,
     normed_ref,
     og_ref,
     sent_ref,
     gate_ref,
     slots_ref,
 ):
-    mix_half(place_ref, 0, left_ref, mine_ref, theirs_ref, sent_ref, slots_ref)
+    mix_half(place_ref, 0, left_ref, mine_ref, theirs_ref, spread_ref, sent_ref, slots_ref)
     gate_ref[...] = sigmoid(contract(normed_ref[...], og_ref[...], 1, 0))
 
 
-def far_kernel(place_ref, left_ref, mine_ref, theirs_ref, half_ref, sent_ref, slots_ref):
+def far_kernel(place_ref, left_ref, mine_ref, theirs_ref, spread_ref, half_ref, sent_ref, slots_ref):
     del half_ref
-    mix_half(place_ref, 1, left_ref, mine_ref, theirs_ref, sent_ref, slots_ref)
+    mix_half(place_ref, 1, left_ref, mine_ref, theirs_ref, spread_ref, sent_ref, slots_ref)
 
 
 def update_kernel(got_ref, gate_ref, columns_ref, weight_ref, out_ref, rows_ref, flat_ref):
@@ -212,31 +224,45 @@
     half = row_block // 8 % 2
     place = jnp.stack([row_block * rows, lax.axis_index("ja") * cols, row_block % 2, half, 1 - half]).astype(jnp.int32)
     struct = jax.ShapeDtypeStruct
-    zeros = pl.pallas_call(
-        zeros_kernel,
-        name="zeros",
-        out_shape=struct((width, width), F32),
-        out_specs=VMEM,
-        compiler_params=params,
-    )()
-    normed, masked = pl.pallas_call(
+    zeros, spread = pl.pallas_call(
+        first_kernel,
+        name="first",
+        out_shape=(struct((width, width), F32), struct((192, 256), BF16)),
+        in_specs=[SMEM],
+        out_specs=(VMEM, VMEM),
+        compiler_params=params,
+    )(place)
+    normed, masked, columns = pl.pallas_call(
         norm_kernel,
         name="norm",
-        out_shape=(struct((rows * cols, width), BF16), struct((rows * WIDE, width), BF16)),
-        in_specs=[SMEM, SMEM] + [VMEM] * 4,
-        out_specs=(VMEM, VMEM),
-        compiler_params=params,
-    )(place, token_mask, pair, norm_in_gain.reshape(1, -1), norm_in_bias.reshape(1, -1), zeros)
+        out_shape=(
+            struct((rows * cols, width), BF16),
+            struct((rows * WIDE, width), BF16),
+            struct((2, width, width), F32),
+        ),
+        in_specs=[SMEM, SMEM] + [VMEM] * 6,
+        out_specs=(VMEM, VMEM, VMEM),
+        compiler_params=params,
+    )(
+        place,
+        token_mask,
+        pair,
+        norm_in_gain.reshape(1, -1),
+        norm_in_bias.reshape(1, -1),
+        norm_out_gain.reshape(1, -1),
+        norm_out_bias.reshape(1, -1),
+        zeros,
+    )
     message = struct((128, 2, rows * WIDE), BF16)
-    sent, columns = pl.pallas_call(
+    sent = pl.pallas_call(
         edges_kernel,
         name="edges",
-        out_shape=(message, struct((2, width, width), F32)),
-        in_specs=[VMEM] * 7,
-        out_specs=(VMEM, VMEM),
+        out_shape=message,
+        in_specs=[VMEM] * 5,
+        out_specs=VMEM,
         scratch_shapes=[pltpu.VMEM((3, 256, 128), F32)],
         compiler_params=params,
-    )(masked, left_gate, left_value, right_gate, right_value, norm_out_gain.reshape(1, -1), norm_out_bias.reshape(1, -1))
+    )(masked, left_gate, left_value, right_gate, right_value)
     got = lax.all_to_all(sent, BOTH, 0, 0, axis_index_groups=SHARING)
     scratch = [pltpu.VMEM((3, 256, 128), F32), pltpu.VMEM((384, 128), F32)]
     right = pl.pallas_call(
@@ -264,21 +290,21 @@
         near_kernel,
         name="near",
         out_shape=(message, struct((rows * cols, width), F32)),
-        in_specs=[SMEM] + [VMEM] * 5,
+        in_specs=[SMEM] + [VMEM] * 6,
         out_specs=(VMEM, VMEM),
         scratch_shapes=[pltpu.VMEM((6, 64, 128), F32)],
         compiler_params=params,
-    )(place, left, right, near, normed, output_gate)
+    )(place, left, right, near, spread, normed, output_gate)
     sent = pl.pallas_call(
         far_kernel,
         name="far",
         out_shape=message,
-        in_specs=[SMEM] + [VMEM] * 4,
+        in_specs=[SMEM] + [VMEM] * 5,
         out_specs=VMEM,
         scratch_shapes=[pltpu.VMEM((6, 64, 128), F32)],
-        input_output_aliases={4: 0},
-        compiler_params=params,
-    )(place, left, far, both, sent)
+        input_output_aliases={5: 0},
+        compiler_params=params,
+    )(place, left, far, both, spread, sent)
     got = lax.all_to_all(sent, BOTH, 0, 0, axis_index_groups=SHARING)
     return pl.pallas_call(
         update_kernel,

time: 68.9 us -> 68.8 us (level)
  local copies, waits for them, and re-layouts: 1.51 us -> 0.81 us
    unnamed x24, local copies, waits for them, and re-layouts: 1.42 us -> 0.72 us
where the time goes in v8:
time: 68.8 us; the launch traced here: 68.3 us
  blocking collectives  49 us (71%)
  starting transfers between devices  12.2 us (18%)
  Pallas kernels  6.05 us (9%)
  local copies, waits for them, and re-layouts  0.81 us (1%)
    all_to_all x2, blocking collectives, shards(): got = lax.all_to_all(sent, BOTH, 0, 0, axis_index_groups=SHARING)  49 us
    ppermute x1, starting transfers between devices, shards(): far = lax.ppermute(right, BOTH, HALF_FLIP)  4.42 us
    ppermute x1, starting transfers between devices, shards(): near = lax.ppermute(right, BOTH, CORE_FLIP)  4.31 us
    ppermute x1, starting transfers between devices, shards(): both = lax.ppermute(far, BOTH, CORE_FLIP)  3.52 us
  transfers between devices with their start and end apart: 3, of which 0 were waited for; matrix products, arithmetic and copies ran while one was open for 0% of the time, Pallas kernels for 2%

profile of v8, /device:TPU:1, one launch (start us, length us, event | category | flops | bytes accessed | tf_op | source)
XLA Modules:
  0.0 68.3 jit_solution(17799266257756997730)
XLA Ops:
  0.0 0.1 stack.23.place_ref
  0.1 0.6 first.1
  0.7 0.0 copy-start.11
  0.7 0.0 copy-start.7
  0.7 0.0 copy-start.8
  0.7 0.0 copy-start.9
  0.7 0.0 copy-start.10
  0.7 0.2 copy-done
  0.9 0.5 copy-done.11
  1.3 0.0 copy-done.7
  1.4 0.0 copy-done.8
  1.4 0.0 copy-done.9
  1.4 0.0 copy-done.10
  1.4 0.0 copy-start.4
  1.4 0.0 copy-start.5
  1.4 0.8 %norm.1 = (bf16[288,128]{1,0:T(8,128)(2,1)S(1)}, bf16[384,128]{1,0:T(8,128)(2,1)S(1)}, f32[2,128,128]{2,1,0:T(8,128)S(1)}) custom-call(s32[5]{0:T(128)S(1)} %stack.23.place_ref, s32[384]{0:T(512)S(1)} %copy-done.7, bf16[12,24,128]{2,1,0:T(8,128)(2,1)S(1)} %copy-done, f32[1,128]{1,0:T(1,128)S(1)} %bitcast.9, f32[1,128]{1,0:T(1,128)S(1)} %bitcast.10, ...), custom_call_target="tpu_custom_call" | custom-call | tf_op jit(solution)/shard_map/norm/pallas_call | solution.py:235
  2.3 0.4 edges.1
  2.7 30.4 %all_to_all.10.got_ref = bf16[128,2,384]{2,1,0:T(2,128)(2,1)S(1)} all-to-all(bf16[128,2,384]{2,1,0:T(2,128)(2,1)S(1)} %edges.1), channel_id=1, replica_groups={{0,1,2,3,4,5,6,7,8,9,10,11,12,13,14,15,32,33,34,35,36,37,38,39,40,41,42..., dimensions={0} | all-to-all | bytes 393216 | tf_op jit(solution)/shard_map/all_to_all | solution.py:266
  33.2 0.4 right.1.mine_ref
  33.6 0.0 copy-start.6
  33.6 4.4 %collective-permute-start = (bf16[96,384]{1,0:T(8,128)(2,1)S(1)}, bf16[96,384]{1,0:T(8,128)(2,1)S(1)}, u32[]{:S(2)}, u32[]{:S(2)}) collective-permute-start(bf16[96,384]{1,0:T(8,128)(2,1)S(1)} %right.1.mine_ref), channel_id=1, source_target_pairs={{0,224},{1,225},{2,226},{3,227},{4,228},{5,229},{6,230},{7,231},{8... | collective-permute-start | bytes 221192 | tf_op jit(solution)/shard_map/ppermute | solution.py:287
  38.0 4.3 %collective-permute-start.2 = (bf16[96,384]{1,0:T(8,128)(2,1)S(1)}, bf16[96,384]{1,0:T(8,128)(2,1)S(1)}, u32[]{:S(2)}, u32[]{:S(2)}) collective-permute-start(bf16[96,384]{1,0:T(8,128)(2,1)S(1)} %right.1.mine_ref), channel_id=1, source_target_pairs={{0,16},{1,17},{2,18},{3,19},{4,20},{5,21},{6,22},{7,23},{8,24},{9,... | collective-permute-start | bytes 221192 | tf_op jit(solution)/shard_map/ppermute | solution.py:286
  42.4 0.0 collective-permute-done.mine_ref
  42.4 3.5 %collective-permute-start.1 = (bf16[96,384]{1,0:T(8,128)(2,1)S(1)}, bf16[96,384]{1,0:T(8,128)(2,1)S(1)}, u32[]{:S(2)}, u32[]{:S(2)}) collective-permute-start(bf16[96,384]{1,0:T(8,128)(2,1)S(1)} %collective-permute-done.mine_ref), channel_id=1, source_target_pairs={{0,16},{1,17},{2,18},{3,19},{4,20},{5,21},{6,22},{7,23},{8,24},{9,... | collective-permute-start | bytes 221192 | tf_op jit(solution)/shard_map/ppermute | solution.py:288
  45.9 0.4 left.1.left_ref
  46.3 0.0 collective-permute-done.2.theirs_ref
  46.3 1.2 %near.1 = (bf16[128,2,384]{2,1,0:T(2,128)(2,1)S(1)}, f32[288,128]{1,0:T(8,128)S(1)}) custom-call(s32[5]{0:T(128)S(1)} %stack.23.place_ref, bf16[96,384]{1,0:T(8,128)(2,1)S(1)} %left.1.left_ref, bf16[96,384]{1,0:T(8,128)(2,1)S(1)} %right.1.mine_ref, bf16[96,384]{1,0:T(8,128)(2,1)S(1)} %collective-permute-done.2.theirs_ref, ...), custom_call_target="tpu_custom_call" | custom-call | tf_op jit(solution)/shard_map/near/pallas_call | solution.py:289
  47.5 0.0 collective-permute-done.1.theirs_ref
  47.5 1.2 %far.1 = bf16[128,2,384]{2,1,0:T(2,128)(2,1)S(1)} custom-call(s32[5]{0:T(128)S(1)} %stack.23.place_ref, bf16[96,384]{1,0:T(8,128)(2,1)S(1)} %left.1.left_ref, bf16[96,384]{1,0:T(8,128)(2,1)S(1)} %collective-permute-done.mine_ref, bf16[96,384]{1,0:T(8,128)(2,1)S(1)} %collective-permute-done.1.theirs_ref, ...), custom_call_target="tpu_custom_call", output_to_operand_aliasing={{}: (5, {})} | custom-call | tf_op jit(solution)/shard_map/far/pallas_call | solution.py:298
  48.7 0.0 copy-start.1
  48.7 18.6 %all_to_all.11.got_ref = bf16[128,2,384]{2,1,0:T(2,128)(2,1)S(1)} all-to-all(bf16[128,2,384]{2,1,0:T(2,128)(2,1)S(1)} %far.1), channel_id=1, replica_groups={{0,1,2,3,4,5,6,7,8,9,10,11,12,13,14,15,32,33,34,35,36,37,38,39,40,41,42..., dimensions={0} | all-to-all | bytes 393216 | tf_op jit(solution)/shard_map/all_to_all | solution.py:308
  67.2 1.1 %update.1 = bf16[12,24,128]{2,1,0:T(8,128)(2,1)} custom-call(bf16[128,2,384]{2,1,0:T(2,128)(2,1)S(1)} %all_to_all.11.got_ref, f32[288,128]{1,0:T(8,128)S(1)} %get-tuple-element.17.gate_ref, f32[2,128,128]{2,1,0:T(8,128)S(1)} %get-tuple-element.18.columns_ref, bf16[128,128]{1,0:T(8,128)(2,1)S(1)} %copy-done.1), custom_call_target="tpu_custom_call" | custom-call | tf_op jit(solution)/shard_map/update/pallas_call | solution.py:309
  (9 shorter events, 0.0 us)
Async XLA Ops:
  0.0 0.9 %copy-start = (bf16[12,24,128]{2,1,0:T(8,128)(2,1)S(1)}, bf16[12,24,128]{2,1,0:T(8,128)(2,1)}, u32[]{:S(2)}) copy-start(bf16[12,24,128]{2,1,0:T(8,128)(2,1)} %pair_ref.1) | copy-start | bytes 221188
  0.7 0.7 copy-start.11
  0.7 0.7 %copy-start.7 = (s32[384]{0:T(512)S(1)}, s32[384]{0:T(512)}, u32[]{:S(2)}) copy-start(s32[384]{0:T(512)} %mask_ref.1) | copy-start | bytes 4612
  0.7 0.7 %copy-start.8 = (f32[128]{0:T(128)S(1)}, f32[128]{0:T(128)}, u32[]{:S(2)}) copy-start(f32[128]{0:T(128)} %param.14) | copy-start | bytes 1540
  0.7 0.7 copy-start.9
  0.7 0.7 copy-start.10
  1.4 0.8 %copy-start.2 = (bf16[128,128]{1,0:T(8,128)(2,1)S(1)}, bf16[128,128]{1,0:T(8,128)(2,1)}, u32[]{:S(2)}) copy-start(bf16[128,128]{1,0:T(8,128)(2,1)} %lg_ref.1) | copy-start | bytes 98308
  1.4 0.9 %copy-start.3 = (bf16[128,128]{1,0:T(8,128)(2,1)S(1)}, bf16[128,128]{1,0:T(8,128)(2,1)}, u32[]{:S(2)}) copy-start(bf16[128,128]{1,0:T(8,128)(2,1)} %lv_ref.1) | copy-start | bytes 98308
  1.4 0.9 %copy-start.4 = (bf16[128,128]{1,0:T(8,128)(2,1)S(1)}, bf16[128,128]{1,0:T(8,128)(2,1)}, u32[]{:S(2)}) copy-start(bf16[128,128]{1,0:T(8,128)(2,1)} %rg_ref.1) | copy-start | bytes 98308
  1.4 0.9 %copy-start.5 = (bf16[128,128]{1,0:T(8,128)(2,1)S(1)}, bf16[128,128]{1,0:T(8,128)(2,1)}, u32[]{:S(2)}) copy-start(bf16[128,128]{1,0:T(8,128)(2,1)} %rv_ref.1) | copy-start | bytes 98308
  33.6 12.7 %copy-start.6 = (bf16[128,128]{1,0:T(8,128)(2,1)S(1)}, bf16[128,128]{1,0:T(8,128)(2,1)}, u32[]{:S(2)}) copy-start(bf16[128,128]{1,0:T(8,128)(2,1)} %og_ref.1) | copy-start | bytes 98308
  33.6 8.8 %collective-permute-start = (bf16[96,384]{1,0:T(8,128)(2,1)S(1)}, bf16[96,384]{1,0:T(8,128)(2,1)S(1)}, u32[]{:S(2)}, u32[]{:S(2)}) collective-permute-start(bf16[96,384]{1,0:T(8,128)(2,1)S(1)} %right.1.mine_ref), channel_id=1, source_target_pairs={{0,224},{1,225},{2,226},{3,227},{4,228},{5,229},{6,230},{7,231},{8... | collective-permute-start | bytes 221192 | tf_op jit(solution)/shard_map/ppermute | solution.py:287
  38.0 8.3 %collective-permute-start.2 = (bf16[96,384]{1,0:T(8,128)(2,1)S(1)}, bf16[96,384]{1,0:T(8,128)(2,1)S(1)}, u32[]{:S(2)}, u32[]{:S(2)}) collective-permute-start(bf16[96,384]{1,0:T(8,128)(2,1)S(1)} %right.1.mine_ref), channel_id=1, source_target_pairs={{0,16},{1,17},{2,18},{3,19},{4,20},{5,21},{6,22},{7,23},{8,24},{9,... | collective-permute-start | bytes 221192 | tf_op jit(solution)/shard_map/ppermute | solution.py:286
  42.4 5.1 %collective-permute-start.1 = (bf16[96,384]{1,0:T(8,128)(2,1)S(1)}, bf16[96,384]{1,0:T(8,128)(2,1)S(1)}, u32[]{:S(2)}, u32[]{:S(2)}) collective-permute-start(bf16[96,384]{1,0:T(8,128)(2,1)S(1)} %collective-permute-done.mine_ref), channel_id=1, source_target_pairs={{0,16},{1,17},{2,18},{3,19},{4,20},{5,21},{6,22},{7,23},{8,24},{9,... | collective-permute-start | bytes 221192 | tf_op jit(solution)/shard_map/ppermute | solution.py:288
  48.7 18.6 %copy-start.1 = (bf16[128,128]{1,0:T(8,128)(2,1)S(1)}, bf16[128,128]{1,0:T(8,128)(2,1)}, u32[]{:S(2)}) copy-start(bf16[128,128]{1,0:T(8,128)(2,1)} %weight_ref.1) | copy-start | bytes 98308

commit v9 on v8

--- a/solution.py
+++ b/solution.py
@@ -12,6 +12,7 @@
 BF16 = jnp.bfloat16
 VMEM = pl.BlockSpec(memory_space=pltpu.VMEM)
 SMEM = pl.BlockSpec(memory_space=pltpu.SMEM)
+HBM = pl.BlockSpec(memory_space=pltpu.HBM)
 
 
 def device(xl, y, core, xh, z):
@@ -44,8 +45,50 @@
     return lax.dot_general(a, b, (((da,), (db,)), ((), ())), preferred_element_type=F32)
 
 
-def first_kernel(place_ref, zeros_ref, spread_ref):
-    zeros_ref[...] = jnp.zeros_like(zeros_ref)
+def edges_kernel(
+    place_ref,
+    pair_hbm,
+    mask_hbm,
+    gain_hbm,
+    bias_hbm,
+    out_gain_hbm,
+    out_bias_hbm,
+    lg_hbm,
+    lv_hbm,
+    rg_hbm,
+    rv_hbm,
+    sent_ref,
+    normed_ref,
+    columns_ref,
+    spread_ref,
+    pair_ref,
+    mask_ref,
+    gain_ref,
+    bias_ref,
+    out_gain_ref,
+    out_bias_ref,
+    lg_ref,
+    lv_ref,
+    rg_ref,
+    rv_ref,
+    rows_ref,
+    arrived,
+):
+    fetches = [
+        (pair_hbm, pair_ref),
+        (mask_hbm, mask_ref),
+        (gain_hbm, gain_ref),
+        (bias_hbm, bias_ref),
+        (lg_hbm, lg_ref),
+        (lv_hbm, lv_ref),
+        (rg_hbm, rg_ref),
+        (rv_hbm, rv_ref),
+        (out_gain_hbm, out_gain_ref),
+        (out_bias_hbm, out_bias_ref),
+    ]
+    copies = [pltpu.make_async_copy(source, to, arrived.at[n]) for n, (source, to) in enumerate(fetches)]
+    for copy in copies:
+        copy.start()
     row = iota(spread_ref.shape, 0)
     side = jnp.where(row >= 96, 1, 0)
     row = row - 96 * side
@@ -53,30 +96,16 @@
     core = place_ref[2]
     to_lane = row + 20 * run + 16 * jnp.where(side == 0, core, 1 - core)
     spread_ref[...] = jnp.where(iota(spread_ref.shape, 1) == to_lane, 1.0, 0.0).astype(BF16)
-
-
-def norm_kernel(
-    place_ref,
-    mask_ref,
-    pair_ref,
-    gain_ref,
-    bias_ref,
-    out_gain_ref,
-    out_bias_ref,
-    zeros_ref,
-    normed_ref,
-    masked_ref,
-    columns_ref,
-):
-    rows, cols, width = pair_ref.shape
-    x = pair_ref[...].astype(F32).reshape(rows * cols, width)
+    for copy in copies[:4]:
+        copy.wait()
+    width = lg_ref.shape[0]
+    rows, cols = 12, 24
+    x = pair_ref[...].astype(F32)
     mean = jnp.mean(x, axis=-1, keepdims=True)
     centered = x - mean
     variance = jnp.mean(centered * centered, axis=-1, keepdims=True)
     normed = centered * lax.rsqrt(variance + EPS) * gain_ref[...] + bias_ref[...]
     normed_ref[...] = normed.astype(BF16)
-    columns_ref[0] = jnp.transpose(jnp.broadcast_to(out_gain_ref[...], (width, width)))
-    columns_ref[1] = jnp.transpose(jnp.broadcast_to(out_bias_ref[...], (width, width)))
     place = iota((cols, width), 0)
     col_valid = jnp.zeros((cols, width), F32)
     for k in range(cols):
@@ -85,13 +114,10 @@
     for i in [3 * ii + iq for iq in range(3) for ii in range(4)]:
         row_valid = mask_ref[place_ref[0] + i].astype(F32)
         parts.append(normed[i * cols : (i + 1) * cols] * (col_valid * row_valid))
-        parts.append(zeros_ref[0 : WIDE - cols])
-    masked_ref[...] = jnp.concatenate(parts, axis=0).astype(BF16)
-
-
-def edges_kernel(masked_ref, lg_ref, lv_ref, rg_ref, rv_ref, sent_ref, rows_ref):
-    width = lg_ref.shape[0]
-    masked = masked_ref[...]
+        parts.append(jnp.zeros((WIDE - cols, width), F32))
+    masked = jnp.concatenate(parts, axis=0).astype(BF16)
+    for copy in copies[4:]:
+        copy.wait()
     left = sigmoid(contract(lg_ref[...], masked, 0, 1)) * contract(lv_ref[...], masked, 0, 1)
     right = sigmoid(contract(rg_ref[...], masked, 0, 1)) * contract(rv_ref[...], masked, 0, 1)
     for t in range(3):
@@ -99,6 +125,8 @@
         rows_ref[t, pl.ds(0, width, stride=2), :] = right[:, lanes]
         rows_ref[t, pl.ds(1, width, stride=2), :] = left[:, lanes]
         sent_ref[:, :, lanes] = rows_ref[t].astype(BF16).reshape(width, 2, 128)
+    columns_ref[0] = jnp.transpose(jnp.broadcast_to(out_gain_ref[...], (width, width)))
+    columns_ref[1] = jnp.transpose(jnp.broadcast_to(out_bias_ref[...], (width, width)))
 
 
 def swap_blocks(blocks, lane):
@@ -133,14 +161,6 @@
             dense_ref[v, pl.ds(ii * 3 + iq, 8, stride=12), :] = dense[v]
     for v in range(3):
         right_ref[:, v * 128 : (v + 1) * 128] = dense_ref[v].astype(BF16)
-
-
-def left_kernel(got_ref, left_ref, rows_ref, quads_ref):
-    spread = spread_side(1, got_ref, rows_ref, quads_ref)
-    for iq in range(3):
-        for v in range(3):
-            block = jnp.concatenate([spread[iq, ii][v] for ii in range(4)], axis=0)
-            left_ref[iq * 32 : (iq + 1) * 32, v * 128 : (v + 1) * 128] = block.astype(BF16)
 
 
 def mix_half(place_ref, other, left_ref, mine_ref, theirs_ref, spread_ref, sent_ref, slots_ref):
@@ -166,7 +186,7 @@
 
 def near_kernel(
     place_ref,
-    left_ref,
+    got_ref,
     mine_ref,
     theirs_ref,
     spread_ref,
@@ -174,10 +194,18 @@
     og_ref,
     sent_ref,
     gate_ref,
+    left_ref,
     slots_ref,
+    rows_ref,
+    quads_ref,
 ):
+    blocks = spread_side(1, got_ref, rows_ref, quads_ref)
+    for iq in range(3):
+        for v in range(3):
+            block = jnp.concatenate([blocks[iq, ii][v] for ii in range(4)], axis=0)
+            left_ref[iq * 32 : (iq + 1) * 32, v * 128 : (v + 1) * 128] = block.astype(BF16)
+    gate_ref[...] = sigmoid(contract(normed_ref[...], og_ref[...], 1, 0))
     mix_half(place_ref, 0, left_ref, mine_ref, theirs_ref, spread_ref, sent_ref, slots_ref)
-    gate_ref[...] = sigmoid(contract(normed_ref[...], og_ref[...], 1, 0))
 
 
 def far_kernel(place_ref, left_ref, mine_ref, theirs_ref, spread_ref, half_ref, sent_ref, slots_ref):
@@ -224,45 +252,26 @@
     half = row_block // 8 % 2
     place = jnp.stack([row_block * rows, lax.axis_index("ja") * cols, row_block % 2, half, 1 - half]).astype(jnp.int32)
     struct = jax.ShapeDtypeStruct
-    zeros, spread = pl.pallas_call(
-        first_kernel,
-        name="first",
-        out_shape=(struct((width, width), F32), struct((192, 256), BF16)),
-        in_specs=[SMEM],
-        out_specs=(VMEM, VMEM),
-        compiler_params=params,
-    )(place)
-    normed, masked, columns = pl.pallas_call(
-        norm_kernel,
-        name="norm",
-        out_shape=(
-            struct((rows * cols, width), BF16),
-            struct((rows * WIDE, width), BF16),
-            struct((2, width, width), F32),
-        ),
-        in_specs=[SMEM, SMEM] + [VMEM] * 6,
-        out_specs=(VMEM, VMEM, VMEM),
-        compiler_params=params,
-    )(
-        place,
-        token_mask,
-        pair,
-        norm_in_gain.reshape(1, -1),
-        norm_in_bias.reshape(1, -1),
-        norm_out_gain.reshape(1, -1),
-        norm_out_bias.reshape(1, -1),
-        zeros,
-    )
-    message = struct((128, 2, rows * WIDE), BF16)
-    sent = pl.pallas_call(
+    message = struct((width, 2, rows * WIDE), BF16)
+    arrays = [pair.reshape(rows * cols, width), token_mask]
+    arrays += [v.reshape(1, -1) for v in (norm_in_gain, norm_in_bias, norm_out_gain, norm_out_bias)]
+    arrays += [left_gate, left_value, right_gate, right_value]
+    fetched = [pltpu.VMEM(array.shape, array.dtype) for array in arrays]
+    fetched[1] = pltpu.SMEM(token_mask.shape, token_mask.dtype)
+    sent, normed, columns, spread = pl.pallas_call(
         edges_kernel,
         name="edges",
-        out_shape=message,
-        in_specs=[VMEM] * 5,
-        out_specs=VMEM,
-        scratch_shapes=[pltpu.VMEM((3, 256, 128), F32)],
-        compiler_params=params,
-    )(masked, left_gate, left_value, right_gate, right_value)
+        out_shape=(
+            message,
+            struct((rows * cols, width), BF16),
+            struct((2, width, width), F32),
+            struct((192, 256), BF16),
+        ),
+        in_specs=[SMEM] + [HBM] * 10,
+        out_specs=(VMEM,) * 4,
+        scratch_shapes=fetched + [pltpu.VMEM((3, 256, 128), F32), pltpu.SemaphoreType.DMA((10,))],
+        compiler_params=params,
+    )(place, *[pltpu.with_memory_space_constraint(array, pltpu.HBM) for array in arrays])
     got = lax.all_to_all(sent, BOTH, 0, 0, axis_index_groups=SHARING)
     scratch = [pltpu.VMEM((3, 256, 128), F32), pltpu.VMEM((384, 128), F32)]
     right = pl.pallas_call(
@@ -274,27 +283,18 @@
         scratch_shapes=scratch + [pltpu.VMEM((3, 96, 128), F32)],
         compiler_params=params,
     )(got)
-    left = pl.pallas_call(
-        left_kernel,
-        name="left",
-        out_shape=struct((96, 384), BF16),
-        in_specs=[VMEM],
-        out_specs=VMEM,
-        scratch_shapes=scratch,
-        compiler_params=params,
-    )(got)
     near = lax.ppermute(right, BOTH, CORE_FLIP)
     far = lax.ppermute(right, BOTH, HALF_FLIP)
     both = lax.ppermute(far, BOTH, CORE_FLIP)
-    sent, gate = pl.pallas_call(
+    sent, gate, left = pl.pallas_call(
         near_kernel,
         name="near",
-        out_shape=(message, struct((rows * cols, width), F32)),
+        out_shape=(message, struct((rows * cols, width), F32), struct((96, 384), BF16)),
         in_specs=[SMEM] + [VMEM] * 6,
-        out_specs=(VMEM, VMEM),
-        scratch_shapes=[pltpu.VMEM((6, 64, 128), F32)],
-        compiler_params=params,
-    )(place, left, right, near, spread, normed, output_gate)
+        out_specs=(VMEM,) * 3,
+        scratch_shapes=[pltpu.VMEM((6, 64, 128), F32)] + scratch,
+        compiler_params=params,
+    )(place, got, right, near, spread, normed, output_gate)
     sent = pl.pallas_call(
         far_kernel,
         name="far",

time: 68.8 us -> 68.1 us (0.990)
  local copies, waits for them, and re-layouts: 0.81 us -> 0.09 us
    unnamed x24 -> x4, local copies, waits for them, and re-layouts: 0.72 us -> 0.01 us
    pallas_call x4 -> x1, Pallas kernels: 2.22 us -> 2.18 us  [shards(): pl.pallas_call(edges_kernel, name='edges', out_shape=(message, struct((ro...]
where the time goes in v9:
time: 68.1 us; the launch traced here: 67.7 us
  blocking collectives  49 us (72%)
  starting transfers between devices  12.2 us (18%)
  Pallas kernels  6.28 us (9%)
    all_to_all x2, blocking collectives, shards(): got = lax.all_to_all(sent, BOTH, 0, 0, axis_index_groups=SHARING)  49 us
    ppermute x1, starting transfers between devices, shards(): far = lax.ppermute(right, BOTH, HALF_FLIP)  4.42 us
    ppermute x1, starting transfers between devices, shards(): near = lax.ppermute(right, BOTH, CORE_FLIP)  4.31 us
    ppermute x1, starting transfers between devices, shards(): both = lax.ppermute(far, BOTH, CORE_FLIP)  3.52 us
    pallas_call x1, Pallas kernels, shards(): pl.pallas_call(edges_kernel, name='edges', out_shape=(message, struct((ro...  2.18 us
    pallas_call x1, Pallas kernels, shards(): pl.pallas_call(near_kernel, name='near', out_shape=(message, struct((rows...  1.43 us
  transfers between devices with their start and end apart: 3, of which 0 were waited for; matrix products, arithmetic and copies ran while one was open for 0% of the time, Pallas kernels for 2%

profile of v9, /device:TPU:1, one launch (start us, length us, event | category | flops | bytes accessed | tf_op | source)
XLA Modules:
  0.0 67.7 jit_solution(5684845906232943187)
XLA Ops:
  0.0 0.1 stack.23.place_ref
  0.1 2.2 %edges.1 = (bf16[128,2,384]{2,1,0:T(2,128)(2,1)S(1)}, bf16[288,128]{1,0:T(8,128)(2,1)S(1)}, f32[2,128,128]{2,1,0:T(8,128)S(1)}, bf16[192,256]{1,0:T(8,128)(2,1)S(1)}) custom-call(s32[5]{0:T(128)S(1)} %stack.23.place_ref, bf16[288,128]{1,0:T(8,128)(2,1)} %bitcast.10, s32[384]{0:T(512)} %mask_hbm.1, f32[1,128]{1,0:T(1,128)} %bitcast.11, f32[1,128]{1,0:T(1,128)} %bitcast.12, ...), custom_call_target="tpu_custom_call" | custom-call | tf_op jit(solution)/shard_map/edges/pallas_call | solution.py:261
  2.3 30.4 %all_to_all.10.got_ref = bf16[128,2,384]{2,1,0:T(2,128)(2,1)S(1)} all-to-all(bf16[128,2,384]{2,1,0:T(2,128)(2,1)S(1)} %get-tuple-element.12), channel_id=1, replica_groups={{0,1,2,3,4,5,6,7,8,9,10,11,12,13,14,15,32,33,34,35,36,37,38,39,40,41,42..., dimensions={0} | all-to-all | bytes 393216 | tf_op jit(solution)/shard_map/all_to_all | solution.py:275
  32.7 0.0 copy-start
  32.7 0.4 right.1.mine_ref
  33.1 4.4 %collective-permute-start.1 = (bf16[96,384]{1,0:T(8,128)(2,1)S(1)}, bf16[96,384]{1,0:T(8,128)(2,1)S(1)}, u32[]{:S(2)}, u32[]{:S(2)}) collective-permute-start(bf16[96,384]{1,0:T(8,128)(2,1)S(1)} %right.1.mine_ref), channel_id=1, source_target_pairs={{0,224},{1,225},{2,226},{3,227},{4,228},{5,229},{6,230},{7,231},{8... | collective-permute-start | bytes 221192 | tf_op jit(solution)/shard_map/ppermute | solution.py:287
  37.6 4.3 %collective-permute-start = (bf16[96,384]{1,0:T(8,128)(2,1)S(1)}, bf16[96,384]{1,0:T(8,128)(2,1)S(1)}, u32[]{:S(2)}, u32[]{:S(2)}) collective-permute-start(bf16[96,384]{1,0:T(8,128)(2,1)S(1)} %right.1.mine_ref), channel_id=1, source_target_pairs={{0,16},{1,17},{2,18},{3,19},{4,20},{5,21},{6,22},{7,23},{8,24},{9,... | collective-permute-start | bytes 221192 | tf_op jit(solution)/shard_map/ppermute | solution.py:286
  41.9 0.0 collective-permute-done.1.mine_ref
  41.9 3.5 %collective-permute-start.2 = (bf16[96,384]{1,0:T(8,128)(2,1)S(1)}, bf16[96,384]{1,0:T(8,128)(2,1)S(1)}, u32[]{:S(2)}, u32[]{:S(2)}) collective-permute-start(bf16[96,384]{1,0:T(8,128)(2,1)S(1)} %collective-permute-done.1.mine_ref), channel_id=1, source_target_pairs={{0,16},{1,17},{2,18},{3,19},{4,20},{5,21},{6,22},{7,23},{8,24},{9,... | collective-permute-start | bytes 221192 | tf_op jit(solution)/shard_map/ppermute | solution.py:288
  45.4 0.0 collective-permute-done.theirs_ref
  45.4 0.0 copy-done
  45.5 1.4 %near.1 = (bf16[128,2,384]{2,1,0:T(2,128)(2,1)S(1)}, f32[288,128]{1,0:T(8,128)S(1)}, bf16[96,384]{1,0:T(8,128)(2,1)S(1)}) custom-call(s32[5]{0:T(128)S(1)} %stack.23.place_ref, bf16[128,2,384]{2,1,0:T(2,128)(2,1)S(1)} %all_to_all.10.got_ref, bf16[96,384]{1,0:T(8,128)(2,1)S(1)} %right.1.mine_ref, bf16[96,384]{1,0:T(8,128)(2,1)S(1)} %collective-permute-done.theirs_ref, ...), custom_call_target="tpu_custom_call" | custom-call | tf_op jit(solution)/shard_map/near/pallas_call | solution.py:289
  46.9 0.0 collective-permute-done.2.theirs_ref
  46.9 1.1 %far.1 = bf16[128,2,384]{2,1,0:T(2,128)(2,1)S(1)} custom-call(s32[5]{0:T(128)S(1)} %stack.23.place_ref, bf16[96,384]{1,0:T(8,128)(2,1)S(1)} %get-tuple-element.15.left_ref, bf16[96,384]{1,0:T(8,128)(2,1)S(1)} %collective-permute-done.1.mine_ref, bf16[96,384]{1,0:T(8,128)(2,1)S(1)} %collective-permute-done.2.theirs_ref, ...), custom_call_target="tpu_custom_call", output_to_operand_aliasing={{}: (5, {})} | custom-call | tf_op jit(solution)/shard_map/far/pallas_call | solution.py:298
  48.1 0.0 copy-start.1
  48.1 18.6 %all_to_all.11.got_ref = bf16[128,2,384]{2,1,0:T(2,128)(2,1)S(1)} all-to-all(bf16[128,2,384]{2,1,0:T(2,128)(2,1)S(1)} %far.1), channel_id=1, replica_groups={{0,1,2,3,4,5,6,7,8,9,10,11,12,13,14,15,32,33,34,35,36,37,38,39,40,41,42..., dimensions={0} | all-to-all | bytes 393216 | tf_op jit(solution)/shard_map/all_to_all | solution.py:308
  66.6 0.0 copy-done.1
  66.6 1.1 %update.1 = bf16[12,24,128]{2,1,0:T(8,128)(2,1)} custom-call(bf16[128,2,384]{2,1,0:T(2,128)(2,1)S(1)} %all_to_all.11.got_ref, f32[288,128]{1,0:T(8,128)S(1)} %get-tuple-element.17.gate_ref, f32[2,128,128]{2,1,0:T(8,128)S(1)} %get-tuple-element.18.columns_ref, bf16[128,128]{1,0:T(8,128)(2,1)S(1)} %copy-done.1), custom_call_target="tpu_custom_call" | custom-call | tf_op jit(solution)/shard_map/update/pallas_call | solution.py:309
Async XLA Ops:
  32.7 12.7 %copy-start = (bf16[128,128]{1,0:T(8,128)(2,1)S(1)}, bf16[128,128]{1,0:T(8,128)(2,1)}, u32[]{:S(2)}) copy-start(bf16[128,128]{1,0:T(8,128)(2,1)} %og_ref.1) | copy-start | bytes 98308
  33.1 8.8 %collective-permute-start.1 = (bf16[96,384]{1,0:T(8,128)(2,1)S(1)}, bf16[96,384]{1,0:T(8,128)(2,1)S(1)}, u32[]{:S(2)}, u32[]{:S(2)}) collective-permute-start(bf16[96,384]{1,0:T(8,128)(2,1)S(1)} %right.1.mine_ref), channel_id=1, source_target_pairs={{0,224},{1,225},{2,226},{3,227},{4,228},{5,229},{6,230},{7,231},{8... | collective-permute-start | bytes 221192 | tf_op jit(solution)/shard_map/ppermute | solution.py:287
  37.6 7.9 %collective-permute-start = (bf16[96,384]{1,0:T(8,128)(2,1)S(1)}, bf16[96,384]{1,0:T(8,128)(2,1)S(1)}, u32[]{:S(2)}, u32[]{:S(2)}) collective-permute-start(bf16[96,384]{1,0:T(8,128)(2,1)S(1)} %right.1.mine_ref), channel_id=1, source_target_pairs={{0,16},{1,17},{2,18},{3,19},{4,20},{5,21},{6,22},{7,23},{8,24},{9,... | collective-permute-start | bytes 221192 | tf_op jit(solution)/shard_map/ppermute | solution.py:286
  41.9 5.0 %collective-permute-start.2 = (bf16[96,384]{1,0:T(8,128)(2,1)S(1)}, bf16[96,384]{1,0:T(8,128)(2,1)S(1)}, u32[]{:S(2)}, u32[]{:S(2)}) collective-permute-start(bf16[96,384]{1,0:T(8,128)(2,1)S(1)} %collective-permute-done.1.mine_ref), channel_id=1, source_target_pairs={{0,16},{1,17},{2,18},{3,19},{4,20},{5,21},{6,22},{7,23},{8,24},{9,... | collective-permute-start | bytes 221192 | tf_op jit(solution)/shard_map/ppermute | solution.py:288
  48.1 18.6 %copy-start.1 = (bf16[128,128]{1,0:T(8,128)(2,1)S(1)}, bf16[128,128]{1,0:T(8,128)(2,1)}, u32[]{:S(2)}) copy-start(bf16[128,128]{1,0:T(8,128)(2,1)} %weight_ref.1) | copy-start | bytes 98308

commit v10 on v9

--- a/solution.py
+++ b/solution.py
@@ -163,7 +163,7 @@
         right_ref[:, v * 128 : (v + 1) * 128] = dense_ref[v].astype(BF16)
 
 
-def mix_half(place_ref, other, left_ref, mine_ref, theirs_ref, spread_ref, sent_ref, slots_ref):
+def mix_half(place_ref, other, left_ref, mine_ref, theirs_ref, spread_ref, rows_ref):
     lane = iota((8, 128), 1)
     half = place_ref[3 + other]
     mixed = contract(left_ref[...], jnp.concatenate([mine_ref[...], theirs_ref[...]], axis=0), 1, 1)
@@ -176,12 +176,8 @@
                 at = part * 96 + iq * 32
                 blocks = [parts[at + ii * 8 : at + (ii + 1) * 8, xl * 128 : (xl + 1) * 128] for ii in range(4)]
                 for m, block in enumerate(swap_blocks(blocks, lane)):
-                    slot = (m + half * (3 - 2 * m)) * 2 + part
-                    slots_ref[xl * 3 + iq, pl.ds(pl.multiple_of(slot * 8, 8), 8), :] = block
-            for g in range(8):
-                rows = slots_ref[xl * 3 + iq, pl.ds(g, 8, stride=8), :]
-                to = g * 16 + xl * 8 + half * 4
-                sent_ref[pl.ds(to, 4), :, iq * 128 : (iq + 1) * 128] = rows.astype(BF16).reshape(4, 2, 128)
+                    to = (xl * 8 + m + half * (7 - 2 * m)) * 2 + part
+                    rows_ref[iq, pl.ds(to, 8, stride=32), :] = block
 
 
 def near_kernel(
@@ -192,25 +188,26 @@
     spread_ref,
     normed_ref,
     og_ref,
-    sent_ref,
+    rows_ref,
     gate_ref,
     left_ref,
-    slots_ref,
-    rows_ref,
+    got_rows_ref,
     quads_ref,
 ):
-    blocks = spread_side(1, got_ref, rows_ref, quads_ref)
+    blocks = spread_side(1, got_ref, got_rows_ref, quads_ref)
     for iq in range(3):
         for v in range(3):
             block = jnp.concatenate([blocks[iq, ii][v] for ii in range(4)], axis=0)
             left_ref[iq * 32 : (iq + 1) * 32, v * 128 : (v + 1) * 128] = block.astype(BF16)
     gate_ref[...] = sigmoid(contract(normed_ref[...], og_ref[...], 1, 0))
-    mix_half(place_ref, 0, left_ref, mine_ref, theirs_ref, spread_ref, sent_ref, slots_ref)
-
-
-def far_kernel(place_ref, left_ref, mine_ref, theirs_ref, spread_ref, half_ref, sent_ref, slots_ref):
-    del half_ref
-    mix_half(place_ref, 1, left_ref, mine_ref, theirs_ref, spread_ref, sent_ref, slots_ref)
+    mix_half(place_ref, 0, left_ref, mine_ref, theirs_ref, spread_ref, rows_ref)
+
+
+def far_kernel(place_ref, left_ref, mine_ref, theirs_ref, spread_ref, near_ref, rows_ref, sent_ref):
+    del near_ref
+    mix_half(place_ref, 1, left_ref, mine_ref, theirs_ref, spread_ref, rows_ref)
+    for t in range(3):
+        sent_ref[:, :, t * 128 : (t + 1) * 128] = rows_ref[t].astype(BF16).reshape(128, 2, 128)
 
 
 def update_kernel(got_ref, gate_ref, columns_ref, weight_ref, out_ref, rows_ref, flat_ref):
@@ -286,25 +283,24 @@
     near = lax.ppermute(right, BOTH, CORE_FLIP)
     far = lax.ppermute(right, BOTH, HALF_FLIP)
     both = lax.ppermute(far, BOTH, CORE_FLIP)
-    sent, gate, left = pl.pallas_call(
+    near_rows, gate, left = pl.pallas_call(
         near_kernel,
         name="near",
-        out_shape=(message, struct((rows * cols, width), F32), struct((96, 384), BF16)),
+        out_shape=(struct((3, 256, 128), F32), struct((rows * cols, width), F32), struct((96, 384), BF16)),
         in_specs=[SMEM] + [VMEM] * 6,
         out_specs=(VMEM,) * 3,
-        scratch_shapes=[pltpu.VMEM((6, 64, 128), F32)] + scratch,
+        scratch_shapes=scratch,
         compiler_params=params,
     )(place, got, right, near, spread, normed, output_gate)
-    sent = pl.pallas_call(
+    _, sent = pl.pallas_call(
         far_kernel,
         name="far",
-        out_shape=message,
+        out_shape=(struct((3, 256, 128), F32), message),
         in_specs=[SMEM] + [VMEM] * 5,
-        out_specs=VMEM,
-        scratch_shapes=[pltpu.VMEM((6, 64, 128), F32)],
+        out_specs=(VMEM, VMEM),
         input_output_aliases={5: 0},
         compiler_params=params,
-    )(place, left, far, both, spread, sent)
+    )(place, left, far, both, spread, near_rows)
     got = lax.all_to_all(sent, BOTH, 0, 0, axis_index_groups=SHARING)
     return pl.pallas_call(
         update_kernel,

time: 68.1 us -> 68.2 us (level)
  no operation moved by 1% of the time
where the time goes in v10:
time: 68.2 us; the launch traced here: 67.9 us
  blocking collectives  49 us (72%)
  starting transfers between devices  12.2 us (18%)
  Pallas kernels  6.4 us (9%)
    all_to_all x2, blocking collectives, shards(): got = lax.all_to_all(sent, BOTH, 0, 0, axis_index_groups=SHARING)  49 us
    ppermute x1, starting transfers between devices, shards(): far = lax.ppermute(right, BOTH, HALF_FLIP)  4.42 us
    ppermute x1, starting transfers between devices, shards(): near = lax.ppermute(right, BOTH, CORE_FLIP)  4.31 us
    ppermute x1, starting transfers between devices, shards(): both = lax.ppermute(far, BOTH, CORE_FLIP)  3.52 us
    pallas_call x1, Pallas kernels, shards(): pl.pallas_call(edges_kernel, name='edges', out_shape=(message, struct((ro...  2.18 us
    pallas_call x1, Pallas kernels, shards(): pl.pallas_call(near_kernel, name='near', out_shape=(struct((3, 256, 128),...  1.43 us
  transfers between devices with their start and end apart: 3, of which 0 were waited for; matrix products, arithmetic and copies ran while one was open for 0% of the time, Pallas kernels for 2%

profile of v10, /device:TPU:1, one launch (start us, length us, event | category | flops | bytes accessed | tf_op | source)
XLA Modules:
  0.0 67.9 jit_solution(17319991005061249971)
XLA Ops:
  0.0 0.1 stack.23.place_ref
  0.1 2.2 %edges.1 = (bf16[128,2,384]{2,1,0:T(2,128)(2,1)S(1)}, bf16[288,128]{1,0:T(8,128)(2,1)S(1)}, f32[2,128,128]{2,1,0:T(8,128)S(1)}, bf16[192,256]{1,0:T(8,128)(2,1)S(1)}) custom-call(s32[5]{0:T(128)S(1)} %stack.23.place_ref, bf16[288,128]{1,0:T(8,128)(2,1)} %bitcast.10, s32[384]{0:T(512)} %mask_hbm.1, f32[1,128]{1,0:T(1,128)} %bitcast.11, f32[1,128]{1,0:T(1,128)} %bitcast.12, ...), custom_call_target="tpu_custom_call" | custom-call | tf_op jit(solution)/shard_map/edges/pallas_call | solution.py:258
  2.3 30.4 %all_to_all.10.got_ref = bf16[128,2,384]{2,1,0:T(2,128)(2,1)S(1)} all-to-all(bf16[128,2,384]{2,1,0:T(2,128)(2,1)S(1)} %get-tuple-element.13), channel_id=1, replica_groups={{0,1,2,3,4,5,6,7,8,9,10,11,12,13,14,15,32,33,34,35,36,37,38,39,40,41,42..., dimensions={0} | all-to-all | bytes 393216 | tf_op jit(solution)/shard_map/all_to_all | solution.py:272
  32.7 0.0 copy-start
  32.7 0.4 right.1.mine_ref
  33.1 4.4 %collective-permute-start.1 = (bf16[96,384]{1,0:T(8,128)(2,1)S(1)}, bf16[96,384]{1,0:T(8,128)(2,1)S(1)}, u32[]{:S(2)}, u32[]{:S(2)}) collective-permute-start(bf16[96,384]{1,0:T(8,128)(2,1)S(1)} %right.1.mine_ref), channel_id=1, source_target_pairs={{0,224},{1,225},{2,226},{3,227},{4,228},{5,229},{6,230},{7,231},{8... | collective-permute-start | bytes 221192 | tf_op jit(solution)/shard_map/ppermute | solution.py:284
  37.6 4.3 %collective-permute-start = (bf16[96,384]{1,0:T(8,128)(2,1)S(1)}, bf16[96,384]{1,0:T(8,128)(2,1)S(1)}, u32[]{:S(2)}, u32[]{:S(2)}) collective-permute-start(bf16[96,384]{1,0:T(8,128)(2,1)S(1)} %right.1.mine_ref), channel_id=1, source_target_pairs={{0,16},{1,17},{2,18},{3,19},{4,20},{5,21},{6,22},{7,23},{8,24},{9,... | collective-permute-start | bytes 221192 | tf_op jit(solution)/shard_map/ppermute | solution.py:283
  41.9 0.0 collective-permute-done.1.mine_ref
  41.9 3.5 %collective-permute-start.2 = (bf16[96,384]{1,0:T(8,128)(2,1)S(1)}, bf16[96,384]{1,0:T(8,128)(2,1)S(1)}, u32[]{:S(2)}, u32[]{:S(2)}) collective-permute-start(bf16[96,384]{1,0:T(8,128)(2,1)S(1)} %collective-permute-done.1.mine_ref), channel_id=1, source_target_pairs={{0,16},{1,17},{2,18},{3,19},{4,20},{5,21},{6,22},{7,23},{8,24},{9,... | collective-permute-start | bytes 221192 | tf_op jit(solution)/shard_map/ppermute | solution.py:285
  45.4 0.0 collective-permute-done.theirs_ref
  45.4 0.0 copy-done
  45.5 1.4 %near.1 = (f32[3,256,128]{2,1,0:T(8,128)S(1)}, f32[288,128]{1,0:T(8,128)S(1)}, bf16[96,384]{1,0:T(8,128)(2,1)S(1)}) custom-call(s32[5]{0:T(128)S(1)} %stack.23.place_ref, bf16[128,2,384]{2,1,0:T(2,128)(2,1)S(1)} %all_to_all.10.got_ref, bf16[96,384]{1,0:T(8,128)(2,1)S(1)} %right.1.mine_ref, bf16[96,384]{1,0:T(8,128)(2,1)S(1)} %collective-permute-done.theirs_ref, ...), custom_call_target="tpu_custom_call" | custom-call | tf_op jit(solution)/shard_map/near/pallas_call | solution.py:286
  46.9 0.0 collective-permute-done.2.theirs_ref
  46.9 1.3 %far.1 = (f32[3,256,128]{2,1,0:T(8,128)S(1)}, bf16[128,2,384]{2,1,0:T(2,128)(2,1)S(1)}) custom-call(s32[5]{0:T(128)S(1)} %stack.23.place_ref, bf16[96,384]{1,0:T(8,128)(2,1)S(1)} %get-tuple-element.16.left_ref, bf16[96,384]{1,0:T(8,128)(2,1)S(1)} %collective-permute-done.1.mine_ref, ...), custom_call_target="tpu_custom_call", output_to_operand_aliasing={{0}: (5, {})} | custom-call | tf_op jit(solution)/shard_map/far/pallas_call | solution.py:295
  48.2 0.0 copy-start.1
  48.2 18.6 %all_to_all.11.got_ref = bf16[128,2,384]{2,1,0:T(2,128)(2,1)S(1)} all-to-all(bf16[128,2,384]{2,1,0:T(2,128)(2,1)S(1)} %get-tuple-element.18), channel_id=1, replica_groups={{0,1,2,3,4,5,6,7,8,9,10,11,12,13,14,15,32,33,34,35,36,37,38,39,40,41,42..., dimensions={0} | all-to-all | bytes 393216 | tf_op jit(solution)/shard_map/all_to_all | solution.py:304
  66.8 0.0 copy-done.1
  66.8 1.1 %update.1 = bf16[12,24,128]{2,1,0:T(8,128)(2,1)} custom-call(bf16[128,2,384]{2,1,0:T(2,128)(2,1)S(1)} %all_to_all.11.got_ref, f32[288,128]{1,0:T(8,128)S(1)} %get-tuple-element.19.gate_ref, f32[2,128,128]{2,1,0:T(8,128)S(1)} %get-tuple-element.20.columns_ref, bf16[128,128]{1,0:T(8,128)(2,1)S(1)} %copy-done.1), custom_call_target="tpu_custom_call" | custom-call | tf_op jit(solution)/shard_map/update/pallas_call | solution.py:305
Async XLA Ops:
  32.7 12.7 %copy-start = (bf16[128,128]{1,0:T(8,128)(2,1)S(1)}, bf16[128,128]{1,0:T(8,128)(2,1)}, u32[]{:S(2)}) copy-start(bf16[128,128]{1,0:T(8,128)(2,1)} %og_ref.1) | copy-start | bytes 98308
  33.1 8.8 %collective-permute-start.1 = (bf16[96,384]{1,0:T(8,128)(2,1)S(1)}, bf16[96,384]{1,0:T(8,128)(2,1)S(1)}, u32[]{:S(2)}, u32[]{:S(2)}) collective-permute-start(bf16[96,384]{1,0:T(8,128)(2,1)S(1)} %right.1.mine_ref), channel_id=1, source_target_pairs={{0,224},{1,225},{2,226},{3,227},{4,228},{5,229},{6,230},{7,231},{8... | collective-permute-start | bytes 221192 | tf_op jit(solution)/shard_map/ppermute | solution.py:284
  37.6 7.9 %collective-permute-start = (bf16[96,384]{1,0:T(8,128)(2,1)S(1)}, bf16[96,384]{1,0:T(8,128)(2,1)S(1)}, u32[]{:S(2)}, u32[]{:S(2)}) collective-permute-start(bf16[96,384]{1,0:T(8,128)(2,1)S(1)} %right.1.mine_ref), channel_id=1, source_target_pairs={{0,16},{1,17},{2,18},{3,19},{4,20},{5,21},{6,22},{7,23},{8,24},{9,... | collective-permute-start | bytes 221192 | tf_op jit(solution)/shard_map/ppermute | solution.py:283
  41.9 5.0 %collective-permute-start.2 = (bf16[96,384]{1,0:T(8,128)(2,1)S(1)}, bf16[96,384]{1,0:T(8,128)(2,1)S(1)}, u32[]{:S(2)}, u32[]{:S(2)}) collective-permute-start(bf16[96,384]{1,0:T(8,128)(2,1)S(1)} %collective-permute-done.1.mine_ref), channel_id=1, source_target_pairs={{0,16},{1,17},{2,18},{3,19},{4,20},{5,21},{6,22},{7,23},{8,24},{9,... | collective-permute-start | bytes 221192 | tf_op jit(solution)/shard_map/ppermute | solution.py:285
  48.2 18.6 %copy-start.1 = (bf16[128,128]{1,0:T(8,128)(2,1)S(1)}, bf16[128,128]{1,0:T(8,128)(2,1)}, u32[]{:S(2)}) copy-start(bf16[128,128]{1,0:T(8,128)(2,1)} %weight_ref.1) | copy-start | bytes 98308

commit v11 on v9

--- a/solution.py
+++ b/solution.py
@@ -11,7 +11,6 @@
 F32 = jnp.float32
 BF16 = jnp.bfloat16
 VMEM = pl.BlockSpec(memory_space=pltpu.VMEM)
-SMEM = pl.BlockSpec(memory_space=pltpu.SMEM)
 HBM = pl.BlockSpec(memory_space=pltpu.HBM)
 
 
@@ -33,6 +32,11 @@
 HALF_FLIP = [(device(xl, y, core, xh, z), device(xl, 7 - y, core, xh, z)) for xl, y, core, xh, z in PLACES]
 
 
+def place_of():
+    block = lax.axis_index("ia")
+    return block * 12, lax.axis_index("ja") * 24, lax.rem(block, 2), lax.rem(lax.div(block, 8), 2)
+
+
 def sigmoid(x):
     return 1.0 / (1.0 + jnp.exp(-x))
 
@@ -46,7 +50,6 @@
 
 
 def edges_kernel(
-    place_ref,
     pair_hbm,
     mask_hbm,
     gain_hbm,
@@ -93,7 +96,7 @@
     side = jnp.where(row >= 96, 1, 0)
     row = row - 96 * side
     run = sum(jnp.where(row >= 12 * n, 1, 0) for n in range(1, 8))
-    core = place_ref[2]
+    first_row, first_col, core, _ = place_of()
     to_lane = row + 20 * run + 16 * jnp.where(side == 0, core, 1 - core)
     spread_ref[...] = jnp.where(iota(spread_ref.shape, 1) == to_lane, 1.0, 0.0).astype(BF16)
     for copy in copies[:4]:
@@ -109,10 +112,10 @@
     place = iota((cols, width), 0)
     col_valid = jnp.zeros((cols, width), F32)
     for k in range(cols):
-        col_valid = jnp.where(place == k, mask_ref[place_ref[1] + k].astype(F32), col_valid)
+        col_valid = jnp.where(place == k, mask_ref[first_col + k].astype(F32), col_valid)
     parts = []
     for i in [3 * ii + iq for iq in range(3) for ii in range(4)]:
-        row_valid = mask_ref[place_ref[0] + i].astype(F32)
+        row_valid = mask_ref[first_row + i].astype(F32)
         parts.append(normed[i * cols : (i + 1) * cols] * (col_valid * row_valid))
         parts.append(jnp.zeros((WIDE - cols, width), F32))
     masked = jnp.concatenate(parts, axis=0).astype(BF16)
@@ -163,9 +166,10 @@
         right_ref[:, v * 128 : (v + 1) * 128] = dense_ref[v].astype(BF16)
 
 
-def mix_half(place_ref, other, left_ref, mine_ref, theirs_ref, spread_ref, sent_ref, slots_ref):
+def mix_half(other, left_ref, mine_ref, theirs_ref, spread_ref, sent_ref, slots_ref):
     lane = iota((8, 128), 1)
-    half = place_ref[3 + other]
+    half = place_of()[3]
+    half = 1 - half if other else half
     mixed = contract(left_ref[...], jnp.concatenate([mine_ref[...], theirs_ref[...]], axis=0), 1, 1)
     high = mixed.astype(BF16)
     low = (mixed - high.astype(F32)).astype(BF16)
@@ -185,7 +189,6 @@
 
 
 def near_kernel(
-    place_ref,
     got_ref,
     mine_ref,
     theirs_ref,
@@ -205,12 +208,12 @@
             block = jnp.concatenate([blocks[iq, ii][v] for ii in range(4)], axis=0)
             left_ref[iq * 32 : (iq + 1) * 32, v * 128 : (v + 1) * 128] = block.astype(BF16)
     gate_ref[...] = sigmoid(contract(normed_ref[...], og_ref[...], 1, 0))
-    mix_half(place_ref, 0, left_ref, mine_ref, theirs_ref, spread_ref, sent_ref, slots_ref)
-
-
-def far_kernel(place_ref, left_ref, mine_ref, theirs_ref, spread_ref, half_ref, sent_ref, slots_ref):
+    mix_half(0, left_ref, mine_ref, theirs_ref, spread_ref, sent_ref, slots_ref)
+
+
+def far_kernel(left_ref, mine_ref, theirs_ref, spread_ref, half_ref, sent_ref, slots_ref):
     del half_ref
-    mix_half(place_ref, 1, left_ref, mine_ref, theirs_ref, spread_ref, sent_ref, slots_ref)
+    mix_half(1, left_ref, mine_ref, theirs_ref, spread_ref, sent_ref, slots_ref)
 
 
 def update_kernel(got_ref, gate_ref, columns_ref, weight_ref, out_ref, rows_ref, flat_ref):
@@ -248,9 +251,6 @@
 ):
     rows, cols, width = pair.shape
     params = pltpu.CompilerParams(vmem_limit_bytes=32 * 1024 * 1024)
-    row_block = lax.axis_index("ia")
-    half = row_block // 8 % 2
-    place = jnp.stack([row_block * rows, lax.axis_index("ja") * cols, row_block % 2, half, 1 - half]).astype(jnp.int32)
     struct = jax.ShapeDtypeStruct
     message = struct((width, 2, rows * WIDE), BF16)
     arrays = [pair.reshape(rows * cols, width), token_mask]
@@ -267,11 +267,11 @@
             struct((2, width, width), F32),
             struct((192, 256), BF16),
         ),
-        in_specs=[SMEM] + [HBM] * 10,
+        in_specs=[HBM] * 10,
         out_specs=(VMEM,) * 4,
         scratch_shapes=fetched + [pltpu.VMEM((3, 256, 128), F32), pltpu.SemaphoreType.DMA((10,))],
         compiler_params=params,
-    )(place, *[pltpu.with_memory_space_constraint(array, pltpu.HBM) for array in arrays])
+    )(*[pltpu.with_memory_space_constraint(array, pltpu.HBM) for array in arrays])
     got = lax.all_to_all(sent, BOTH, 0, 0, axis_index_groups=SHARING)
     scratch = [pltpu.VMEM((3, 256, 128), F32), pltpu.VMEM((384, 128), F32)]
     right = pl.pallas_call(
@@ -290,21 +290,21 @@
         near_kernel,
         name="near",
         out_shape=(message, struct((rows * cols, width), F32), struct((96, 384), BF16)),
-        in_specs=[SMEM] + [VMEM] * 6,
+        in_specs=[VMEM] * 6,
         out_specs=(VMEM,) * 3,
         scratch_shapes=[pltpu.VMEM((6, 64, 128), F32)] + scratch,
         compiler_params=params,
-    )(place, got, right, near, spread, normed, output_gate)
+    )(got, right, near, spread, normed, output_gate)
     sent = pl.pallas_call(
         far_kernel,
         name="far",
         out_shape=message,
-        in_specs=[SMEM] + [VMEM] * 5,
+        in_specs=[VMEM] * 5,
         out_specs=VMEM,
         scratch_shapes=[pltpu.VMEM((6, 64, 128), F32)],
-        input_output_aliases={5: 0},
-        compiler_params=params,
-    )(place, left, far, both, spread, sent)
+        input_output_aliases={4: 0},
+        compiler_params=params,
+    )(left, far, both, spread, sent)
     got = lax.all_to_all(sent, BOTH, 0, 0, axis_index_groups=SHARING)
     return pl.pallas_call(
         update_kernel,

time: 68.1 us -> 66.3 us (0.974)
  Pallas kernels: 6.28 us -> 4.68 us
  transfers between devices with their start and end apart: 3 -> 3, of which waited for: 0 -> 0; matrix products, arithmetic and copies ran while one was open for 0% -> 0% of each run, Pallas kernels for 2% -> 1%
where the time goes in v11:
time: 66.3 us; the launch traced here: 66 us
  blocking collectives  48.9 us (74%)
  starting transfers between devices  12.2 us (18%)
  Pallas kernels  4.68 us (7%)
    all_to_all x2, blocking collectives, shards(): got = lax.all_to_all(sent, BOTH, 0, 0, axis_index_groups=SHARING)  48.9 us
    ppermute x1, starting transfers between devices, shards(): far = lax.ppermute(right, BOTH, HALF_FLIP)  4.41 us
    ppermute x1, starting transfers between devices, shards(): near = lax.ppermute(right, BOTH, CORE_FLIP)  4.32 us
    ppermute x1, starting transfers between devices, shards(): both = lax.ppermute(far, BOTH, CORE_FLIP)  3.52 us
    pallas_call x1, Pallas kernels, shards(): pl.pallas_call(edges_kernel, name='edges', out_shape=(message, struct((ro...  1.64 us
  transfers between devices with their start and end apart: 3, of which 0 were waited for; matrix products, arithmetic and copies ran while one was open for 0% of the time, Pallas kernels for 1%

profile of v11, /device:TPU:1, one launch (start us, length us, event | category | flops | bytes accessed | tf_op | source)
XLA Modules:
  0.0 66.0 jit_solution(14293503690358804400)
XLA Ops:
  0.0 1.6 %edges.1 = (bf16[128,2,384]{2,1,0:T(2,128)(2,1)S(1)}, bf16[288,128]{1,0:T(8,128)(2,1)S(1)}, f32[2,128,128]{2,1,0:T(8,128)S(1)}, bf16[192,256]{1,0:T(8,128)(2,1)S(1)}) custom-call(bf16[288,128]{1,0:T(8,128)(2,1)} %bitcast.5, s32[384]{0:T(512)} %mask_hbm.1, f32[1,128]{1,0:T(1,128)} %bitcast.6, f32[1,128]{1,0:T(1,128)} %bitcast.7, f32[1,128]{1,0:T(1,128)} %bitcast.8, ...), custom_call_target="tpu_custom_call" | custom-call | tf_op jit(solution)/shard_map/edges/pallas_call | solution.py:261
  1.6 30.4 %all_to_all.10.got_ref = bf16[128,2,384]{2,1,0:T(2,128)(2,1)S(1)} all-to-all(bf16[128,2,384]{2,1,0:T(2,128)(2,1)S(1)} %get-tuple-element.12), channel_id=1, replica_groups={{0,1,2,3,4,5,6,7,8,9,10,11,12,13,14,15,32,33,34,35,36,37,38,39,40,41,42..., dimensions={0} | all-to-all | bytes 393216 | tf_op jit(solution)/shard_map/all_to_all | solution.py:275
  32.1 0.0 copy-start
  32.1 0.4 right.1.mine_ref
  32.5 4.4 %collective-permute-start.1 = (bf16[96,384]{1,0:T(8,128)(2,1)S(1)}, bf16[96,384]{1,0:T(8,128)(2,1)S(1)}, u32[]{:S(2)}, u32[]{:S(2)}) collective-permute-start(bf16[96,384]{1,0:T(8,128)(2,1)S(1)} %right.1.mine_ref), channel_id=1, source_target_pairs={{0,224},{1,225},{2,226},{3,227},{4,228},{5,229},{6,230},{7,231},{8... | collective-permute-start | bytes 221192 | tf_op jit(solution)/shard_map/ppermute | solution.py:287
  36.9 4.3 %collective-permute-start = (bf16[96,384]{1,0:T(8,128)(2,1)S(1)}, bf16[96,384]{1,0:T(8,128)(2,1)S(1)}, u32[]{:S(2)}, u32[]{:S(2)}) collective-permute-start(bf16[96,384]{1,0:T(8,128)(2,1)S(1)} %right.1.mine_ref), channel_id=1, source_target_pairs={{0,16},{1,17},{2,18},{3,19},{4,20},{5,21},{6,22},{7,23},{8,24},{9,... | collective-permute-start | bytes 221192 | tf_op jit(solution)/shard_map/ppermute | solution.py:286
  41.3 0.0 collective-permute-done.1.mine_ref
  41.3 3.5 %collective-permute-start.2 = (bf16[96,384]{1,0:T(8,128)(2,1)S(1)}, bf16[96,384]{1,0:T(8,128)(2,1)S(1)}, u32[]{:S(2)}, u32[]{:S(2)}) collective-permute-start(bf16[96,384]{1,0:T(8,128)(2,1)S(1)} %collective-permute-done.1.mine_ref), channel_id=1, source_target_pairs={{0,16},{1,17},{2,18},{3,19},{4,20},{5,21},{6,22},{7,23},{8,24},{9,... | collective-permute-start | bytes 221192 | tf_op jit(solution)/shard_map/ppermute | solution.py:288
  44.8 0.0 collective-permute-done.theirs_ref
  44.8 0.0 copy-done
  44.8 0.9 %near.1 = (bf16[128,2,384]{2,1,0:T(2,128)(2,1)S(1)}, f32[288,128]{1,0:T(8,128)S(1)}, bf16[96,384]{1,0:T(8,128)(2,1)S(1)}) custom-call(bf16[128,2,384]{2,1,0:T(2,128)(2,1)S(1)} %all_to_all.10.got_ref, bf16[96,384]{1,0:T(8,128)(2,1)S(1)} %right.1.mine_ref, bf16[96,384]{1,0:T(8,128)(2,1)S(1)} %collective-permute-done.theirs_ref, ...), custom_call_target="tpu_custom_call" | custom-call | tf_op jit(solution)/shard_map/near/pallas_call | solution.py:289
  45.7 0.0 collective-permute-done.2.theirs_ref
  45.7 0.6 far.1
  46.4 0.0 copy-start.1
  46.4 18.5 %all_to_all.11.got_ref = bf16[128,2,384]{2,1,0:T(2,128)(2,1)S(1)} all-to-all(bf16[128,2,384]{2,1,0:T(2,128)(2,1)S(1)} %far.1), channel_id=1, replica_groups={{0,1,2,3,4,5,6,7,8,9,10,11,12,13,14,15,32,33,34,35,36,37,38,39,40,41,42..., dimensions={0} | all-to-all | bytes 393216 | tf_op jit(solution)/shard_map/all_to_all | solution.py:308
  64.9 0.0 copy-done.1
  64.9 1.1 %update.1 = bf16[12,24,128]{2,1,0:T(8,128)(2,1)} custom-call(bf16[128,2,384]{2,1,0:T(2,128)(2,1)S(1)} %all_to_all.11.got_ref, f32[288,128]{1,0:T(8,128)S(1)} %get-tuple-element.17.gate_ref, f32[2,128,128]{2,1,0:T(8,128)S(1)} %get-tuple-element.18.columns_ref, bf16[128,128]{1,0:T(8,128)(2,1)S(1)} %copy-done.1), custom_call_target="tpu_custom_call" | custom-call | tf_op jit(solution)/shard_map/update/pallas_call | solution.py:309
Async XLA Ops:
  32.1 12.7 %copy-start = (bf16[128,128]{1,0:T(8,128)(2,1)S(1)}, bf16[128,128]{1,0:T(8,128)(2,1)}, u32[]{:S(2)}) copy-start(bf16[128,128]{1,0:T(8,128)(2,1)} %og_ref.1) | copy-start | bytes 98308
  32.5 8.8 %collective-permute-start.1 = (bf16[96,384]{1,0:T(8,128)(2,1)S(1)}, bf16[96,384]{1,0:T(8,128)(2,1)S(1)}, u32[]{:S(2)}, u32[]{:S(2)}) collective-permute-start(bf16[96,384]{1,0:T(8,128)(2,1)S(1)} %right.1.mine_ref), channel_id=1, source_target_pairs={{0,224},{1,225},{2,226},{3,227},{4,228},{5,229},{6,230},{7,231},{8... | collective-permute-start | bytes 221192 | tf_op jit(solution)/shard_map/ppermute | solution.py:287
  36.9 7.9 %collective-permute-start = (bf16[96,384]{1,0:T(8,128)(2,1)S(1)}, bf16[96,384]{1,0:T(8,128)(2,1)S(1)}, u32[]{:S(2)}, u32[]{:S(2)}) collective-permute-start(bf16[96,384]{1,0:T(8,128)(2,1)S(1)} %right.1.mine_ref), channel_id=1, source_target_pairs={{0,16},{1,17},{2,18},{3,19},{4,20},{5,21},{6,22},{7,23},{8,24},{9,... | collective-permute-start | bytes 221192 | tf_op jit(solution)/shard_map/ppermute | solution.py:286
  41.3 4.5 %collective-permute-start.2 = (bf16[96,384]{1,0:T(8,128)(2,1)S(1)}, bf16[96,384]{1,0:T(8,128)(2,1)S(1)}, u32[]{:S(2)}, u32[]{:S(2)}) collective-permute-start(bf16[96,384]{1,0:T(8,128)(2,1)S(1)} %collective-permute-done.1.mine_ref), channel_id=1, source_target_pairs={{0,16},{1,17},{2,18},{3,19},{4,20},{5,21},{6,22},{7,23},{8,24},{9,... | collective-permute-start | bytes 221192 | tf_op jit(solution)/shard_map/ppermute | solution.py:288
  46.4 18.5 %copy-start.1 = (bf16[128,128]{1,0:T(8,128)(2,1)S(1)}, bf16[128,128]{1,0:T(8,128)(2,1)}, u32[]{:S(2)}) copy-start(bf16[128,128]{1,0:T(8,128)(2,1)} %weight_ref.1) | copy-start | bytes 98308

commit v12 on v11

--- a/solution.py
+++ b/solution.py
@@ -133,14 +133,18 @@
 
 
 def swap_blocks(blocks, lane):
-    out = []
-    for b in range(4):
-        total = None
+    axis = blocks[0].ndim - 1
+    run = lane // WIDE
+    for step in (2, 1):
+        high = run // step % 2 == 1
+        swapped = list(blocks)
         for a in range(4):
-            moved = blocks[a] if a == b else pltpu.roll(blocks[a], (WIDE * (a - b)) % 128, blocks[a].ndim - 1)
-            total = moved if total is None else jnp.where(lane // WIDE == a, moved, total)
-        out.append(total)
-    return out
+            b = a + step
+            if a // step % 2 == 0:
+                swapped[a] = jnp.where(high, pltpu.roll(blocks[b], step * WIDE, axis), blocks[a])
+                swapped[b] = jnp.where(high, blocks[b], pltpu.roll(blocks[a], 128 - step * WIDE, axis))
+        blocks = swapped
+    return blocks
 
 
 def spread_side(side, got_ref, rows_ref, quads_ref):
@@ -166,14 +170,17 @@
         right_ref[:, v * 128 : (v + 1) * 128] = dense_ref[v].astype(BF16)
 
 
-def mix_half(other, left_ref, mine_ref, theirs_ref, spread_ref, sent_ref, slots_ref):
+def mix_block(left_ref, right_ref, spread):
+    mixed = contract(left_ref[...], right_ref[...], 1, 1)
+    high = mixed.astype(BF16)
+    low = (mixed - high.astype(F32)).astype(BF16)
+    return contract(jnp.concatenate([high, low], axis=0), spread, 1, 0)
+
+
+def write_half(other, parts, sent_ref, slots_ref):
     lane = iota((8, 128), 1)
     half = place_of()[3]
     half = 1 - half if other else half
-    mixed = contract(left_ref[...], jnp.concatenate([mine_ref[...], theirs_ref[...]], axis=0), 1, 1)
-    high = mixed.astype(BF16)
-    low = (mixed - high.astype(F32)).astype(BF16)
-    parts = contract(jnp.concatenate([high, low], axis=0), spread_ref[...], 1, 0)
     for xl in range(2):
         for iq in range(3):
             for part in range(2):
@@ -192,12 +199,14 @@
     got_ref,
     mine_ref,
     theirs_ref,
+    far_ref,
     spread_ref,
     normed_ref,
     og_ref,
     sent_ref,
     gate_ref,
     left_ref,
+    parts_ref,
     slots_ref,
     rows_ref,
     quads_ref,
@@ -208,12 +217,16 @@
             block = jnp.concatenate([blocks[iq, ii][v] for ii in range(4)], axis=0)
             left_ref[iq * 32 : (iq + 1) * 32, v * 128 : (v + 1) * 128] = block.astype(BF16)
     gate_ref[...] = sigmoid(contract(normed_ref[...], og_ref[...], 1, 0))
-    mix_half(0, left_ref, mine_ref, theirs_ref, spread_ref, sent_ref, slots_ref)
-
-
-def far_kernel(left_ref, mine_ref, theirs_ref, spread_ref, half_ref, sent_ref, slots_ref):
+    mine, theirs = spread_ref[0:96], spread_ref[96:192]
+    parts = mix_block(left_ref, mine_ref, mine) + mix_block(left_ref, theirs_ref, theirs)
+    write_half(0, parts, sent_ref, slots_ref)
+    parts_ref[...] = mix_block(left_ref, far_ref, mine)
+
+
+def far_kernel(left_ref, theirs_ref, spread_ref, parts_ref, half_ref, sent_ref, slots_ref):
     del half_ref
-    mix_half(1, left_ref, mine_ref, theirs_ref, spread_ref, sent_ref, slots_ref)
+    parts = parts_ref[...] + mix_block(left_ref, theirs_ref, spread_ref[96:192])
+    write_half(1, parts, sent_ref, slots_ref)
 
 
 def update_kernel(got_ref, gate_ref, columns_ref, weight_ref, out_ref, rows_ref, flat_ref):
@@ -286,15 +299,20 @@
     near = lax.ppermute(right, BOTH, CORE_FLIP)
     far = lax.ppermute(right, BOTH, HALF_FLIP)
     both = lax.ppermute(far, BOTH, CORE_FLIP)
-    sent, gate, left = pl.pallas_call(
+    sent, gate, left, parts = pl.pallas_call(
         near_kernel,
         name="near",
-        out_shape=(message, struct((rows * cols, width), F32), struct((96, 384), BF16)),
-        in_specs=[VMEM] * 6,
-        out_specs=(VMEM,) * 3,
+        out_shape=(
+            message,
+            struct((rows * cols, width), F32),
+            struct((96, 384), BF16),
+            struct((192, 256), F32),
+        ),
+        in_specs=[VMEM] * 7,
+        out_specs=(VMEM,) * 4,
         scratch_shapes=[pltpu.VMEM((6, 64, 128), F32)] + scratch,
         compiler_params=params,
-    )(got, right, near, spread, normed, output_gate)
+    )(got, right, near, far, spread, normed, output_gate)
     sent = pl.pallas_call(
         far_kernel,
         name="far",
@@ -304,7 +322,7 @@
         scratch_shapes=[pltpu.VMEM((6, 64, 128), F32)],
         input_output_aliases={4: 0},
         compiler_params=params,
-    )(left, far, both, spread, sent)
+    )(left, both, spread, parts, sent)
     got = lax.all_to_all(sent, BOTH, 0, 0, axis_index_groups=SHARING)
     return pl.pallas_call(
         update_kernel,

time: 66.3 us -> 66.4 us (level)
  transfers between devices with their start and end apart: 3 -> 3, of which waited for: 0 -> 0; matrix products, arithmetic and copies ran while one was open for 0% -> 0% of each run, Pallas kernels for 1% -> 2%
where the time goes in v12:
time: 66.4 us; the launch traced here: 66 us
  blocking collectives  48.9 us (74%)
  starting transfers between devices  12.2 us (18%)
  Pallas kernels  4.74 us (7%)
    all_to_all x2, blocking collectives, shards(): got = lax.all_to_all(sent, BOTH, 0, 0, axis_index_groups=SHARING)  48.9 us
    ppermute x1, starting transfers between devices, shards(): far = lax.ppermute(right, BOTH, HALF_FLIP)  4.41 us
    ppermute x1, starting transfers between devices, shards(): near = lax.ppermute(right, BOTH, CORE_FLIP)  4.32 us
    ppermute x1, starting transfers between devices, shards(): both = lax.ppermute(far, BOTH, CORE_FLIP)  3.52 us
    pallas_call x1, Pallas kernels, shards(): pl.pallas_call(edges_kernel, name='edges', out_shape=(message, struct((ro...  1.64 us
  transfers between devices with their start and end apart: 3, of which 0 were waited for; matrix products, arithmetic and copies ran while one was open for 0% of the time, Pallas kernels for 2%

profile of v12, /device:TPU:1, one launch (start us, length us, event | category | flops | bytes accessed | tf_op | source)
XLA Modules:
  0.0 66.0 jit_solution(4313157630393605941)
XLA Ops:
  0.0 1.6 %edges.1 = (bf16[128,2,384]{2,1,0:T(2,128)(2,1)S(1)}, bf16[288,128]{1,0:T(8,128)(2,1)S(1)}, f32[2,128,128]{2,1,0:T(8,128)S(1)}, bf16[192,256]{1,0:T(8,128)(2,1)S(1)}) custom-call(bf16[288,128]{1,0:T(8,128)(2,1)} %bitcast.5, s32[384]{0:T(512)} %mask_hbm.1, f32[1,128]{1,0:T(1,128)} %bitcast.6, f32[1,128]{1,0:T(1,128)} %bitcast.7, f32[1,128]{1,0:T(1,128)} %bitcast.8, ...), custom_call_target="tpu_custom_call" | custom-call | tf_op jit(solution)/shard_map/edges/pallas_call | solution.py:274
  1.6 30.4 %all_to_all.10.got_ref = bf16[128,2,384]{2,1,0:T(2,128)(2,1)S(1)} all-to-all(bf16[128,2,384]{2,1,0:T(2,128)(2,1)S(1)} %get-tuple-element.13), channel_id=1, replica_groups={{0,1,2,3,4,5,6,7,8,9,10,11,12,13,14,15,32,33,34,35,36,37,38,39,40,41,42..., dimensions={0} | all-to-all | bytes 393216 | tf_op jit(solution)/shard_map/all_to_all | solution.py:288
  32.1 0.0 copy-start
  32.1 0.4 right.1.mine_ref
  32.5 4.4 %collective-permute-start.1 = (bf16[96,384]{1,0:T(8,128)(2,1)S(1)}, bf16[96,384]{1,0:T(8,128)(2,1)S(1)}, u32[]{:S(2)}, u32[]{:S(2)}) collective-permute-start(bf16[96,384]{1,0:T(8,128)(2,1)S(1)} %right.1.mine_ref), channel_id=1, source_target_pairs={{0,224},{1,225},{2,226},{3,227},{4,228},{5,229},{6,230},{7,231},{8... | collective-permute-start | bytes 221192 | tf_op jit(solution)/shard_map/ppermute | solution.py:300
  36.9 4.3 %collective-permute-start = (bf16[96,384]{1,0:T(8,128)(2,1)S(1)}, bf16[96,384]{1,0:T(8,128)(2,1)S(1)}, u32[]{:S(2)}, u32[]{:S(2)}) collective-permute-start(bf16[96,384]{1,0:T(8,128)(2,1)S(1)} %right.1.mine_ref), channel_id=1, source_target_pairs={{0,16},{1,17},{2,18},{3,19},{4,20},{5,21},{6,22},{7,23},{8,24},{9,... | collective-permute-start | bytes 221192 | tf_op jit(solution)/shard_map/ppermute | solution.py:299
  41.2 0.0 collective-permute-done.1.far_ref
  41.3 3.5 %collective-permute-start.2 = (bf16[96,384]{1,0:T(8,128)(2,1)S(1)}, bf16[96,384]{1,0:T(8,128)(2,1)S(1)}, u32[]{:S(2)}, u32[]{:S(2)}) collective-permute-start(bf16[96,384]{1,0:T(8,128)(2,1)S(1)} %collective-permute-done.1.far_ref), channel_id=1, source_target_pairs={{0,16},{1,17},{2,18},{3,19},{4,20},{5,21},{6,22},{7,23},{8,24},{9,... | collective-permute-start | bytes 221192 | tf_op jit(solution)/shard_map/ppermute | solution.py:301
  44.8 0.0 collective-permute-done.theirs_ref
  44.8 0.0 copy-done
  44.8 1.0 %near.1 = (bf16[128,2,384]{2,1,0:T(2,128)(2,1)S(1)}, f32[288,128]{1,0:T(8,128)S(1)}, bf16[96,384]{1,0:T(8,128)(2,1)S(1)}, f32[192,256]{1,0:T(8,128)S(1)}) custom-call(bf16[128,2,384]{2,1,0:T(2,128)(2,1)S(1)} %all_to_all.10.got_ref, bf16[96,384]{1,0:T(8,128)(2,1)S(1)} %right.1.mine_ref, bf16[96,384]{1,0:T(8,128)(2,1)S(1)} %collective-permute-done.theirs_ref, ...), custom_call_target="tpu_custom_call" | custom-call | tf_op jit(solution)/shard_map/near/pallas_call | solution.py:302
  45.8 0.0 collective-permute-done.2.theirs_ref
  45.8 0.6 far.1
  46.4 0.0 copy-start.1
  46.4 18.5 %all_to_all.11.got_ref = bf16[128,2,384]{2,1,0:T(2,128)(2,1)S(1)} all-to-all(bf16[128,2,384]{2,1,0:T(2,128)(2,1)S(1)} %far.1), channel_id=1, replica_groups={{0,1,2,3,4,5,6,7,8,9,10,11,12,13,14,15,32,33,34,35,36,37,38,39,40,41,42..., dimensions={0} | all-to-all | bytes 393216 | tf_op jit(solution)/shard_map/all_to_all | solution.py:326
  64.9 0.0 copy-done.1
  64.9 1.1 %update.1 = bf16[12,24,128]{2,1,0:T(8,128)(2,1)} custom-call(bf16[128,2,384]{2,1,0:T(2,128)(2,1)S(1)} %all_to_all.11.got_ref, f32[288,128]{1,0:T(8,128)S(1)} %get-tuple-element.19.gate_ref, f32[2,128,128]{2,1,0:T(8,128)S(1)} %get-tuple-element.20.columns_ref, bf16[128,128]{1,0:T(8,128)(2,1)S(1)} %copy-done.1), custom_call_target="tpu_custom_call" | custom-call | tf_op jit(solution)/shard_map/update/pallas_call | solution.py:327
Async XLA Ops:
  32.1 12.7 %copy-start = (bf16[128,128]{1,0:T(8,128)(2,1)S(1)}, bf16[128,128]{1,0:T(8,128)(2,1)}, u32[]{:S(2)}) copy-start(bf16[128,128]{1,0:T(8,128)(2,1)} %og_ref.1) | copy-start | bytes 98308
  32.5 8.8 %collective-permute-start.1 = (bf16[96,384]{1,0:T(8,128)(2,1)S(1)}, bf16[96,384]{1,0:T(8,128)(2,1)S(1)}, u32[]{:S(2)}, u32[]{:S(2)}) collective-permute-start(bf16[96,384]{1,0:T(8,128)(2,1)S(1)} %right.1.mine_ref), channel_id=1, source_target_pairs={{0,224},{1,225},{2,226},{3,227},{4,228},{5,229},{6,230},{7,231},{8... | collective-permute-start | bytes 221192 | tf_op jit(solution)/shard_map/ppermute | solution.py:300
  36.9 7.9 %collective-permute-start = (bf16[96,384]{1,0:T(8,128)(2,1)S(1)}, bf16[96,384]{1,0:T(8,128)(2,1)S(1)}, u32[]{:S(2)}, u32[]{:S(2)}) collective-permute-start(bf16[96,384]{1,0:T(8,128)(2,1)S(1)} %right.1.mine_ref), channel_id=1, source_target_pairs={{0,16},{1,17},{2,18},{3,19},{4,20},{5,21},{6,22},{7,23},{8,24},{9,... | collective-permute-start | bytes 221192 | tf_op jit(solution)/shard_map/ppermute | solution.py:299
  41.3 4.6 %collective-permute-start.2 = (bf16[96,384]{1,0:T(8,128)(2,1)S(1)}, bf16[96,384]{1,0:T(8,128)(2,1)S(1)}, u32[]{:S(2)}, u32[]{:S(2)}) collective-permute-start(bf16[96,384]{1,0:T(8,128)(2,1)S(1)} %collective-permute-done.1.far_ref), channel_id=1, source_target_pairs={{0,16},{1,17},{2,18},{3,19},{4,20},{5,21},{6,22},{7,23},{8,24},{9,... | collective-permute-start | bytes 221192 | tf_op jit(solution)/shard_map/ppermute | solution.py:301
  46.4 18.5 %copy-start.1 = (bf16[128,128]{1,0:T(8,128)(2,1)S(1)}, bf16[128,128]{1,0:T(8,128)(2,1)}, u32[]{:S(2)}) copy-start(bf16[128,128]{1,0:T(8,128)(2,1)} %weight_ref.1) | copy-start | bytes 98308

commit v13 on v12

--- a/solution.py
+++ b/solution.py
@@ -70,10 +70,7 @@
     bias_ref,
     out_gain_ref,
     out_bias_ref,
-    lg_ref,
-    lv_ref,
-    rg_ref,
-    rv_ref,
+    weights_ref,
     rows_ref,
     arrived,
 ):
@@ -82,10 +79,10 @@
         (mask_hbm, mask_ref),
         (gain_hbm, gain_ref),
         (bias_hbm, bias_ref),
-        (lg_hbm, lg_ref),
-        (lv_hbm, lv_ref),
-        (rg_hbm, rg_ref),
-        (rv_hbm, rv_ref),
+        (lg_hbm, weights_ref.at[:, 0:128]),
+        (lv_hbm, weights_ref.at[:, 128:256]),
+        (rg_hbm, weights_ref.at[:, 256:384]),
+        (rv_hbm, weights_ref.at[:, 384:512]),
         (out_gain_hbm, out_gain_ref),
         (out_bias_hbm, out_bias_ref),
     ]
@@ -101,7 +98,7 @@
     spread_ref[...] = jnp.where(iota(spread_ref.shape, 1) == to_lane, 1.0, 0.0).astype(BF16)
     for copy in copies[:4]:
         copy.wait()
-    width = lg_ref.shape[0]
+    width = pair_ref.shape[1]
     rows, cols = 12, 24
     x = pair_ref[...].astype(F32)
     mean = jnp.mean(x, axis=-1, keepdims=True)
@@ -121,8 +118,9 @@
     masked = jnp.concatenate(parts, axis=0).astype(BF16)
     for copy in copies[4:]:
         copy.wait()
-    left = sigmoid(contract(lg_ref[...], masked, 0, 1)) * contract(lv_ref[...], masked, 0, 1)
-    right = sigmoid(contract(rg_ref[...], masked, 0, 1)) * contract(rv_ref[...], masked, 0, 1)
+    projected = contract(weights_ref[...], masked, 0, 1)
+    left = sigmoid(projected[0:128]) * projected[128:256]
+    right = sigmoid(projected[256:384]) * projected[384:512]
     for t in range(3):
         lanes = slice(t * 128, (t + 1) * 128)
         rows_ref[t, pl.ds(0, width, stride=2), :] = right[:, lanes]
@@ -269,7 +267,7 @@
     arrays = [pair.reshape(rows * cols, width), token_mask]
     arrays += [v.reshape(1, -1) for v in (norm_in_gain, norm_in_bias, norm_out_gain, norm_out_bias)]
     arrays += [left_gate, left_value, right_gate, right_value]
-    fetched = [pltpu.VMEM(array.shape, array.dtype) for array in arrays]
+    fetched = [pltpu.VMEM(array.shape, array.dtype) for array in arrays[:6]] + [pltpu.VMEM((width, 4 * width), BF16)]
     fetched[1] = pltpu.SMEM(token_mask.shape, token_mask.dtype)
     sent, normed, columns, spread = pl.pallas_call(
         edges_kernel,

time: 66.4 us -> 66.4 us (level)
  no operation moved by 1% of the time
where the time goes in v13:
time: 66.4 us; the launch traced here: 66 us
  blocking collectives  48.9 us (74%)
  starting transfers between devices  12.2 us (18%)
  Pallas kernels  4.75 us (7%)
    all_to_all x2, blocking collectives, shards(): got = lax.all_to_all(sent, BOTH, 0, 0, axis_index_groups=SHARING)  48.9 us
    ppermute x1, starting transfers between devices, shards(): far = lax.ppermute(right, BOTH, HALF_FLIP)  4.41 us
    ppermute x1, starting transfers between devices, shards(): near = lax.ppermute(right, BOTH, CORE_FLIP)  4.32 us
    ppermute x1, starting transfers between devices, shards(): both = lax.ppermute(far, BOTH, CORE_FLIP)  3.52 us
    pallas_call x1, Pallas kernels, shards(): pl.pallas_call(edges_kernel, name='edges', out_shape=(message, struct((ro...  1.65 us
  transfers between devices with their start and end apart: 3, of which 0 were waited for; matrix products, arithmetic and copies ran while one was open for 0% of the time, Pallas kernels for 2%

profile of v13, /device:TPU:1, one launch (start us, length us, event | category | flops | bytes accessed | tf_op | source)
XLA Modules:
  0.0 66.0 jit_solution(8036357793169946372)
XLA Ops:
  0.0 1.6 %edges.1 = (bf16[128,2,384]{2,1,0:T(2,128)(2,1)S(1)}, bf16[288,128]{1,0:T(8,128)(2,1)S(1)}, f32[2,128,128]{2,1,0:T(8,128)S(1)}, bf16[192,256]{1,0:T(8,128)(2,1)S(1)}) custom-call(bf16[288,128]{1,0:T(8,128)(2,1)} %bitcast.5, s32[384]{0:T(512)} %mask_hbm.1, f32[1,128]{1,0:T(1,128)} %bitcast.6, f32[1,128]{1,0:T(1,128)} %bitcast.7, f32[1,128]{1,0:T(1,128)} %bitcast.8, ...), custom_call_target="tpu_custom_call" | custom-call | tf_op jit(solution)/shard_map/edges/pallas_call | solution.py:272
  1.7 30.4 %all_to_all.10.got_ref = bf16[128,2,384]{2,1,0:T(2,128)(2,1)S(1)} all-to-all(bf16[128,2,384]{2,1,0:T(2,128)(2,1)S(1)} %get-tuple-element.13), channel_id=1, replica_groups={{0,1,2,3,4,5,6,7,8,9,10,11,12,13,14,15,32,33,34,35,36,37,38,39,40,41,42..., dimensions={0} | all-to-all | bytes 393216 | tf_op jit(solution)/shard_map/all_to_all | solution.py:286
  32.1 0.0 copy-start
  32.1 0.4 right.1.mine_ref
  32.5 4.4 %collective-permute-start.1 = (bf16[96,384]{1,0:T(8,128)(2,1)S(1)}, bf16[96,384]{1,0:T(8,128)(2,1)S(1)}, u32[]{:S(2)}, u32[]{:S(2)}) collective-permute-start(bf16[96,384]{1,0:T(8,128)(2,1)S(1)} %right.1.mine_ref), channel_id=1, source_target_pairs={{0,224},{1,225},{2,226},{3,227},{4,228},{5,229},{6,230},{7,231},{8... | collective-permute-start | bytes 221192 | tf_op jit(solution)/shard_map/ppermute | solution.py:298
  36.9 4.3 %collective-permute-start = (bf16[96,384]{1,0:T(8,128)(2,1)S(1)}, bf16[96,384]{1,0:T(8,128)(2,1)S(1)}, u32[]{:S(2)}, u32[]{:S(2)}) collective-permute-start(bf16[96,384]{1,0:T(8,128)(2,1)S(1)} %right.1.mine_ref), channel_id=1, source_target_pairs={{0,16},{1,17},{2,18},{3,19},{4,20},{5,21},{6,22},{7,23},{8,24},{9,... | collective-permute-start | bytes 221192 | tf_op jit(solution)/shard_map/ppermute | solution.py:297
  41.3 0.0 collective-permute-done.1.far_ref
  41.3 3.5 %collective-permute-start.2 = (bf16[96,384]{1,0:T(8,128)(2,1)S(1)}, bf16[96,384]{1,0:T(8,128)(2,1)S(1)}, u32[]{:S(2)}, u32[]{:S(2)}) collective-permute-start(bf16[96,384]{1,0:T(8,128)(2,1)S(1)} %collective-permute-done.1.far_ref), channel_id=1, source_target_pairs={{0,16},{1,17},{2,18},{3,19},{4,20},{5,21},{6,22},{7,23},{8,24},{9,... | collective-permute-start | bytes 221192 | tf_op jit(solution)/shard_map/ppermute | solution.py:299
  44.8 0.0 collective-permute-done.theirs_ref
  44.8 0.0 copy-done
  44.8 1.0 %near.1 = (bf16[128,2,384]{2,1,0:T(2,128)(2,1)S(1)}, f32[288,128]{1,0:T(8,128)S(1)}, bf16[96,384]{1,0:T(8,128)(2,1)S(1)}, f32[192,256]{1,0:T(8,128)S(1)}) custom-call(bf16[128,2,384]{2,1,0:T(2,128)(2,1)S(1)} %all_to_all.10.got_ref, bf16[96,384]{1,0:T(8,128)(2,1)S(1)} %right.1.mine_ref, bf16[96,384]{1,0:T(8,128)(2,1)S(1)} %collective-permute-done.theirs_ref, ...), custom_call_target="tpu_custom_call" | custom-call | tf_op jit(solution)/shard_map/near/pallas_call | solution.py:300
  45.8 0.0 collective-permute-done.2.theirs_ref
  45.8 0.6 far.1
  46.4 0.0 copy-start.1
  46.4 18.5 %all_to_all.11.got_ref = bf16[128,2,384]{2,1,0:T(2,128)(2,1)S(1)} all-to-all(bf16[128,2,384]{2,1,0:T(2,128)(2,1)S(1)} %far.1), channel_id=1, replica_groups={{0,1,2,3,4,5,6,7,8,9,10,11,12,13,14,15,32,33,34,35,36,37,38,39,40,41,42..., dimensions={0} | all-to-all | bytes 393216 | tf_op jit(solution)/shard_map/all_to_all | solution.py:324
  64.9 0.0 copy-done.1
  64.9 1.1 %update.1 = bf16[12,24,128]{2,1,0:T(8,128)(2,1)} custom-call(bf16[128,2,384]{2,1,0:T(2,128)(2,1)S(1)} %all_to_all.11.got_ref, f32[288,128]{1,0:T(8,128)S(1)} %get-tuple-element.19.gate_ref, f32[2,128,128]{2,1,0:T(8,128)S(1)} %get-tuple-element.20.columns_ref, bf16[128,128]{1,0:T(8,128)(2,1)S(1)} %copy-done.1), custom_call_target="tpu_custom_call" | custom-call | tf_op jit(solution)/shard_map/update/pallas_call | solution.py:325
Async XLA Ops:
  32.1 12.7 %copy-start = (bf16[128,128]{1,0:T(8,128)(2,1)S(1)}, bf16[128,128]{1,0:T(8,128)(2,1)}, u32[]{:S(2)}) copy-start(bf16[128,128]{1,0:T(8,128)(2,1)} %og_ref.1) | copy-start | bytes 98308
  32.5 8.8 %collective-permute-start.1 = (bf16[96,384]{1,0:T(8,128)(2,1)S(1)}, bf16[96,384]{1,0:T(8,128)(2,1)S(1)}, u32[]{:S(2)}, u32[]{:S(2)}) collective-permute-start(bf16[96,384]{1,0:T(8,128)(2,1)S(1)} %right.1.mine_ref), channel_id=1, source_target_pairs={{0,224},{1,225},{2,226},{3,227},{4,228},{5,229},{6,230},{7,231},{8... | collective-permute-start | bytes 221192 | tf_op jit(solution)/shard_map/ppermute | solution.py:298
  36.9 7.9 %collective-permute-start = (bf16[96,384]{1,0:T(8,128)(2,1)S(1)}, bf16[96,384]{1,0:T(8,128)(2,1)S(1)}, u32[]{:S(2)}, u32[]{:S(2)}) collective-permute-start(bf16[96,384]{1,0:T(8,128)(2,1)S(1)} %right.1.mine_ref), channel_id=1, source_target_pairs={{0,16},{1,17},{2,18},{3,19},{4,20},{5,21},{6,22},{7,23},{8,24},{9,... | collective-permute-start | bytes 221192 | tf_op jit(solution)/shard_map/ppermute | solution.py:297
  41.3 4.6 %collective-permute-start.2 = (bf16[96,384]{1,0:T(8,128)(2,1)S(1)}, bf16[96,384]{1,0:T(8,128)(2,1)S(1)}, u32[]{:S(2)}, u32[]{:S(2)}) collective-permute-start(bf16[96,384]{1,0:T(8,128)(2,1)S(1)} %collective-permute-done.1.far_ref), channel_id=1, source_target_pairs={{0,16},{1,17},{2,18},{3,19},{4,20},{5,21},{6,22},{7,23},{8,24},{9,... | collective-permute-start | bytes 221192 | tf_op jit(solution)/shard_map/ppermute | solution.py:299
  46.4 18.5 %copy-start.1 = (bf16[128,128]{1,0:T(8,128)(2,1)S(1)}, bf16[128,128]{1,0:T(8,128)(2,1)}, u32[]{:S(2)}) copy-start(bf16[128,128]{1,0:T(8,128)(2,1)} %weight_ref.1) | copy-start | bytes 98308

commit v14 on v11

--- a/solution.py
+++ b/solution.py
@@ -99,20 +99,21 @@
     first_row, first_col, core, _ = place_of()
     to_lane = row + 20 * run + 16 * jnp.where(side == 0, core, 1 - core)
     spread_ref[...] = jnp.where(iota(spread_ref.shape, 1) == to_lane, 1.0, 0.0).astype(BF16)
-    for copy in copies[:4]:
-        copy.wait()
     width = lg_ref.shape[0]
     rows, cols = 12, 24
+    copies[1].wait()
+    place = iota((cols, width), 0)
+    col_valid = jnp.zeros((cols, width), F32)
+    for k in range(cols):
+        col_valid = jnp.where(place == k, mask_ref[first_col + k].astype(F32), col_valid)
+    for copy in (copies[0], copies[2], copies[3]):
+        copy.wait()
     x = pair_ref[...].astype(F32)
     mean = jnp.mean(x, axis=-1, keepdims=True)
     centered = x - mean
     variance = jnp.mean(centered * centered, axis=-1, keepdims=True)
     normed = centered * lax.rsqrt(variance + EPS) * gain_ref[...] + bias_ref[...]
     normed_ref[...] = normed.astype(BF16)
-    place = iota((cols, width), 0)
-    col_valid = jnp.zeros((cols, width), F32)
-    for k in range(cols):
-        col_valid = jnp.where(place == k, mask_ref[first_col + k].astype(F32), col_valid)
     parts = []
     for i in [3 * ii + iq for iq in range(3) for ii in range(4)]:
         row_valid = mask_ref[first_row + i].astype(F32)

time: 66.3 us -> 66.3 us (level)
  no operation moved by 1% of the time
where the time goes in v14:
time: 66.3 us; the launch traced here: 65.9 us
  blocking collectives  48.9 us (74%)
  starting transfers between devices  12.2 us (18%)
  Pallas kernels  4.67 us (7%)
    all_to_all x2, blocking collectives, shards(): got = lax.all_to_all(sent, BOTH, 0, 0, axis_index_groups=SHARING)  48.9 us
    ppermute x1, starting transfers between devices, shards(): far = lax.ppermute(right, BOTH, HALF_FLIP)  4.41 us
    ppermute x1, starting transfers between devices, shards(): near = lax.ppermute(right, BOTH, CORE_FLIP)  4.32 us
    ppermute x1, starting transfers between devices, shards(): both = lax.ppermute(far, BOTH, CORE_FLIP)  3.52 us
    pallas_call x1, Pallas kernels, shards(): pl.pallas_call(edges_kernel, name='edges', out_shape=(message, struct((ro...  1.63 us
  transfers between devices with their start and end apart: 3, of which 0 were waited for; matrix products, arithmetic and copies ran while one was open for 0% of the time, Pallas kernels for 1%

profile of v14, /device:TPU:1, one launch (start us, length us, event | category | flops | bytes accessed | tf_op | source)
XLA Modules:
  0.0 65.9 jit_solution(6030481744985200403)
XLA Ops:
  0.0 1.6 %edges.1 = (bf16[128,2,384]{2,1,0:T(2,128)(2,1)S(1)}, bf16[288,128]{1,0:T(8,128)(2,1)S(1)}, f32[2,128,128]{2,1,0:T(8,128)S(1)}, bf16[192,256]{1,0:T(8,128)(2,1)S(1)}) custom-call(bf16[288,128]{1,0:T(8,128)(2,1)} %bitcast.5, s32[384]{0:T(512)} %mask_hbm.1, f32[1,128]{1,0:T(1,128)} %bitcast.6, f32[1,128]{1,0:T(1,128)} %bitcast.7, f32[1,128]{1,0:T(1,128)} %bitcast.8, ...), custom_call_target="tpu_custom_call" | custom-call | tf_op jit(solution)/shard_map/edges/pallas_call | solution.py:262
  1.6 30.4 %all_to_all.10.got_ref = bf16[128,2,384]{2,1,0:T(2,128)(2,1)S(1)} all-to-all(bf16[128,2,384]{2,1,0:T(2,128)(2,1)S(1)} %get-tuple-element.12), channel_id=1, replica_groups={{0,1,2,3,4,5,6,7,8,9,10,11,12,13,14,15,32,33,34,35,36,37,38,39,40,41,42..., dimensions={0} | all-to-all | bytes 393216 | tf_op jit(solution)/shard_map/all_to_all | solution.py:276
  32.1 0.0 copy-start
  32.1 0.4 right.1.mine_ref
  32.5 4.4 %collective-permute-start.1 = (bf16[96,384]{1,0:T(8,128)(2,1)S(1)}, bf16[96,384]{1,0:T(8,128)(2,1)S(1)}, u32[]{:S(2)}, u32[]{:S(2)}) collective-permute-start(bf16[96,384]{1,0:T(8,128)(2,1)S(1)} %right.1.mine_ref), channel_id=1, source_target_pairs={{0,224},{1,225},{2,226},{3,227},{4,228},{5,229},{6,230},{7,231},{8... | collective-permute-start | bytes 221192 | tf_op jit(solution)/shard_map/ppermute | solution.py:288
  36.9 4.3 %collective-permute-start = (bf16[96,384]{1,0:T(8,128)(2,1)S(1)}, bf16[96,384]{1,0:T(8,128)(2,1)S(1)}, u32[]{:S(2)}, u32[]{:S(2)}) collective-permute-start(bf16[96,384]{1,0:T(8,128)(2,1)S(1)} %right.1.mine_ref), channel_id=1, source_target_pairs={{0,16},{1,17},{2,18},{3,19},{4,20},{5,21},{6,22},{7,23},{8,24},{9,... | collective-permute-start | bytes 221192 | tf_op jit(solution)/shard_map/ppermute | solution.py:287
  41.3 0.0 collective-permute-done.1.mine_ref
  41.3 3.5 %collective-permute-start.2 = (bf16[96,384]{1,0:T(8,128)(2,1)S(1)}, bf16[96,384]{1,0:T(8,128)(2,1)S(1)}, u32[]{:S(2)}, u32[]{:S(2)}) collective-permute-start(bf16[96,384]{1,0:T(8,128)(2,1)S(1)} %collective-permute-done.1.mine_ref), channel_id=1, source_target_pairs={{0,16},{1,17},{2,18},{3,19},{4,20},{5,21},{6,22},{7,23},{8,24},{9,... | collective-permute-start | bytes 221192 | tf_op jit(solution)/shard_map/ppermute | solution.py:289
  44.8 0.0 collective-permute-done.theirs_ref
  44.8 0.0 copy-done
  44.8 0.9 %near.1 = (bf16[128,2,384]{2,1,0:T(2,128)(2,1)S(1)}, f32[288,128]{1,0:T(8,128)S(1)}, bf16[96,384]{1,0:T(8,128)(2,1)S(1)}) custom-call(bf16[128,2,384]{2,1,0:T(2,128)(2,1)S(1)} %all_to_all.10.got_ref, bf16[96,384]{1,0:T(8,128)(2,1)S(1)} %right.1.mine_ref, bf16[96,384]{1,0:T(8,128)(2,1)S(1)} %collective-permute-done.theirs_ref, ...), custom_call_target="tpu_custom_call" | custom-call | tf_op jit(solution)/shard_map/near/pallas_call | solution.py:290
  45.7 0.0 collective-permute-done.2.theirs_ref
  45.7 0.6 far.1
  46.4 0.0 copy-start.1
  46.4 18.5 %all_to_all.11.got_ref = bf16[128,2,384]{2,1,0:T(2,128)(2,1)S(1)} all-to-all(bf16[128,2,384]{2,1,0:T(2,128)(2,1)S(1)} %far.1), channel_id=1, replica_groups={{0,1,2,3,4,5,6,7,8,9,10,11,12,13,14,15,32,33,34,35,36,37,38,39,40,41,42..., dimensions={0} | all-to-all | bytes 393216 | tf_op jit(solution)/shard_map/all_to_all | solution.py:309
  64.8 0.0 copy-done.1
  64.8 1.1 %update.1 = bf16[12,24,128]{2,1,0:T(8,128)(2,1)} custom-call(bf16[128,2,384]{2,1,0:T(2,128)(2,1)S(1)} %all_to_all.11.got_ref, f32[288,128]{1,0:T(8,128)S(1)} %get-tuple-element.17.gate_ref, f32[2,128,128]{2,1,0:T(8,128)S(1)} %get-tuple-element.18.columns_ref, bf16[128,128]{1,0:T(8,128)(2,1)S(1)} %copy-done.1), custom_call_target="tpu_custom_call" | custom-call | tf_op jit(solution)/shard_map/update/pallas_call | solution.py:310
Async XLA Ops:
  32.1 12.7 %copy-start = (bf16[128,128]{1,0:T(8,128)(2,1)S(1)}, bf16[128,128]{1,0:T(8,128)(2,1)}, u32[]{:S(2)}) copy-start(bf16[128,128]{1,0:T(8,128)(2,1)} %og_ref.1) | copy-start | bytes 98308
  32.5 8.8 %collective-permute-start.1 = (bf16[96,384]{1,0:T(8,128)(2,1)S(1)}, bf16[96,384]{1,0:T(8,128)(2,1)S(1)}, u32[]{:S(2)}, u32[]{:S(2)}) collective-permute-start(bf16[96,384]{1,0:T(8,128)(2,1)S(1)} %right.1.mine_ref), channel_id=1, source_target_pairs={{0,224},{1,225},{2,226},{3,227},{4,228},{5,229},{6,230},{7,231},{8... | collective-permute-start | bytes 221192 | tf_op jit(solution)/shard_map/ppermute | solution.py:288
  36.9 7.9 %collective-permute-start = (bf16[96,384]{1,0:T(8,128)(2,1)S(1)}, bf16[96,384]{1,0:T(8,128)(2,1)S(1)}, u32[]{:S(2)}, u32[]{:S(2)}) collective-permute-start(bf16[96,384]{1,0:T(8,128)(2,1)S(1)} %right.1.mine_ref), channel_id=1, source_target_pairs={{0,16},{1,17},{2,18},{3,19},{4,20},{5,21},{6,22},{7,23},{8,24},{9,... | collective-permute-start | bytes 221192 | tf_op jit(solution)/shard_map/ppermute | solution.py:287
  41.3 4.5 %collective-permute-start.2 = (bf16[96,384]{1,0:T(8,128)(2,1)S(1)}, bf16[96,384]{1,0:T(8,128)(2,1)S(1)}, u32[]{:S(2)}, u32[]{:S(2)}) collective-permute-start(bf16[96,384]{1,0:T(8,128)(2,1)S(1)} %collective-permute-done.1.mine_ref), channel_id=1, source_target_pairs={{0,16},{1,17},{2,18},{3,19},{4,20},{5,21},{6,22},{7,23},{8,24},{9,... | collective-permute-start | bytes 221192 | tf_op jit(solution)/shard_map/ppermute | solution.py:289
  46.4 18.5 %copy-start.1 = (bf16[128,128]{1,0:T(8,128)(2,1)S(1)}, bf16[128,128]{1,0:T(8,128)(2,1)}, u32[]{:S(2)}) copy-start(bf16[128,128]{1,0:T(8,128)(2,1)} %weight_ref.1) | copy-start | bytes 98308
